TPU v7x, 512 devices: a whole 4x4x16 slice. The times are simulated.
512 devices in a mesh: row: 32 (over x, z_lo), col: 16 (over z_hi, y, core).
Axes of the slice: x: 4, y: 4, z: 16 (z_hi: 2, z_lo: 8; z = z_hi * 8 + z_lo), core: 2. Of those that a mesh axis runs over, the one named last changes fastest.
Arguments:
- covariance: float32 [16384, 16384], P('row', 'col'), may hold values from -6 to 6
- left_ops: float32 [32, 3, 512, 512], P('row', None, None, 'col'), may hold values from -0.15625 to 0.15625
- right_ops: float32 [32, 3, 512, 512], P('col', None, 'row'), may hold values from -0.15625 to 0.15625
- edge_rows: float32 [2, 512, 16384], P(None, 'row', 'col'), may hold values from -6 to 6
- edge_cols: float32 [16384, 2, 512], P('row', None, 'col'), may hold values from -6 to 6
Outputs:
- forecast: float32 [16384, 16384], P('row', 'col')
All inputs are finite; a program needn't handle non-finite values.
Results may differ from a plain program's by a relative error of at most 0.0003.
Values sent between devices are 32-bit elements; how exact they have to be, the bound alone decides.
No kernel may reach another device: no remote copies, remote signals or barrier semaphores. Data moves between devices by JAX's collectives and lax.ppermute only.
A program may use at most 64 MiB of HBM per device.

v0:
```python
import jax
import jax.numpy as jnp
from jax import lax
from jax.sharding import PartitionSpec as P


def extended(cells, sides, width):
    for axis, dim in sides:
        count = lax.axis_size(axis)
        ends = count - 1
        head = lax.slice_in_dim(cells, 0, width, axis=dim)
        tail = lax.slice_in_dim(cells, cells.shape[dim] - width, cells.shape[dim], axis=dim)
        cells = jnp.concatenate(
            [
                lax.ppermute(tail, axis, [(i, (i + 1) % count) for i in range(ends)]),
                cells,
                lax.ppermute(head, axis, [((i + 1) % count, i) for i in range(ends)]),
            ],
            axis=dim,
        )
    return cells


def on_device(covariance, left_ops, right_ops, edge_rows, edge_cols):
    row_index = lax.axis_index("row")
    col_index = lax.axis_index("col")
    row_count = lax.axis_size("row")
    col_count = lax.axis_size("col")
    block = covariance.shape[0]
    bands_here = right_ops.shape[0]
    left_full, side_full = (
        lax.all_gather(left_ops, "col", axis=3, tiled=True),
        lax.all_gather(edge_cols[None], "col", axis=3, tiled=True),
    )
    left_blocks = left_full[0]
    sides = side_full[0]
    outside = lax.all_gather(edge_rows, "row", axis=1, tiled=True)
    padded = extended(covariance, (("row", 0),), block)
    upper = jnp.where(row_index == 0, outside[0], padded[:block])
    lower = jnp.where(row_index == row_count - 1, outside[1], padded[2 * block :])
    half = jnp.dot(
        left_blocks[0], upper, preferred_element_type=jnp.float32, precision=lax.Precision.HIGHEST
    )
    half = half + jnp.dot(
        left_blocks[1],
        covariance,
        preferred_element_type=jnp.float32,
        precision=lax.Precision.HIGHEST,
    )
    half = half + jnp.dot(
        left_blocks[2], lower, preferred_element_type=jnp.float32, precision=lax.Precision.HIGHEST
    )
    half_padded = extended(half, (("col", 1),), block)
    before = jnp.where(col_index == 0, sides[:, 0], half_padded[:, :block])
    after = jnp.where(
        col_index == col_count - 1, sides[:, 1], half_padded[:, half_padded.shape[1] - block :]
    )
    cols_ext = jnp.concatenate([before, half, after], axis=1)
    windows = jnp.stack(
        [cols_ext[:, band * block : (band + 3) * block] for band in range(bands_here)]
    )
    windows = windows.reshape(bands_here, block, 3, block)
    result = jnp.einsum(
        "kamb,kmcb->kac",
        windows,
        lax.all_gather(right_ops, "row", axis=2, tiled=True),
        preferred_element_type=jnp.float32,
        precision=lax.Precision.HIGHEST,
    )
    return jnp.transpose(result, (1, 0, 2)).reshape(block, bands_here * block)


def solution(mesh):
    return jax.shard_map(
        on_device,
        mesh=mesh,
        in_specs=(
            P("row", "col"),
            P("row", None, None, "col"),
            P("col", None, "row", None),
            P(None, "row", "col"),
            P("row", None, "col"),
        ),
        out_specs=P("row", "col"),
        check_vma=False,
    )
```

profile of v0, /device:TPU:24, one launch (start us, length us, event | category | flops | bytes accessed | tf_op | source)
XLA Modules:
  0.0 796.3 jit_solution(3280187313834740720)
XLA Ops:
  6.5 0.0 all-gather.8.cloned.1.call-start
  6.5 0.7 all-gather.8.cloned.1.call-update
  7.3 0.0 all-gather.6.cloned.1.call-start
  7.3 0.7 all-gather.6.cloned.1.call-update
  8.0 0.0 all-gather.12.cloned.1.call-start
  8.1 0.7 all-gather.12.cloned.1.call-update
  8.7 0.0 all-gather.10.cloned.1.call-start
  8.8 0.5 all-gather.10.cloned.1.call-update
  9.3 4.0 collective-permute-start
  13.3 1.3 collective-permute-start.1
  14.6 142.8 %all-gather.8.cloned.1.call-done = f32[1,3,512,512]{2,3,1,0:T(8,128)} async-done(((f32[1,3,512,32]{2,3,1,0:T(8,128)}), f32[1,3,512,512]{2,3,1,0:T(8,128)}) %all-gather.8.cloned.1.call-update) | async-done | bytes 3145744 | tf_op jit(solution)/shard_map/all_gather | solution.py:32
  157.4 6.7 fusion.13
  164.1 0.0 collective-permute-done
  164.1 239.9 %all-gather.6.cloned.1.call-done = f32[2,512,1024]{2,1,0:T(8,128)} async-done(((f32[2,16,1024]{2,1,0:T(8,128)}), f32[2,512,1024]{2,1,0:T(8,128)}) %all-gather.6.cloned.1.call-update) | async-done | bytes 4194320 | tf_op jit(solution)/shard_map/all_gather | solution.py:37
  404.0 0.0 copy-start
  404.0 0.0 copy-start.1
  404.0 5.6 fusion.8
  409.6 0.0 collective-permute-done.1
  409.6 0.0 copy-done
  409.6 0.0 copy-done.1
  409.6 5.7 bitcast_add_fusion
  415.3 1.6 fusion.18
  416.8 1.9 collective-permute-start.2
  418.8 3.8 collective-permute-start.3
  422.6 110.0 %all-gather.12.cloned.1.call-done = f32[512,2,512]{0,2,1:T(8,128)} async-done(((f32[512,2,32]{0,2,1:T(8,128)}), f32[512,2,512]{0,2,1:T(8,128)}) %all-gather.12.cloned.1.call-update) | async-done | bytes 2097168 | tf_op jit(solution)/shard_map/all_gather | solution.py:33
  532.5 0.0 collective-permute-done.2
  532.6 0.0 collective-permute-done.3
  532.6 2.3 fusion.14
  534.9 3.4 pad_maximum_fusion
  538.3 2.4 copy.7
  540.7 3.6 copy.8
  544.3 228.5 %all-gather.10.cloned.1.call-done = f32[2,3,512,512]{3,2,1,0:T(8,128)} async-done(((f32[2,3,16,512]{3,2,1,0:T(8,128)}), f32[2,3,512,512]{3,2,1,0:T(8,128)}) %all-gather.10.cloned.1.call-update) | async-done | bytes 6291472 | tf_op jit(solution)/shard_map/all_gather | solution.py:66
  772.8 14.1 %fusion = f32[2,512,512,1]{1,2,3,0:T(8,128)} fusion(f32[2,3,512,512]{3,2,1,0:T(8,128)} %all-gather.10.cloned.1.call-done, f32[1,512,3,512]{3,1,2,0:T(8,128)} %copy.8, f32[1,512,3,512]{3,1,2,0:T(8,128)S(1)} %copy.7), kind=kOutput, calls=%fused_computation | convolution fusion | flops 9665249280 | bytes 14680064 | tf_op jit(solution)/shard_map/kamb,kmcb->kac/dot_general | solution.py:63
  786.9 2.9 copy.9
Async XLA Ops:
  6.5 150.9 %all-gather.8.cloned.1.call-start = ((), (), s32[]{:S(2)}) async-start(), calls=%async_computation.1 | async-start | bytes 3342336 | tf_op jit(solution)/shard_map/all_gather | solution.py:32
  7.3 396.8 %all-gather.6.cloned.1.call-start = ((), (), s32[]{:S(2)}) async-start(), calls=%async_computation | async-start | bytes 4325376 | tf_op jit(solution)/shard_map/all_gather | solution.py:37
  8.0 524.5 %all-gather.12.cloned.1.call-start = ((), (), s32[]{:S(2)}) async-start(), calls=%async_computation.3 | async-start | bytes 2228224 | tf_op jit(solution)/shard_map/all_gather | solution.py:33
  8.7 764.1 %all-gather.10.cloned.1.call-start = ((), (), s32[]{:S(2)}) async-start(), calls=%async_computation.2 | async-start | bytes 6488064 | tf_op jit(solution)/shard_map/all_gather | solution.py:66
  9.3 154.8 %collective-permute-start = (f32[512,1024]{1,0:T(8,128)}, f32[512,1024]{1,0:T(8,128)S(1)}, u32[]{:S(2)}, u32[]{:S(2)}) collective-permute-start(f32[512,1024]{1,0:T(8,128)} %param.5), channel_id=1, source_target_pairs={{0,16},{16,32},{32,48},{48,64},{64,80},{80,96},{96,112},{112,128},... | collective-permute-start | bytes 6291464 | tf_op jit(solution)/shard_map/ppermute | solution.py:15
  13.3 396.3 %collective-permute-start.1 = (f32[512,1024]{1,0:T(8,128)}, f32[512,1024]{1,0:T(8,128)}, u32[]{:S(2)}, u32[]{:S(2)}) collective-permute-start(f32[512,1024]{1,0:T(8,128)} %param.5), channel_id=1, source_target_pairs={{16,0},{32,16},{48,32},{64,48},{80,64},{96,80},{112,96},{128,112},... | collective-permute-start | bytes 6291464 | tf_op jit(solution)/shard_map/ppermute | solution.py:17
  404.0 5.6 copy-start
  404.0 5.6 copy-start.1
  416.8 115.7 %collective-permute-start.2 = (f32[512,512]{0,1:T(8,128)}, f32[512,512]{0,1:T(8,128)S(1)}, u32[]{:S(2)}, u32[]{:S(2)}) collective-permute-start(f32[512,512]{0,1:T(8,128)} %get-tuple-element.9), channel_id=1, source_target_pairs={{0,1},{1,2},{2,3},{3,4},{4,5},{5,6},{6,7},{7,8},{8,9},{9,10},{10,1... | collective-permute-start | bytes 3145736 | tf_op jit(solution)/shard_map/ppermute | solution.py:15
  418.8 113.8 %collective-permute-start.3 = (f32[512,512]{0,1:T(8,128)}, f32[512,512]{0,1:T(8,128)}, u32[]{:S(2)}, u32[]{:S(2)}) collective-permute-start(f32[512,512]{0,1:T(8,128)} %get-tuple-element.10), channel_id=1, source_target_pairs={{1,0},{2,1},{3,2},{4,3},{5,4},{6,5},{7,6},{8,7},{9,8},{10,9},{11,1... | collective-permute-start | bytes 3145736 | tf_op jit(solution)/shard_map/ppermute | solution.py:17
Sparse Core Ops, SparseCore 0:
  10.7 146.6 all-gather.7
  159.5 244.5 all-gather.5
  407.4 125.1 all-gather.11
  534.5 238.2 all-gather.9
where the time goes:
time: 797 us; the launch traced here: 796 us
  waiting for transfers between devices  724 us (91%)
  matrix products  32 us (4%)
  between operations  13.2 us (2%)
  starting transfers between devices  11.1 us (1%)
  local copies, waits for them, and re-layouts  10.4 us (1%)
    all_gather x1, waiting for transfers between devices, on_device(): outside = lax.all_gather(edge_rows, 'row', axis=1, tiled=True)  240 us
    all_gather x1, waiting for transfers between devices, on_device(): lax.all_gather(right_ops, 'row', axis=2, tiled=True)  229 us
    all_gather x1, waiting for transfers between devices, on_device(): lax.all_gather(left_ops, 'col', axis=3, tiled=True)  143 us
    all_gather x1, waiting for transfers between devices, on_device(): lax.all_gather(edge_cols[None], 'col', axis=3, tiled=True)  110 us
  transfers between devices with their start and end apart: 8, of which 4 were waited for; matrix products, arithmetic and copies ran while one was open for 4% of the time, Pallas kernels for 0%

commit v1 on v0

v1 whole, which is shorter than its diff:
```python
import jax
import jax.numpy as jnp
from jax import lax
from jax.sharding import PartitionSpec as P

NX, NZ, NH, NY, NC = 4, 8, 2, 4, 2
HIGH = lax.Precision.HIGH
AXES = ("row", "col")


def moved(array, target):
    pairs = []
    for x in range(NX):
        for z in range(NZ):
            for h in range(NH):
                for y in range(NY):
                    for c in range(NC):
                        to = target(x, z, h, y, c)
                        if to is not None:
                            pairs.append((flat(x, z, h, y, c), flat(*to)))
    return lax.ppermute(array, AXES, pairs)


def flat(x, z, h, y, c):
    return (((x * NZ + z) * NH + h) * NY + y) * NC + c


def row_step(d):
    def target(x, z, h, y, c):
        r = x * NZ + z + d
        return (r // NZ, r % NZ, h, y, c) if 0 <= r < NX * NZ else None

    return target


def col_step(d):
    def target(x, z, h, y, c):
        k = (h * NY + y) * NC + c + d
        return (x, z, k // 8, k % 8 // 2, k % 2) if 0 <= k < 16 else None

    return target


def x_step(d):
    return lambda x, z, h, y, c: ((x + d) % NX, z, h, y, c)


def y_step(d):
    return lambda x, z, h, y, c: (x, z, h, (y + d) % NY, c)


def z_swap(bit):
    return lambda x, z, h, y, c: (x, z ^ bit, h, y, c)


def h_swap(x, z, h, y, c):
    return (x, z, 1 - h, y, c)


def core_swap(x, z, h, y, c):
    return (x, z, h, y, 1 - c)


def dot(a, b, dims):
    return lax.dot_general(
        a, b, (dims, ((), ())), precision=HIGH, preferred_element_type=jnp.float32
    )


def gather_left(left, edge, h, y, c):
    own = jnp.concatenate([left, jnp.where(h == 0, edge[1], edge[0])], axis=0)
    keep = jnp.concatenate([left, jnp.where(h == 0, edge[0], edge[1])], axis=0)
    other = moved(own, h_swap)
    pair = jnp.stack([jnp.where(h == 0, keep, other), jnp.where(h == 0, other, keep)])
    below = moved(pair, y_step(1))
    above = moved(pair, y_step(-1))
    across = moved(pair, y_step(2))
    ring = jnp.stack([pair, above, across, below])
    ring = jnp.concatenate([ring, ring])
    ring = lax.dynamic_slice_in_dim(ring, NY - y, NY, axis=0)
    mate = moved(ring, core_swap)
    both = jnp.stack([jnp.where(c == 0, ring, mate), jnp.where(c == 0, mate, ring)])
    full = both.reshape(NC, NY, NH, 4, 32, 512).transpose(3, 2, 1, 0, 4, 5)
    full = full.reshape(4, 512, 512)
    return full[:3], full[3]


def gather_right(right, x, z):
    b2, b1, b0 = z // 4, z // 2 % 2, z % 2
    zero = jnp.int32(0)
    full = jnp.zeros((2, 3, NX, 2, 2, 2, 16, 512), jnp.float32)

    def put(full, block, where):
        return lax.dynamic_update_slice(full, block, (zero, zero, *where, zero, zero))

    def put_all(full, block, where):
        full = put(full, block, (x, *where))
        for d in (1, -1, 2):
            full = put(full, moved(block, x_step(d)), ((x + NX - d) % NX, *where))
        return full

    own = right.reshape(2, 3, 1, 1, 1, 1, 16, 512)
    far = moved(own, z_swap(4))
    pair = jnp.concatenate([jnp.where(b2 == 0, own, far), jnp.where(b2 == 0, far, own)], axis=3)
    mid = moved(pair, z_swap(2))
    quad = jnp.concatenate([jnp.where(b1 == 0, pair, mid), jnp.where(b1 == 0, mid, pair)], axis=4)
    near = moved(quad, z_swap(1))
    full = put_all(full, pair, (zero, b1, b0))
    full = put_all(full, mid, (zero, 1 - b1, b0))
    full = put_all(full, near, (zero, zero, 1 - b0))
    return full.reshape(2, 3, 512, 512)


def gather_rows(edge, z):
    def toward(bit, size):
        def target(x, z, h, y, c):
            if bit == 4:
                return (x, z ^ 4, h, y, c)
            low = z < 4
            rest = z if low else 7 - z
            if rest < 2 * bit and rest >= bit:
                return (x, z - bit if low else z + bit, h, y, c)
            return None

        return target

    low = z < 4
    keep = jnp.where(low, edge[0], edge[1])[None]
    send = jnp.where(low, edge[1], edge[0])[None]
    got = moved(send, toward(4, 1))
    block = jnp.concatenate([jnp.where(low, keep, got), jnp.where(low, got, keep)])
    block = block.reshape(2, 1, 1, 16, 1024)
    got = moved(block, toward(2, 2))
    block = jnp.concatenate([jnp.where(low, block, got), jnp.where(low, got, block)], axis=1)
    got = moved(block, toward(1, 4))
    block = jnp.concatenate([jnp.where(low, block, got), jnp.where(low, got, block)], axis=2)
    block = block.reshape(1, 128, 1024)

    def x_one(x, z, h, y, c):
        if z == 0:
            return (x - 1, z, h, y, c) if x % 2 == 1 else None
        if z == NZ - 1:
            return (x + 1, z, h, y, c) if x % 2 == 0 else None
        return None

    def x_two(x, z, h, y, c):
        if z == 0:
            return (0, z, h, y, c) if x == 2 else None
        if z == NZ - 1:
            return (3, z, h, y, c) if x == 1 else None
        return None

    got = moved(block, x_one)
    block = jnp.concatenate([jnp.where(low, block, got), jnp.where(low, got, block)])
    got = moved(block, x_two)
    block = jnp.concatenate([jnp.where(low, block, got), jnp.where(low, got, block)])
    return block.reshape(512, 1024)


def on_device(covariance, left_ops, right_ops, edge_rows, edge_cols):
    row, col = lax.axis_index("row"), lax.axis_index("col")
    x, z = row // NZ, row % NZ
    h, y, c = col // 8, col // 2 % NY, col % NC
    size = covariance.shape[0]

    left = left_ops[0].transpose(0, 2, 1).reshape(96, 512)
    edge = edge_cols.transpose(1, 2, 0)
    left_full, side = gather_left(left, edge, h, y, c)

    bands = [covariance[:, :size], covariance[:, size:]]
    upper = [moved(band, row_step(1)) for band in bands]
    lower = [moved(band, row_step(-1)) for band in bands]
    outside = gather_rows(edge_rows, z)
    right_full = gather_right(right_ops, x, z)

    half = []
    for k, band in enumerate(bands):
        out = outside[:, k * size : (k + 1) * size]
        top = jnp.where(row == 0, out, upper[k])
        bottom = jnp.where(row == NX * NZ - 1, out, lower[k])
        part = dot(left_full[1], band, ((0,), (0,)))
        part = part + dot(left_full[0], top, ((0,), (0,)))
        half.append(part + dot(left_full[2], bottom, ((0,), (0,))))

    before = moved(half[1], col_step(1))
    after = moved(half[0], col_step(-1))
    before = jnp.where(col == 0, side.T, before)
    after = jnp.where(col == 15, side.T, after)
    line = [before, half[0], half[1], after]
    result = []
    for j in range(2):
        part = dot(half[0], right_full[j, 1 - j], ((1,), (1,)))
        part = part + dot(half[1], right_full[j, 2 - j], ((1,), (1,)))
        part = part + dot(line[3 * j], right_full[j, 2 * j], ((1,), (1,)))
        result.append(part)
    return jnp.concatenate(result, axis=1)


def solution(mesh):
    return jax.shard_map(
        on_device,
        mesh=mesh,
        in_specs=(
            P("row", "col"),
            P("row", None, None, "col"),
            P("col", None, "row", None),
            P(None, "row", "col"),
            P("row", None, "col"),
        ),
        out_specs=P("row", "col"),
        check_vma=False,
    )
```

time: 797 us -> 349 us (0.44)
  the two profiles are of different devices: /device:TPU:24 before, /device:TPU:59 now
where the time goes in v1:
time: 349 us; the launch traced here: 347 us
  starting transfers between devices  149 us (43%)
  waiting for transfers between devices  136 us (39%)
  local copies, waits for them, and re-layouts  25.1 us (7%)
  matrix products  23.2 us (7%)
  other arithmetic  12.9 us (4%)
    ppermute x28, starting transfers between devices, moved(): return lax.ppermute(array, AXES, pairs)  149 us
    ppermute x28, waiting for transfers between devices, moved(): return lax.ppermute(array, AXES, pairs)  136 us
    dot_general x12, matrix products, dot(): lax.dot_general(a, b, (dims, ((), ())), precision=HIGH, preferred_element...  23.2 us
    dynamic_update_slice x11, local copies, waits for them, and re-layouts, put(): lax.dynamic_update_slice(full, block, (zero, zero, *where, zero, zero))  14.8 us
  transfers between devices with their start and end apart: 28, of which 12 were waited for; matrix products, arithmetic and copies ran while one was open for 16% of the time, Pallas kernels for 0%

profile of v1, /device:TPU:59, one launch (start us, length us, event | category | flops | bytes accessed | tf_op | source)
XLA Modules:
  0.0 347.3 jit_solution(7487701271589092903)
XLA Ops:
  0.9 8.8 %collective-permute-start.5 = (f32[1,16,1024]{2,1,0:T(8,128)S(1)}, f32[1,16,1024]{2,1,0:T(8,128)S(1)}, u32[]{:S(2)}, u32[]{:S(2)}) collective-permute-start(f32[1,16,1024]{2,1,0:T(8,128)S(1)} %slice_select_fusion), channel_id=1, source_target_pairs={{0,64},{1,65},{2,66},{3,67},{4,68},{5,69},{6,70},{7,71},{8,72},{9,... | collective-permute-start | bytes 196616 | tf_op jit(solution)/shard_map/ppermute | solution.py:21
  9.8 1.9 collective-permute-start.12
  12.9 1.3 collective-permute-start.6
  16.0 15.7 %collective-permute-start = (f32[128,512]{1,0:T(8,128)S(1)}, f32[128,512]{1,0:T(8,128)S(1)}, u32[]{:S(2)}, u32[]{:S(2)}) collective-permute-start(f32[128,512]{1,0:T(8,128)S(1)} %pad_maximum_fusion.7), channel_id=1, source_target_pairs={{0,8},{1,9},{2,10},{3,11},{4,12},{5,13},{6,14},{7,15},{8,0},{9,1},... | collective-permute-start | bytes 786440 | tf_op jit(solution)/shard_map/ppermute | solution.py:21
  31.8 10.5 %collective-permute-done.6 = f32[2,1,1,16,1024]{4,3,2,1,0:T(8,128)S(1)} collective-permute-done((f32[2,1,1,16,1024]{4,3,2,1,0:T(8,128)S(1)}, f32[2,1,1,16,1024]{4,3,2,1,0:T(8,128)S(1)}, u32[]{:S(2)}, u32[]{:S(2)}) %collective-permute-start.6) | collective-permute-done | bytes 131104 | tf_op jit(solution)/shard_map/ppermute | solution.py:21
  42.4 20.6 %collective-permute-start.7 = (f32[2,2,1,16,1024]{4,3,2,1,0:T(8,128)S(1)}, f32[2,2,1,16,1024]{4,3,2,1,0:T(8,128)S(1)}, u32[]{:S(2)}, u32[]{:S(2)}) collective-permute-start(f32[2,2,1,16,1024]{4,3,2,1,0:T(8,128)S(1)} %pad_maximum_fusion.9), channel_id=1, source_target_pairs={{16,0},{17,1},{18,2},{19,3},{20,4},{21,5},{22,6},{23,7},{24,8},{25... | collective-permute-start | bytes 786440 | tf_op jit(solution)/shard_map/ppermute | solution.py:21
  64.8 1.9 collective-permute-start.16
  66.7 3.1 collective-permute-start.13
  69.8 2.2 collective-permute-start.14
  72.2 2.4 collective-permute-start.1
  74.6 2.6 collective-permute-start.2
  77.2 6.1 %collective-permute-done.16 = f32[2,3,1,2,1,1,16,512]{7,6,5,4,3,2,1,0:T(8,128)S(1)} collective-permute-done((f32[2,3,1,2,1,1,16,512]{7,6,5,4,3,2,1,0:T(8,128)}, f32[2,3,1,2,1,1,16,512]{7,6,5,4,3,2,1,0:T(8,128)S(1)}, u32[]{:S(2)}, u32[]{:S(2)}) %collective-permute-start.16) | collective-permute-done | bytes 393248 | tf_op jit(solution)/shard_map/ppermute | solution.py:21
  83.4 1.9 collective-permute-start.3
  86.2 1.0 pad_maximum_fusion.3
  88.2 3.7 %collective-permute-start.15 = (f32[2,3,1,2,1,1,16,512]{7,6,5,4,3,2,1,0:T(8,128)}, f32[2,3,1,2,1,1,16,512]{7,6,5,4,3,2,1,0:T(8,128)}, u32[]{:S(2)}, u32[]{:S(2)}) collective-permute-start(f32[2,3,1,2,1,1,16,512]{7,6,5,4,3,2,1,0:T(8,128)} %pad_maximum_fusion.6), channel_id=1, source_target_pairs={{0,256},{1,257},{2,258},{3,259},{4,260},{5,261},{6,262},{7,263},{8... | collective-permute-start | bytes 1179656 | tf_op jit(solution)/shard_map/ppermute | solution.py:21
  92.0 4.4 %collective-permute-done.2 = f32[2,128,512]{2,1,0:T(8,128)S(1)} collective-permute-done((f32[2,128,512]{2,1,0:T(8,128)S(1)}, f32[2,128,512]{2,1,0:T(8,128)S(1)}, u32[]{:S(2)}, u32[]{:S(2)}) %collective-permute-start.2) | collective-permute-done | bytes 524320 | tf_op jit(solution)/shard_map/ppermute | solution.py:21
  97.2 4.7 %collective-permute-done.3 = f32[2,128,512]{2,1,0:T(8,128)S(1)} collective-permute-done((f32[2,128,512]{2,1,0:T(8,128)S(1)}, f32[2,128,512]{2,1,0:T(8,128)S(1)}, u32[]{:S(2)}, u32[]{:S(2)}) %collective-permute-start.3) | collective-permute-done | bytes 524320 | tf_op jit(solution)/shard_map/ppermute | solution.py:21
  101.9 1.9 collective-permute-start.20
  104.0 1.5 constant_dynamic-slice_fusion
  105.5 3.2 collective-permute-start.17
  108.9 1.1 pad_maximum_fusion.2
  110.7 6.9 %collective-permute-start.4 = (f32[4,2,128,512]{3,2,1,0:T(8,128)}, f32[4,2,128,512]{3,2,1,0:T(8,128)}, u32[]{:S(2)}, u32[]{:S(2)}) collective-permute-start(f32[4,2,128,512]{3,2,1,0:T(8,128)} %constant_dynamic-slice_fusion), channel_id=1, source_target_pairs={{0,1},{1,0},{2,3},{3,2},{4,5},{5,4},{6,7},{7,6},{8,9},{9,8},{10,11... | collective-permute-start | bytes 6291464 | tf_op jit(solution)/shard_map/ppermute | solution.py:21
  117.6 1.7 collective-permute-start.9
  119.2 1.5 fusion.21
  120.8 1.9 constant_dynamic-update-slice_fusion.10
  122.6 3.6 %collective-permute-start.18 = (f32[2,3,1,2,1,1,16,512]{7,6,5,4,3,2,1,0:T(8,128)S(1)}, f32[2,3,1,2,1,1,16,512]{7,6,5,4,3,2,1,0:T(8,128)S(1)}, u32[]{:S(2)}, u32[]{:S(2)}) collective-permute-start(f32[2,3,1,2,1,1,16,512]{7,6,5,4,3,2,1,0:T(8,128)S(1)} %collective-permute-done.16), channel_id=1, source_target_pairs={{0,384},{1,385},{2,386},{3,387},{4,388},{5,389},{6,390},{7,391},{8... | collective-permute-start | bytes 1179656 | tf_op jit(solution)/shard_map/ppermute | solution.py:21
  126.3 1.8 constant_dynamic-update-slice_fusion.9
  128.1 2.7 collective-permute-start.19
  130.8 1.8 constant_dynamic-update-slice_fusion.8
  133.4 1.8 constant_dynamic-update-slice_fusion.6
  135.2 2.6 collective-permute-start.21
  138.6 2.6 collective-permute-start.22
  141.2 3.5 %collective-permute-done.19 = f32[2,3,1,2,1,1,16,512]{7,6,5,4,3,2,1,0:T(8,128)S(1)} collective-permute-done((f32[2,3,1,2,1,1,16,512]{7,6,5,4,3,2,1,0:T(8,128)S(1)}, f32[2,3,1,2,1,1,16,512]{7,6,5,4,3,2,1,0:T(8,128)S(1)}, u32[]{:S(2)}, u32[]{:S(2)}) %collective-permute-start.19) | collective-permute-done | bytes 393248 | tf_op jit(solution)/shard_map/ppermute | solution.py:21
  145.6 4.0 %collective-permute-start.23 = (f32[2,3,1,2,2,1,16,512]{7,6,5,4,3,2,1,0:T(8,128)}, f32[2,3,1,2,2,1,16,512]{7,6,5,4,3,2,1,0:T(8,128)S(1)}, u32[]{:S(2)}, u32[]{:S(2)}) collective-permute-start(f32[2,3,1,2,2,1,16,512]{7,6,5,4,3,2,1,0:T(8,128)} %collective-permute-done.20), channel_id=1, source_target_pairs={{0,256},{1,257},{2,258},{3,259},{4,260},{5,261},{6,262},{7,263},{8... | collective-permute-start | bytes 2359304 | tf_op jit(solution)/shard_map/ppermute | solution.py:21
  149.6 2.1 constant_dynamic-update-slice_fusion.3
  151.8 6.6 %collective-permute-start.24 = (f32[512,512]{1,0:T(8,128)S(1)}, f32[512,512]{1,0:T(8,128)S(1)}, u32[]{:S(2)}, u32[]{:S(2)}) collective-permute-start(f32[512,512]{1,0:T(8,128)S(1)} %copy-done.6), channel_id=1, source_target_pairs={{0,16},{1,17},{2,18},{3,19},{4,20},{5,21},{6,22},{7,23},{8,24},{9,... | collective-permute-start | bytes 3145736 | tf_op jit(solution)/shard_map/ppermute | solution.py:21
  158.4 1.5 broadcast_select_fusion.3
  160.1 6.5 %collective-permute-start.25 = (f32[512,512]{1,0:T(8,128)S(1)}, f32[512,512]{1,0:T(8,128)S(1)}, u32[]{:S(2)}, u32[]{:S(2)}) collective-permute-start(f32[512,512]{1,0:T(8,128)S(1)} %copy-done.6), channel_id=1, source_target_pairs={{16,0},{17,1},{18,2},{19,3},{20,4},{21,5},{22,6},{23,7},{24,8},{25... | collective-permute-start | bytes 3145736 | tf_op jit(solution)/shard_map/ppermute | solution.py:21
  167.6 1.9 collective-permute-start.10
  169.5 1.0 constant_dynamic-update-slice_fusion.1
  170.5 7.2 %collective-permute-done.23 = f32[2,3,1,2,2,1,16,512]{7,6,5,4,3,2,1,0:T(8,128)S(1)} collective-permute-done((f32[2,3,1,2,2,1,16,512]{7,6,5,4,3,2,1,0:T(8,128)}, f32[2,3,1,2,2,1,16,512]{7,6,5,4,3,2,1,0:T(8,128)S(1)}, u32[]{:S(2)}, u32[]{:S(2)}) %collective-permute-start.23) | collective-permute-done | bytes 786464 | tf_op jit(solution)/shard_map/ppermute | solution.py:21
  177.7 14.1 %collective-permute-start.11 = (f32[512,512]{1,0:T(8,128)S(1)}, f32[512,512]{1,0:T(8,128)S(1)}, u32[]{:S(2)}, u32[]{:S(2)}) collective-permute-start(f32[512,512]{1,0:T(8,128)S(1)} %copy-done.5), channel_id=1, source_target_pairs={{16,0},{17,1},{18,2},{19,3},{20,4},{21,5},{22,6},{23,7},{24,8},{25... | collective-permute-start | bytes 3145736 | tf_op jit(solution)/shard_map/ppermute | solution.py:21
  191.9 1.0 constant_dynamic-update-slice_fusion
  192.9 2.3 broadcast_select_fusion.1
  196.9 1.1 fusion.16
  198.1 1.1 convolution_add_fusion.4
  199.3 10.9 %collective-permute-done.25 = f32[512,512]{1,0:T(8,128)S(1)} collective-permute-done((f32[512,512]{1,0:T(8,128)S(1)}, f32[512,512]{1,0:T(8,128)S(1)}, u32[]{:S(2)}, u32[]{:S(2)}) %collective-permute-start.25) | collective-permute-done | bytes 1048608 | tf_op jit(solution)/shard_map/ppermute | solution.py:21
  210.2 1.1 convolution_add_fusion.3
  211.3 17.6 %collective-permute-start.26 = (f32[512,512]{1,0:T(8,128)S(1)}, f32[512,512]{1,0:T(8,128)}, u32[]{:S(2)}, u32[]{:S(2)}) collective-permute-start(f32[512,512]{1,0:T(8,128)S(1)} %convolution_add_fusion.3), channel_id=1, source_target_pairs={{0,1},{1,2},{2,3},{3,4},{4,5},{5,6},{6,7},{7,8},{8,9},{9,10},{10,1... | collective-permute-start | bytes 3145736 | tf_op jit(solution)/shard_map/ppermute | solution.py:21
  228.9 1.1 fusion.18
  230.9 1.1 convolution_add_fusion.7
  232.0 56.9 %collective-permute-done.11 = f32[512,512]{1,0:T(8,128)S(1)} collective-permute-done((f32[512,512]{1,0:T(8,128)S(1)}, f32[512,512]{1,0:T(8,128)S(1)}, u32[]{:S(2)}, u32[]{:S(2)}) %collective-permute-start.11) | collective-permute-done | bytes 1048608 | tf_op jit(solution)/shard_map/ppermute | solution.py:21
  288.9 1.1 convolution_add_fusion.6
  289.9 3.2 fusion.1
  293.2 6.0 %collective-permute-start.27 = (f32[512,512]{1,0:T(8,128)S(1)}, f32[512,512]{1,0:T(8,128)}, u32[]{:S(2)}, u32[]{:S(2)}) collective-permute-start(f32[512,512]{1,0:T(8,128)S(1)} %convolution_add_fusion.6), channel_id=1, source_target_pairs={{1,0},{2,1},{3,2},{4,3},{5,4},{6,5},{7,6},{8,7},{9,8},{10,9},{11,1... | collective-permute-start | bytes 3145736 | tf_op jit(solution)/shard_map/ppermute | solution.py:21
  299.1 3.2 fusion
  302.4 1.1 copy.10
  303.4 1.6 copy.11
  305.0 2.7 convolution_add_fusion.5
  307.7 2.3 convolution_add_fusion.1
  310.1 2.6 convolution_add_fusion.2
  312.7 30.0 %collective-permute-done.27 = f32[512,512]{1,0:T(8,128)} collective-permute-done((f32[512,512]{1,0:T(8,128)S(1)}, f32[512,512]{1,0:T(8,128)}, u32[]{:S(2)}, u32[]{:S(2)}) %collective-permute-start.27) | collective-permute-done | bytes 1048608 | tf_op jit(solution)/shard_map/ppermute | solution.py:21
  342.7 2.6 convolution_add_fusion
  345.5 1.8 copy.12
  (73 shorter events, 16.3 us)
Async XLA Ops:
  0.0 72.0 %copy-start.7 = (f32[1,3,512,32]{2,3,1,0:T(8,128)S(1)}, f32[1,3,512,32]{2,3,1,0:T(8,128)}, u32[]{:S(2)}) copy-start(f32[1,3,512,32]{2,3,1,0:T(8,128)} %param.6) | copy-start | bytes 589828
  0.9 11.1 %collective-permute-start.5 = (f32[1,16,1024]{2,1,0:T(8,128)S(1)}, f32[1,16,1024]{2,1,0:T(8,128)S(1)}, u32[]{:S(2)}, u32[]{:S(2)}) collective-permute-start(f32[1,16,1024]{2,1,0:T(8,128)S(1)} %slice_select_fusion), channel_id=1, source_target_pairs={{0,64},{1,65},{2,66},{3,67},{4,68},{5,69},{6,70},{7,71},{8,72},{9,... | collective-permute-start | bytes 196616 | tf_op jit(solution)/shard_map/ppermute | solution.py:21
  9.8 53.3 %collective-permute-start.12 = (f32[2,3,1,1,1,1,16,512]{7,6,5,4,3,2,1,0:T(8,128)}, f32[2,3,1,1,1,1,16,512]{7,6,5,4,3,2,1,0:T(8,128)S(1)}, u32[]{:S(2)}, u32[]{:S(2)}) collective-permute-start(f32[2,3,1,1,1,1,16,512]{7,6,5,4,3,2,1,0:T(8,128)} %bitcast.102), channel_id=1, source_target_pairs={{0,64},{1,65},{2,66},{3,67},{4,68},{5,69},{6,70},{7,71},{8,72},{9,... | collective-permute-start | bytes 589832 | tf_op jit(solution)/shard_map/ppermute | solution.py:21
  12.9 29.4 %collective-permute-start.6 = (f32[2,1,1,16,1024]{4,3,2,1,0:T(8,128)S(1)}, f32[2,1,1,16,1024]{4,3,2,1,0:T(8,128)S(1)}, u32[]{:S(2)}, u32[]{:S(2)}) collective-permute-start(f32[2,1,1,16,1024]{4,3,2,1,0:T(8,128)S(1)} %maximum_bitcast_fusion.1), channel_id=1, source_target_pairs={{32,0},{33,1},{34,2},{35,3},{36,4},{37,5},{38,6},{39,7},{40,8},{41... | collective-permute-start | bytes 393224 | tf_op jit(solution)/shard_map/ppermute | solution.py:21
  16.0 56.0 %collective-permute-start = (f32[128,512]{1,0:T(8,128)S(1)}, f32[128,512]{1,0:T(8,128)S(1)}, u32[]{:S(2)}, u32[]{:S(2)}) collective-permute-start(f32[128,512]{1,0:T(8,128)S(1)} %pad_maximum_fusion.7), channel_id=1, source_target_pairs={{0,8},{1,9},{2,10},{3,11},{4,12},{5,13},{6,14},{7,15},{8,0},{9,1},... | collective-permute-start | bytes 786440 | tf_op jit(solution)/shard_map/ppermute | solution.py:21
  42.4 32.2 %collective-permute-start.7 = (f32[2,2,1,16,1024]{4,3,2,1,0:T(8,128)S(1)}, f32[2,2,1,16,1024]{4,3,2,1,0:T(8,128)S(1)}, u32[]{:S(2)}, u32[]{:S(2)}) collective-permute-start(f32[2,2,1,16,1024]{4,3,2,1,0:T(8,128)S(1)} %pad_maximum_fusion.9), channel_id=1, source_target_pairs={{16,0},{17,1},{18,2},{19,3},{20,4},{21,5},{22,6},{23,7},{24,8},{25... | collective-permute-start | bytes 786440 | tf_op jit(solution)/shard_map/ppermute | solution.py:21
  64.8 18.6 %collective-permute-start.16 = (f32[2,3,1,2,1,1,16,512]{7,6,5,4,3,2,1,0:T(8,128)}, f32[2,3,1,2,1,1,16,512]{7,6,5,4,3,2,1,0:T(8,128)S(1)}, u32[]{:S(2)}, u32[]{:S(2)}) collective-permute-start(f32[2,3,1,2,1,1,16,512]{7,6,5,4,3,2,1,0:T(8,128)} %pad_maximum_fusion.6), channel_id=1, source_target_pairs={{0,32},{1,33},{2,34},{3,35},{4,36},{5,37},{6,38},{7,39},{8,40},{9,... | collective-permute-start | bytes 1179656 | tf_op jit(solution)/shard_map/ppermute | solution.py:21
  66.7 43.2 %collective-permute-start.13 = (f32[2,3,1,2,1,1,16,512]{7,6,5,4,3,2,1,0:T(8,128)}, f32[2,3,1,2,1,1,16,512]{7,6,5,4,3,2,1,0:T(8,128)S(1)}, u32[]{:S(2)}, u32[]{:S(2)}) collective-permute-start(f32[2,3,1,2,1,1,16,512]{7,6,5,4,3,2,1,0:T(8,128)} %pad_maximum_fusion.6), channel_id=1, source_target_pairs={{0,128},{1,129},{2,130},{3,131},{4,132},{5,133},{6,134},{7,135},{8... | collective-permute-start | bytes 1179656 | tf_op jit(solution)/shard_map/ppermute | solution.py:21
  69.8 47.7 %collective-permute-start.14 = (f32[2,3,1,2,1,1,16,512]{7,6,5,4,3,2,1,0:T(8,128)}, f32[2,3,1,2,1,1,16,512]{7,6,5,4,3,2,1,0:T(8,128)}, u32[]{:S(2)}, u32[]{:S(2)}) collective-permute-start(f32[2,3,1,2,1,1,16,512]{7,6,5,4,3,2,1,0:T(8,128)} %pad_maximum_fusion.6), channel_id=1, source_target_pairs={{0,384},{1,385},{2,386},{3,387},{4,388},{5,389},{6,390},{7,391},{8... | collective-permute-start | bytes 1179656 | tf_op jit(solution)/shard_map/ppermute | solution.py:21
  72.2 16.1 %collective-permute-start.1 = (f32[2,128,512]{2,1,0:T(8,128)S(1)}, f32[2,128,512]{2,1,0:T(8,128)S(1)}, u32[]{:S(2)}, u32[]{:S(2)}) collective-permute-start(f32[2,128,512]{2,1,0:T(8,128)S(1)} %pad_maximum_fusion.4), channel_id=1, source_target_pairs={{0,6},{1,7},{2,0},{3,1},{4,2},{5,3},{6,4},{7,5},{8,14},{9,15},{10,... | collective-permute-start | bytes 1572872 | tf_op jit(solution)/shard_map/ppermute | solution.py:21
  74.6 21.9 %collective-permute-start.2 = (f32[2,128,512]{2,1,0:T(8,128)S(1)}, f32[2,128,512]{2,1,0:T(8,128)S(1)}, u32[]{:S(2)}, u32[]{:S(2)}) collective-permute-start(f32[2,128,512]{2,1,0:T(8,128)S(1)} %pad_maximum_fusion.4), channel_id=1, source_target_pairs={{0,4},{1,5},{2,6},{3,7},{4,0},{5,1},{6,2},{7,3},{8,12},{9,13},{10,... | collective-permute-start | bytes 1572872 | tf_op jit(solution)/shard_map/ppermute | solution.py:21
  83.4 18.5 %collective-permute-start.3 = (f32[2,128,512]{2,1,0:T(8,128)S(1)}, f32[2,128,512]{2,1,0:T(8,128)S(1)}, u32[]{:S(2)}, u32[]{:S(2)}) collective-permute-start(f32[2,128,512]{2,1,0:T(8,128)S(1)} %pad_maximum_fusion.4), channel_id=1, source_target_pairs={{0,2},{1,3},{2,4},{3,5},{4,6},{5,7},{6,0},{7,1},{8,10},{9,11},{10,... | collective-permute-start | bytes 1572872 | tf_op jit(solution)/shard_map/ppermute | solution.py:21
  86.2 17.8 %copy-start = (f32[2,3,4,2,2,2,16,512]{7,6,5,4,3,2,1,0:T(8,128)}, f32[2,3,4,2,2,2,16,512]{7,6,5,4,3,2,1,0:T(8,128)S(1)}, u32[]{:S(2)}) copy-start(f32[2,3,4,2,2,2,16,512]{7,6,5,4,3,2,1,0:T(8,128)S(1)} %get-tuple-element.23) | copy-start | bytes 18874372
  88.2 34.4 %collective-permute-start.15 = (f32[2,3,1,2,1,1,16,512]{7,6,5,4,3,2,1,0:T(8,128)}, f32[2,3,1,2,1,1,16,512]{7,6,5,4,3,2,1,0:T(8,128)}, u32[]{:S(2)}, u32[]{:S(2)}) collective-permute-start(f32[2,3,1,2,1,1,16,512]{7,6,5,4,3,2,1,0:T(8,128)} %pad_maximum_fusion.6), channel_id=1, source_target_pairs={{0,256},{1,257},{2,258},{3,259},{4,260},{5,261},{6,262},{7,263},{8... | collective-permute-start | bytes 1179656 | tf_op jit(solution)/shard_map/ppermute | solution.py:21
  96.4 9.1 %collective-permute-start.8 = (f32[1,128,1024]{2,1,0:T(8,128)S(1)}, f32[1,128,1024]{2,1,0:T(8,128)S(1)}, u32[]{:S(2)}, u32[]{:S(2)}) collective-permute-start(f32[1,128,1024]{2,1,0:T(8,128)S(1)} %bitcast.98), channel_id=1, source_target_pairs={{112,240},{113,241},{114,242},{115,243},{116,244},{117,245},{118,2... | collective-permute-start | bytes 1572872 | tf_op jit(solution)/shard_map/ppermute | solution.py:21
  101.9 33.3 %collective-permute-start.20 = (f32[2,3,1,2,2,1,16,512]{7,6,5,4,3,2,1,0:T(8,128)}, f32[2,3,1,2,2,1,16,512]{7,6,5,4,3,2,1,0:T(8,128)}, u32[]{:S(2)}, u32[]{:S(2)}) collective-permute-start(f32[2,3,1,2,2,1,16,512]{7,6,5,4,3,2,1,0:T(8,128)} %pad_maximum_fusion.3), channel_id=1, source_target_pairs={{0,16},{1,17},{2,18},{3,19},{4,20},{5,21},{6,22},{7,23},{8,24},{9,... | collective-permute-start | bytes 2359304 | tf_op jit(solution)/shard_map/ppermute | solution.py:21
  104.0 5.9 %copy-start.2 = (f32[8,2,128,512]{3,2,1,0:T(8,128)}, f32[8,2,128,512]{3,2,1,0:T(8,128)S(1)}, u32[]{:S(2)}) copy-start(f32[8,2,128,512]{3,2,1,0:T(8,128)S(1)} %bitcast_dynamic-update-slice_fusion.1) | copy-start | bytes 12582916
  104.0 15.2 %copy-start.1 = (f32[512,1024]{1,0:T(8,128)S(1)}, f32[512,1024]{1,0:T(8,128)}, u32[]{:S(2)}) copy-start(f32[512,1024]{1,0:T(8,128)} %param.5) | copy-start | bytes 6291460
  105.5 22.6 %collective-permute-start.17 = (f32[2,3,1,2,1,1,16,512]{7,6,5,4,3,2,1,0:T(8,128)S(1)}, f32[2,3,1,2,1,1,16,512]{7,6,5,4,3,2,1,0:T(8,128)}, u32[]{:S(2)}, u32[]{:S(2)}) collective-permute-start(f32[2,3,1,2,1,1,16,512]{7,6,5,4,3,2,1,0:T(8,128)S(1)} %collective-permute-done.16), channel_id=1, source_target_pairs={{0,128},{1,129},{2,130},{3,131},{4,132},{5,133},{6,134},{7,135},{8... | collective-permute-start | bytes 1179656 | tf_op jit(solution)/shard_map/ppermute | solution.py:21
  110.0 0.7 copy-start.8
  110.7 82.2 %collective-permute-start.4 = (f32[4,2,128,512]{3,2,1,0:T(8,128)}, f32[4,2,128,512]{3,2,1,0:T(8,128)}, u32[]{:S(2)}, u32[]{:S(2)}) collective-permute-start(f32[4,2,128,512]{3,2,1,0:T(8,128)} %constant_dynamic-slice_fusion), channel_id=1, source_target_pairs={{0,1},{1,0},{2,3},{3,2},{4,5},{5,4},{6,7},{7,6},{8,9},{9,8},{10,11... | collective-permute-start | bytes 6291464 | tf_op jit(solution)/shard_map/ppermute | solution.py:21
  117.6 34.2 %collective-permute-start.9 = (f32[2,128,1024]{2,1,0:T(8,128)}, f32[2,128,1024]{2,1,0:T(8,128)}, u32[]{:S(2)}, u32[]{:S(2)}) collective-permute-start(f32[2,128,1024]{2,1,0:T(8,128)} %pad_maximum_fusion.2), channel_id=1, source_target_pairs={{240,496},{241,497},{242,498},{243,499},{244,500},{245,501},{246,5... | collective-permute-start | bytes 3145736 | tf_op jit(solution)/shard_map/ppermute | solution.py:21
  120.8 31.0 %copy-start.6 = (f32[512,512]{1,0:T(8,128)S(1)}, f32[512,512]{1,0:T(8,128)}, u32[]{:S(2)}) copy-start(f32[512,512]{1,0:T(8,128)} %get-tuple-element.12) | copy-start | bytes 3145732
  122.6 15.1 %collective-permute-start.18 = (f32[2,3,1,2,1,1,16,512]{7,6,5,4,3,2,1,0:T(8,128)S(1)}, f32[2,3,1,2,1,1,16,512]{7,6,5,4,3,2,1,0:T(8,128)S(1)}, u32[]{:S(2)}, u32[]{:S(2)}) collective-permute-start(f32[2,3,1,2,1,1,16,512]{7,6,5,4,3,2,1,0:T(8,128)S(1)} %collective-permute-done.16), channel_id=1, source_target_pairs={{0,384},{1,385},{2,386},{3,387},{4,388},{5,389},{6,390},{7,391},{8... | collective-permute-start | bytes 1179656 | tf_op jit(solution)/shard_map/ppermute | solution.py:21
  128.1 16.7 %collective-permute-start.19 = (f32[2,3,1,2,1,1,16,512]{7,6,5,4,3,2,1,0:T(8,128)S(1)}, f32[2,3,1,2,1,1,16,512]{7,6,5,4,3,2,1,0:T(8,128)S(1)}, u32[]{:S(2)}, u32[]{:S(2)}) collective-permute-start(f32[2,3,1,2,1,1,16,512]{7,6,5,4,3,2,1,0:T(8,128)S(1)} %collective-permute-done.16), channel_id=1, source_target_pairs={{0,256},{1,257},{2,258},{3,259},{4,260},{5,261},{6,262},{7,263},{8... | collective-permute-start | bytes 1179656 | tf_op jit(solution)/shard_map/ppermute | solution.py:21
  135.2 24.9 %collective-permute-start.21 = (f32[2,3,1,2,2,1,16,512]{7,6,5,4,3,2,1,0:T(8,128)}, f32[2,3,1,2,2,1,16,512]{7,6,5,4,3,2,1,0:T(8,128)S(1)}, u32[]{:S(2)}, u32[]{:S(2)}) collective-permute-start(f32[2,3,1,2,2,1,16,512]{7,6,5,4,3,2,1,0:T(8,128)} %collective-permute-done.20), channel_id=1, source_target_pairs={{0,128},{1,129},{2,130},{3,131},{4,132},{5,133},{6,134},{7,135},{8... | collective-permute-start | bytes 2359304 | tf_op jit(solution)/shard_map/ppermute | solution.py:21
  138.6 29.0 %collective-permute-start.22 = (f32[2,3,1,2,2,1,16,512]{7,6,5,4,3,2,1,0:T(8,128)}, f32[2,3,1,2,2,1,16,512]{7,6,5,4,3,2,1,0:T(8,128)S(1)}, u32[]{:S(2)}, u32[]{:S(2)}) collective-permute-start(f32[2,3,1,2,2,1,16,512]{7,6,5,4,3,2,1,0:T(8,128)} %collective-permute-done.20), channel_id=1, source_target_pairs={{0,384},{1,385},{2,386},{3,387},{4,388},{5,389},{6,390},{7,391},{8... | collective-permute-start | bytes 2359304 | tf_op jit(solution)/shard_map/ppermute | solution.py:21
  145.6 32.1 %collective-permute-start.23 = (f32[2,3,1,2,2,1,16,512]{7,6,5,4,3,2,1,0:T(8,128)}, f32[2,3,1,2,2,1,16,512]{7,6,5,4,3,2,1,0:T(8,128)S(1)}, u32[]{:S(2)}, u32[]{:S(2)}) collective-permute-start(f32[2,3,1,2,2,1,16,512]{7,6,5,4,3,2,1,0:T(8,128)} %collective-permute-done.20), channel_id=1, source_target_pairs={{0,256},{1,257},{2,258},{3,259},{4,260},{5,261},{6,262},{7,263},{8... | collective-permute-start | bytes 2359304 | tf_op jit(solution)/shard_map/ppermute | solution.py:21
  151.8 15.9 %copy-start.5 = (f32[512,512]{1,0:T(8,128)S(1)}, f32[512,512]{1,0:T(8,128)}, u32[]{:S(2)}) copy-start(f32[512,512]{1,0:T(8,128)} %get-tuple-element.11) | copy-start | bytes 3145732
  151.8 46.4 %collective-permute-start.24 = (f32[512,512]{1,0:T(8,128)S(1)}, f32[512,512]{1,0:T(8,128)S(1)}, u32[]{:S(2)}, u32[]{:S(2)}) collective-permute-start(f32[512,512]{1,0:T(8,128)S(1)} %copy-done.6), channel_id=1, source_target_pairs={{0,16},{1,17},{2,18},{3,19},{4,20},{5,21},{6,22},{7,23},{8,24},{9,... | collective-permute-start | bytes 3145736 | tf_op jit(solution)/shard_map/ppermute | solution.py:21
  159.8 33.1 %copy-start.3 = (f32[8,2,128,512]{3,2,1,0:T(8,128)S(1)}, f32[8,2,128,512]{3,2,1,0:T(8,128)}, u32[]{:S(2)}) copy-start(f32[8,2,128,512]{3,2,1,0:T(8,128)} %copy-done.2) | copy-start | bytes 12582916
  160.1 50.1 %collective-permute-start.25 = (f32[512,512]{1,0:T(8,128)S(1)}, f32[512,512]{1,0:T(8,128)S(1)}, u32[]{:S(2)}, u32[]{:S(2)}) collective-permute-start(f32[512,512]{1,0:T(8,128)S(1)} %copy-done.6), channel_id=1, source_target_pairs={{16,0},{17,1},{18,2},{19,3},{20,4},{21,5},{22,6},{23,7},{24,8},{25... | collective-permute-start | bytes 3145736 | tf_op jit(solution)/shard_map/ppermute | solution.py:21
  167.6 63.2 %collective-permute-start.10 = (f32[512,512]{1,0:T(8,128)S(1)}, f32[512,512]{1,0:T(8,128)S(1)}, u32[]{:S(2)}, u32[]{:S(2)}) collective-permute-start(f32[512,512]{1,0:T(8,128)S(1)} %copy-done.5), channel_id=1, source_target_pairs={{0,16},{1,17},{2,18},{3,19},{4,20},{5,21},{6,22},{7,23},{8,24},{9,... | collective-permute-start | bytes 3145736 | tf_op jit(solution)/shard_map/ppermute | solution.py:21
  177.7 111.1 %collective-permute-start.11 = (f32[512,512]{1,0:T(8,128)S(1)}, f32[512,512]{1,0:T(8,128)S(1)}, u32[]{:S(2)}, u32[]{:S(2)}) collective-permute-start(f32[512,512]{1,0:T(8,128)S(1)} %copy-done.5), channel_id=1, source_target_pairs={{16,0},{17,1},{18,2},{19,3},{20,4},{21,5},{22,6},{23,7},{24,8},{25... | collective-permute-start | bytes 3145736 | tf_op jit(solution)/shard_map/ppermute | solution.py:21
  211.3 98.8 %collective-permute-start.26 = (f32[512,512]{1,0:T(8,128)S(1)}, f32[512,512]{1,0:T(8,128)}, u32[]{:S(2)}, u32[]{:S(2)}) collective-permute-start(f32[512,512]{1,0:T(8,128)S(1)} %convolution_add_fusion.3), channel_id=1, source_target_pairs={{0,1},{1,2},{2,3},{3,4},{4,5},{5,6},{6,7},{7,8},{8,9},{9,10},{10,1... | collective-permute-start | bytes 3145736 | tf_op jit(solution)/shard_map/ppermute | solution.py:21
  293.2 49.5 %collective-permute-start.27 = (f32[512,512]{1,0:T(8,128)S(1)}, f32[512,512]{1,0:T(8,128)}, u32[]{:S(2)}, u32[]{:S(2)}) collective-permute-start(f32[512,512]{1,0:T(8,128)S(1)} %convolution_add_fusion.6), channel_id=1, source_target_pairs={{1,0},{2,1},{3,2},{4,3},{5,4},{6,5},{7,6},{8,7},{9,8},{10,9},{11,1... | collective-permute-start | bytes 3145736 | tf_op jit(solution)/shard_map/ppermute | solution.py:21
  305.0 2.7 copy-start.4

commit v2 on v1

v2 whole, which is shorter than its diff:
```python
import jax
import jax.numpy as jnp
from jax import lax
from jax.experimental import pallas as pl
from jax.experimental.pallas import tpu as pltpu
from jax.sharding import PartitionSpec as P

NX, NZ, NH, NY, NC = 4, 8, 2, 4, 2
AXES = ("row", "col")


def moved(array, target):
    pairs = []
    for x in range(NX):
        for z in range(NZ):
            for h in range(NH):
                for y in range(NY):
                    for c in range(NC):
                        to = target(x, z, h, y, c)
                        if to is not None:
                            pairs.append((flat(x, z, h, y, c), flat(*to)))
    return lax.ppermute(array, AXES, pairs)


def flat(x, z, h, y, c):
    return (((x * NZ + z) * NH + h) * NY + y) * NC + c


def row_step(d):
    def target(x, z, h, y, c):
        r = x * NZ + z + d
        return (r // NZ, r % NZ, h, y, c) if 0 <= r < NX * NZ else None

    return target


def col_step(d):
    def target(x, z, h, y, c):
        k = (h * NY + y) * NC + c + d
        return (x, z, k // 8, k % 8 // 2, k % 2) if 0 <= k < 16 else None

    return target


def x_step(d):
    return lambda x, z, h, y, c: ((x + d) % NX, z, h, y, c)


def y_step(d):
    return lambda x, z, h, y, c: (x, z, h, (y + d) % NY, c)


def z_swap(bit):
    return lambda x, z, h, y, c: (x, z ^ bit, h, y, c)


def rows_of(band):
    return moved(band, row_step(1)), moved(band, row_step(-1))


def h_swap(x, z, h, y, c):
    return (x, z, 1 - h, y, c)


def core_swap(x, z, h, y, c):
    return (x, z, h, y, 1 - c)


def after(array, *others):
    return lax.optimization_barrier((array, *others))[0]


def left_first(left, edge, h):
    other = moved(jnp.concatenate([left, jnp.where(h == 0, edge[1], edge[0])], axis=0), h_swap)
    own = jnp.concatenate([left, jnp.where(h == 0, edge[0], edge[1])], axis=0)
    return jnp.stack([own, other])


def left_second(pair, place, *gate):
    pieces = [pair, moved(pair, y_step(-1)), moved(pair, y_step(2)), moved(pair, y_step(1))]
    mates = [moved(after(piece, *gate), core_swap) for piece in pieces]
    return assembled(place, pieces + mates)


def assemble_kernel(place_ref, *refs):
    pieces, (high_ref, low_ref, side_ref) = refs[:8], refs[8:]
    h, y, c = place_ref[0], place_ref[1], place_ref[2]
    for k, piece in enumerate(pieces):
        core = c if k < 4 else 1 - c
        line = lax.rem(y + k % 4, NY)
        for far in range(2):
            side = h if far == 0 else 1 - h
            at = pl.multiple_of(((side * NY + line) * NC + core) * 32, 32)
            for m in range(3):
                high, low = split(piece[far, pl.ds(m * 32, 32), :])
                high_ref[m, pl.ds(at, 32), :] = high
                low_ref[m, pl.ds(at, 32), :] = low
            side_ref[pl.ds(at, 32), :] = piece[far, pl.ds(96, 32), :]


def assembled(place, pieces):
    size = pieces[0].shape[2]
    half = jax.ShapeDtypeStruct((3, size, size), jnp.bfloat16)
    return pl.pallas_call(
        assemble_kernel,
        out_shape=(half, half, jax.ShapeDtypeStruct((size, size), jnp.float32)),
        in_specs=[pl.BlockSpec(memory_space=pltpu.SMEM)]
        + [pl.BlockSpec(memory_space=pltpu.VMEM)] * 8,
        out_specs=(pl.BlockSpec(memory_space=pltpu.VMEM),) * 3,
        compiler_params=PARAMS,
        cost_estimate=pl.CostEstimate(
            flops=0, bytes_accessed=32 * size**2, transcendentals=0
        ),
    )(place, *pieces)


def half_kernel(place_ref, band_ref, outside_ref, high_ref, low_ref, *refs):
    (*parts, out_ref) = refs
    upper, lower = (
        jnp.concatenate([ref[...] for ref in parts[k::2]], axis=1) for k in range(2)
    )
    outside = outside_ref[...]
    blocks = (
        jnp.where(place_ref[1] == 0, outside, upper),
        band_ref[...],
        jnp.where(place_ref[1] == NX * NZ - 1, outside, lower),
    )
    dims = (((0,), (0,)), ((), ()))
    total = None
    for m in (1, 0, 2):
        high, low = split(blocks[m])
        for left, block in ((high_ref, low), (low_ref, high), (high_ref, high)):
            part = lax.dot_general(left[m], block, dims, preferred_element_type=jnp.float32)
            total = part if total is None else total + part
    out_ref[...] = total


def half_products(inner, place, covariance, outside, high, low, parts):
    parts = [piece for part in parts for piece in part]
    size = covariance.shape[0]
    column = pl.BlockSpec((size, size), lambda i, place: (0, place[0] ^ inner))
    return pl.pallas_call(
        half_kernel,
        out_shape=jax.ShapeDtypeStruct((size, size), jnp.float32),
        grid_spec=pltpu.PrefetchScalarGridSpec(
            num_scalar_prefetch=1,
            grid=(1,),
            in_specs=[column, column]
            + [whole(3, size, size)] * 2
            + [whole(*piece.shape) for piece in parts],
            out_specs=whole(size, size),
        ),
        compiler_params=PARAMS,
        cost_estimate=pl.CostEstimate(
            flops=18 * size**3, bytes_accessed=32 * size**2, transcendentals=0
        ),
    )(place, covariance, outside, high, low, *parts)


def gather_line(right):
    lines = [[x * NZ + z for z in range(NZ)] for x in range(NX)]
    return lax.all_gather(right, "row", axis_index_groups=lines, axis=2, tiled=True)


def gather_ring(line):
    rings = [[x * NZ + z for x in range(NX)] for z in range(NZ)]
    return lax.all_gather(line, "row", axis_index_groups=rings, axis=2, tiled=True)


def outward(x, z, h, y, c):
    return col_step(1 if c == 1 else -1)(x, z, h, y, c)


def toward(bit):
    def target(x, z, h, y, c):
        if bit == 4:
            return (x, z ^ 4, h, y, c)
        low = z < 4
        rest = z if low else NZ - 1 - z
        if bit <= rest < 2 * bit:
            return (x, z - bit if low else z + bit, h, y, c)
        return None

    return target


def rows_first(edge, z, gate):
    low = z < 4
    keep = jnp.where(low, edge[0], edge[1])[None]
    send = jnp.where(low, edge[1], edge[0])[None]
    got = moved(send, toward(4))
    block = jnp.concatenate([jnp.where(low, keep, got), jnp.where(low, got, keep)])
    block = block.reshape(2, 1, 1, 16, 1024)
    got = moved(after(block, gate), toward(2))
    block = jnp.concatenate([jnp.where(low, block, got), jnp.where(low, got, block)], axis=1)
    got = moved(block, toward(1))
    block = jnp.concatenate([jnp.where(low, block, got), jnp.where(low, got, block)], axis=2)
    return block.reshape(1, 128, 1024)


def rows_second(block, z, *gate):
    low = z < 4

    def x_one(x, z, h, y, c):
        if z == 0:
            return (x - 1, z, h, y, c) if x % 2 == 1 else None
        if z == NZ - 1:
            return (x + 1, z, h, y, c) if x % 2 == 0 else None
        return None

    def x_two(x, z, h, y, c):
        if z == 0:
            return (0, z, h, y, c) if x == 2 else None
        if z == NZ - 1:
            return (3, z, h, y, c) if x == 1 else None
        return None

    got = moved(block, x_one)
    block = jnp.concatenate([jnp.where(low, block, got), jnp.where(low, got, block)])
    got = moved(after(block, *gate), x_two)
    block = jnp.concatenate([jnp.where(low, block, got), jnp.where(low, got, block)])
    return block.reshape(512, 1024)


def on_device(covariance, left_ops, right_ops, edge_rows, edge_cols):
    row, col = lax.axis_index("row"), lax.axis_index("col")
    x, z = row // NZ, row % NZ
    h, y, c = col // 8, col // 2 % NY, col % NC
    size = covariance.shape[0]

    def band_of(array, inner):
        return lax.dynamic_slice_in_dim(array, (c ^ inner) * size, size, axis=1)

    line = gather_line(right_ops)
    left = left_ops[0].transpose(0, 2, 1).reshape(96, size)
    pair = left_first(left, edge_cols.transpose(1, 2, 0), h)
    shares = rows_first(edge_rows, z, pair)
    lead = size // 4
    band = after(band_of(covariance, 0), pair, shares)
    outer = [rows_of(part) for part in (band[:, :lead], band[:, lead:])]
    high, low, side = left_second(pair, jnp.stack([h, y, c]), *outer[0])
    outside = rows_second(shares, z, *outer[0])
    line, band = lax.optimization_barrier(
        (line, band_of(covariance, 1), *outer[0], *outer[1], side, outside)
    )[:2]
    right_full = gather_ring(line)
    inner = [rows_of(band)]
    place = jnp.stack([c, row])
    half_outer = half_products(0, place, covariance, outside, high, low, outer)
    cross = moved(half_outer, outward)
    half_inner = half_products(1, place, covariance, outside, high, low, inner)
    sibling = moved(half_inner, core_swap)
    core = jnp.stack([c, jnp.where((col == 0) | (col == 15), 1, 0)])
    sums = first_products(core, half_outer, cross, side, right_full)
    return last_products(core, half_inner, sibling, right_full, *sums)


def split(array):
    high = array.astype(jnp.bfloat16)
    return high, (array - high.astype(jnp.float32)).astype(jnp.bfloat16)


def times(a, b):
    dims = (((1,), (1,)), ((), ()))
    total = lax.dot_general(a[0], b[1], dims, preferred_element_type=jnp.float32)
    total += lax.dot_general(a[1], b[0], dims, preferred_element_type=jnp.float32)
    return total + lax.dot_general(a[0], b[0], dims, preferred_element_type=jnp.float32)


def first_kernel(
    c_ref, near_ref, cross_ref, side_ref, r0_ref, r1_ref, r2_ref, outer_ref, inner_ref, held
):
    held[...] = cross_ref[...]

    @pl.when(c_ref[1] == 1)
    def _():
        held[...] = side_ref[...].T

    near, cross = split(near_ref[...]), split(held[...])
    inner_ref[...] = times(near, split(r2_ref[...]))
    outer_ref[...] = times(near, split(r1_ref[...])) + times(cross, split(r0_ref[...]))


def last_kernel(c_ref, near_ref, sibling_ref, r0_ref, r1_ref, r2_ref, outer_ref, inner_ref, out_ref):
    c, size = c_ref[0], near_ref.shape[0]
    near = split(near_ref[...])
    at = pl.multiple_of(c * size, 128)
    out_ref[:, pl.ds(at, size)] = outer_ref[...] + times(near, split(r2_ref[...]))
    at = pl.multiple_of((1 - c) * size, 128)
    total = inner_ref[...] + times(near, split(r1_ref[...]))
    out_ref[:, pl.ds(at, size)] = total + times(split(sibling_ref[...]), split(r0_ref[...]))


def whole(*shape):
    return pl.BlockSpec(shape, lambda i, c: (0,) * len(shape))


def block_at(place, size):
    return pl.BlockSpec((None, None, size, size), lambda i, c: (*place(c[0]), 0, 0))


PARAMS = pltpu.CompilerParams(vmem_limit_bytes=48 * 2**20)


def first_products(c, near, cross, side, right):
    size = near.shape[0]
    square = jax.ShapeDtypeStruct((size, size), jnp.float32)
    return pl.pallas_call(
        first_kernel,
        out_shape=(square, square),
        grid_spec=pltpu.PrefetchScalarGridSpec(
            num_scalar_prefetch=1,
            grid=(1,),
            in_specs=[whole(size, size)] * 3
            + [
                block_at(lambda c: (c, 2 * c), size),
                block_at(lambda c: (c, 1), size),
                block_at(lambda c: (1 - c, 2 * c), size),
            ],
            out_specs=(whole(size, size), whole(size, size)),
            scratch_shapes=[pltpu.VMEM((size, size), jnp.float32)],
        ),
        compiler_params=PARAMS,
        cost_estimate=pl.CostEstimate(
            flops=18 * size**3, bytes_accessed=28 * size**2, transcendentals=0
        ),
    )(c, near, cross, side, right, right, right)


def last_products(c, near, sibling, right, outer, inner):
    size = near.shape[0]
    return pl.pallas_call(
        last_kernel,
        out_shape=jax.ShapeDtypeStruct((size, 2 * size), jnp.float32),
        grid_spec=pltpu.PrefetchScalarGridSpec(
            num_scalar_prefetch=1,
            grid=(1,),
            in_specs=[whole(size, size)] * 2
            + [
                block_at(lambda c: (1 - c, 2 - 2 * c), size),
                block_at(lambda c: (1 - c, 1), size),
                block_at(lambda c: (c, 2 - 2 * c), size),
            ]
            + [whole(size, size)] * 2,
            out_specs=whole(size, 2 * size),
        ),
        compiler_params=PARAMS,
        cost_estimate=pl.CostEstimate(
            flops=18 * size**3, bytes_accessed=36 * size**2, transcendentals=0
        ),
    )(c, near, sibling, right, right, right, outer, inner)


def solution(mesh):
    return jax.shard_map(
        on_device,
        mesh=mesh,
        in_specs=(
            P("row", "col"),
            P("row", None, None, "col"),
            P("col", None, "row", None),
            P(None, "row", "col"),
            P("row", None, "col"),
        ),
        out_specs=P("row", "col"),
        check_vma=False,
    )
```

time: 349 us -> 290 us (0.83)
  the two profiles are of different devices: /device:TPU:59 before, /device:TPU:61 now
where the time goes in v2:
time: 290 us; the launch traced here: 289 us
  starting transfers between devices  115 us (40%)
  waiting for transfers between devices  112 us (39%)
  Pallas kernels  27.2 us (9%)
  between operations  13.9 us (5%)
  local copies, waits for them, and re-layouts  11.2 us (4%)
  other arithmetic  9.84 us (3%)
    ppermute x21, starting transfers between devices, moved(): return lax.ppermute(array, AXES, pairs)  115 us
    ppermute x21, waiting for transfers between devices, moved(): return lax.ppermute(array, AXES, pairs)  112 us
    pallas_call x2, Pallas kernels, half_products(): pl.pallas_call(half_kernel, out_shape=jax.ShapeDtypeStruct((size, size),...  11.5 us
    unnamed x40, local copies, waits for them, and re-layouts  9.03 us
    pallas_call x1, Pallas kernels, last_products(): pl.pallas_call(last_kernel, out_shape=jax.ShapeDtypeStruct((size, 2 * siz...  6.69 us
  transfers between devices with their start and end apart: 23, of which 9 were waited for; matrix products, arithmetic and copies ran while one was open for 4% of the time, Pallas kernels for 7%

profile of v2, /device:TPU:61, one launch (start us, length us, event | category | flops | bytes accessed | tf_op | source)
XLA Modules:
  0.0 289.1 jit_solution(2278460835922428987)
XLA Ops:
  6.5 0.9 slice_select_fusion
  7.4 8.8 %collective-permute-start = (f32[1,16,1024]{2,1,0:T(8,128)S(1)}, f32[1,16,1024]{2,1,0:T(8,128)S(1)}, u32[]{:S(2)}, u32[]{:S(2)}) collective-permute-start(f32[1,16,1024]{2,1,0:T(8,128)S(1)} %slice_select_fusion), channel_id=1, source_target_pairs={{0,64},{1,65},{2,66},{3,67},{4,68},{5,69},{6,70},{7,71},{8,72},{9,... | collective-permute-start | bytes 196616 | tf_op jit(solution)/shard_map/ppermute | solution.py:22
  16.3 0.9 select_bitcast_fusion.1
  17.2 1.0 fusion
  18.1 9.7 %collective-permute-start.1 = (f32[128,512]{1,0:T(8,128)S(1)}, f32[128,512]{1,0:T(8,128)S(1)}, u32[]{:S(2)}, u32[]{:S(2)}) collective-permute-start(f32[128,512]{1,0:T(8,128)S(1)} %get-tuple-element.44), channel_id=1, source_target_pairs={{0,8},{1,9},{2,10},{3,11},{4,12},{5,13},{6,14},{7,15},{8,0},{9,1},... | collective-permute-start | bytes 786440 | tf_op jit(solution)/shard_map/ppermute | solution.py:22
  27.9 0.9 broadcast_select_fusion.9
  28.8 21.7 %collective-permute-done.1 = f32[128,512]{1,0:T(8,128)S(1)} collective-permute-done((f32[128,512]{1,0:T(8,128)S(1)}, f32[128,512]{1,0:T(8,128)S(1)}, u32[]{:S(2)}, u32[]{:S(2)}) %collective-permute-start.1) | collective-permute-done | bytes 262176 | tf_op jit(solution)/shard_map/ppermute | solution.py:22
  50.6 1.4 collective-permute-start.2
  52.0 6.8 %collective-permute-done.2 = f32[2,1,1,16,1024]{4,3,2,1,0:T(8,128)S(1)} collective-permute-done((f32[2,1,1,16,1024]{4,3,2,1,0:T(8,128)S(1)}, f32[2,1,1,16,1024]{4,3,2,1,0:T(8,128)S(1)}, u32[]{:S(2)}, u32[]{:S(2)}) %collective-permute-start.2) | collective-permute-done | bytes 131104 | tf_op jit(solution)/shard_map/ppermute | solution.py:22
  58.8 1.3 collective-permute-start.3
  60.1 0.0 all-gather.3.cloned.1.call-update
  60.2 0.0 all-gather.5.cloned.1.call-start
  60.2 3.2 %collective-permute-done.3 = f32[2,2,1,16,1024]{4,3,2,1,0:T(8,128)S(1)} collective-permute-done((f32[2,2,1,16,1024]{4,3,2,1,0:T(8,128)S(1)}, f32[2,2,1,16,1024]{4,3,2,1,0:T(8,128)S(1)}, u32[]{:S(2)}, u32[]{:S(2)}) %collective-permute-start.3) | collective-permute-done | bytes 262176 | tf_op jit(solution)/shard_map/ppermute | solution.py:22
  63.4 0.1 broadcast_select_fusion.5
  63.5 1.5 collective-permute-start.4
  65.1 1.2 constant_dynamic-slice_fusion
  66.3 1.9 collective-permute-start.10
  68.2 4.1 %collective-permute-start.9 = (f32[2,128,512]{2,1,0:T(8,128)S(1)}, f32[2,128,512]{2,1,0:T(8,128)S(1)}, u32[]{:S(2)}, u32[]{:S(2)}) collective-permute-start(f32[2,128,512]{2,1,0:T(8,128)S(1)} %pad_maximum_fusion.2.refs_0_), channel_id=1, source_target_pairs={{0,4},{1,5},{2,6},{3,7},{4,0},{5,1},{6,2},{7,3},{8,12},{9,13},{10,... | collective-permute-start | bytes 1572872 | tf_op jit(solution)/shard_map/ppermute | solution.py:22
  72.3 1.9 collective-permute-start.8
  74.3 3.6 %collective-permute-start.6 = (f32[512,128]{1,0:T(8,128)S(1)}, f32[512,128]{1,0:T(8,128)S(1)}, u32[]{:S(2)}, u32[]{:S(2)}) collective-permute-start(f32[512,128]{1,0:T(8,128)S(1)} %slice.26), channel_id=1, source_target_pairs={{16,0},{17,1},{18,2},{19,3},{20,4},{21,5},{22,6},{23,7},{24,8},{25... | collective-permute-start | bytes 786440 | tf_op jit(solution)/shard_map/ppermute | solution.py:22
  77.9 1.9 collective-permute-start.5
  79.9 1.1 broadcast_select_fusion.3
  81.0 1.2 pad_maximum_fusion.1
  82.2 3.4 %collective-permute-done.6.refs_1_ = f32[512,128]{1,0:T(8,128)S(1)} collective-permute-done((f32[512,128]{1,0:T(8,128)S(1)}, f32[512,128]{1,0:T(8,128)S(1)}, u32[]{:S(2)}, u32[]{:S(2)}) %collective-permute-start.6) | collective-permute-done | bytes 262176 | tf_op jit(solution)/shard_map/ppermute | solution.py:22
  85.7 13.8 %collective-permute-done.5.refs_0_ = f32[512,128]{1,0:T(8,128)S(1)} collective-permute-done((f32[512,128]{1,0:T(8,128)S(1)}, f32[512,128]{1,0:T(8,128)S(1)}, u32[]{:S(2)}, u32[]{:S(2)}) %collective-permute-start.5) | collective-permute-done | bytes 262176 | tf_op jit(solution)/shard_map/ppermute | solution.py:22
  99.4 1.7 collective-permute-start.7
  101.1 0.0 collective-permute-done.8.refs_1_
  101.1 6.9 %collective-permute-start.11 = (f32[2,128,512]{2,1,0:T(8,128)S(1)}, f32[2,128,512]{2,1,0:T(8,128)S(1)}, u32[]{:S(2)}, u32[]{:S(2)}) collective-permute-start(f32[2,128,512]{2,1,0:T(8,128)S(1)} %pad_maximum_fusion.2.refs_0_), channel_id=1, source_target_pairs={{0,1},{1,0},{2,3},{3,2},{4,5},{5,4},{6,7},{7,6},{8,9},{9,8},{10,11... | collective-permute-start | bytes 1572872 | tf_op jit(solution)/shard_map/ppermute | solution.py:22
  108.0 1.9 collective-permute-start.12
  109.9 0.0 collective-permute-done.10.refs_3_
  109.9 2.4 collective-permute-start.13
  112.3 1.9 collective-permute-start.14
  114.3 1.0 slice.27
  115.2 0.8 copy-done.7
  116.1 7.3 %collective-permute-start.16 = (f32[512,384]{1,0:T(8,128)}, f32[512,384]{1,0:T(8,128)S(1)}, u32[]{:S(2)}, u32[]{:S(2)}) collective-permute-start(f32[512,384]{1,0:T(8,128)} %slice.27), channel_id=1, source_target_pairs={{16,0},{17,1},{18,2},{19,3},{20,4},{21,5},{22,6},{23,7},{24,8},{25... | collective-permute-start | bytes 2359304 | tf_op jit(solution)/shard_map/ppermute | solution.py:22
  123.4 0.0 collective-permute-done.12.refs_5_
  123.5 0.8 copy-done.9
  124.3 1.9 collective-permute-start.15
  126.2 0.1 pad_add_fusion.2.place_ref
  126.3 1.0 copy-done.6
  127.3 1.0 copy-done.8
  128.4 1.0 copy-done.10
  129.4 3.4 %shard_map.55 = (bf16[3,512,512]{2,1,0:T(8,128)(2,1)}, bf16[3,512,512]{2,1,0:T(8,128)(2,1)}, f32[512,512]{1,0:T(8,128)S(1)}) custom-call(s32[3]{0:T(128)S(1)} %pad_add_fusion.2.place_ref, f32[2,128,512]{2,1,0:T(8,128)S(1)} %pad_maximum_fusion.2.refs_0_, f32[2,128,512]{2,1,0:T(8,128)S(1)} %copy-done.6, f32[2,128,512]{2,1,0:T(8,128)S(1)} %collective-permute-done.9.refs_2_, ...), custom_call_target="tpu_custom_call" | custom-call | bytes 8388608 | tf_op jit(solution)/shard_map/pallas_call | solution.py:104
  132.9 1.9 broadcast_select_fusion.1
  134.8 1.6 pad_maximum_fusion
  136.3 8.0 %collective-permute-done.16.refs_3_ = f32[512,384]{1,0:T(8,128)S(1)} collective-permute-done((f32[512,384]{1,0:T(8,128)}, f32[512,384]{1,0:T(8,128)S(1)}, u32[]{:S(2)}, u32[]{:S(2)}) %collective-permute-start.16) | collective-permute-done | bytes 786464 | tf_op jit(solution)/shard_map/ppermute | solution.py:22
  144.4 19.8 %collective-permute-done.15.refs_2_ = f32[512,384]{1,0:T(8,128)S(1)} collective-permute-done((f32[512,384]{1,0:T(8,128)}, f32[512,384]{1,0:T(8,128)S(1)}, u32[]{:S(2)}, u32[]{:S(2)}) %collective-permute-start.15) | collective-permute-done | bytes 786464 | tf_op jit(solution)/shard_map/ppermute | solution.py:22
  164.2 0.0 all-gather.5.cloned.1.call-update
  164.2 4.7 %collective-permute-start.18 = (f32[512,512]{1,0:T(8,128)}, f32[512,512]{1,0:T(8,128)S(1)}, u32[]{:S(2)}, u32[]{:S(2)}) collective-permute-start(f32[512,512]{1,0:T(8,128)} %get-tuple-element.29), channel_id=1, source_target_pairs={{16,0},{17,1},{18,2},{19,3},{20,4},{21,5},{22,6},{23,7},{24,8},{25... | collective-permute-start | bytes 3145736 | tf_op jit(solution)/shard_map/ppermute | solution.py:22
  168.9 1.9 collective-permute-start.17
  170.9 0.1 pad_add_fusion.1.place_ref
  171.0 1.1 copy-done.4
  172.1 0.9 copy-done.12
  173.0 0.9 copy-done.14
  174.0 5.3 %shard_map.57.near_ref = f32[512,512]{1,0:T(8,128)S(1)} custom-call(s32[2]{0:T(128)S(1)} %pad_add_fusion.1.place_ref, f32[512,1024]{1,0:T(8,128)} %band_ref.3, f32[512,1024]{1,0:T(8,128)} %bitcast.26, bf16[3,512,512]{2,1,0:T(8,128)(2,1)S(1)} %copy-done, bf16[3,512,512]{2,1,0:T(8,128)(2,1)} %get-tuple-element.27.low_ref, f32[512,128]{1,0:T(8,128)S(1)} %copy-done.14, ...), custom_call_target="tpu_custom_call" | custom-call | flops 2415919104 | bytes 8388608 | tf_op jit(solution)/shard_map/pallas_call | solution.py:142
  179.3 13.6 %collective-permute-start.20 = (f32[512,512]{1,0:T(8,128)S(1)}, f32[512,512]{1,0:T(8,128)}, u32[]{:S(2)}, u32[]{:S(2)}) collective-permute-start(f32[512,512]{1,0:T(8,128)S(1)} %shard_map.57.near_ref), channel_id=1, source_target_pairs={{1,2},{2,1},{3,4},{4,3},{5,6},{6,5},{7,8},{8,7},{9,10},{10,9},{11,... | collective-permute-start | bytes 3145736 | tf_op jit(solution)/shard_map/ppermute | solution.py:22
  192.8 24.2 %collective-permute-done.17.refs_0_ = f32[512,512]{1,0:T(8,128)S(1)} collective-permute-done((f32[512,512]{1,0:T(8,128)}, f32[512,512]{1,0:T(8,128)S(1)}, u32[]{:S(2)}, u32[]{:S(2)}) %collective-permute-start.17) | collective-permute-done | bytes 1048608 | tf_op jit(solution)/shard_map/ppermute | solution.py:22
  217.1 6.3 %shard_map.56.near_ref = f32[512,512]{1,0:T(8,128)} custom-call(s32[2]{0:T(128)S(1)} %pad_add_fusion.1.place_ref, f32[512,1024]{1,0:T(8,128)} %band_ref.3, f32[512,1024]{1,0:T(8,128)} %bitcast.27, bf16[3,512,512]{2,1,0:T(8,128)(2,1)S(1)} %copy-done, bf16[3,512,512]{2,1,0:T(8,128)(2,1)} %get-tuple-element.27.low_ref, ...), custom_call_target="tpu_custom_call" | custom-call | flops 2415919104 | bytes 8388608 | tf_op jit(solution)/shard_map/pallas_call | solution.py:142
  223.3 34.4 %collective-permute-start.19 = (f32[512,512]{1,0:T(8,128)}, f32[512,512]{1,0:T(8,128)S(1)}, u32[]{:S(2)}, u32[]{:S(2)}) collective-permute-start(f32[512,512]{1,0:T(8,128)} %shard_map.56.near_ref), channel_id=1, source_target_pairs={{0,1},{1,0},{2,3},{3,2},{4,5},{5,4},{6,7},{7,6},{8,9},{9,8},{10,11... | collective-permute-start | bytes 3145736 | tf_op jit(solution)/shard_map/ppermute | solution.py:22
  257.7 0.1 pad_add_fusion.c_ref
  257.8 11.0 %collective-permute-done.20.cross_ref = f32[512,512]{1,0:T(8,128)} collective-permute-done((f32[512,512]{1,0:T(8,128)S(1)}, f32[512,512]{1,0:T(8,128)}, u32[]{:S(2)}, u32[]{:S(2)}) %collective-permute-start.20) | collective-permute-done | bytes 1048608 | tf_op jit(solution)/shard_map/ppermute | solution.py:22
  268.8 1.2 copy-done.2
  270.0 5.6 %shard_map.58 = (f32[512,512]{1,0:T(8,128)S(1)}, f32[512,512]{1,0:T(8,128)S(1)}) custom-call(s32[2]{0:T(128)S(1)} %pad_add_fusion.c_ref, f32[512,512]{1,0:T(8,128)S(1)} %shard_map.57.near_ref, f32[512,512]{1,0:T(8,128)} %collective-permute-done.20.cross_ref, f32[512,512]{1,0:T(8,128)S(1)} %copy-done.2, ...), custom_call_target="tpu_custom_call" | custom-call | flops 2415919104 | bytes 7340032 | tf_op jit(solution)/shard_map/pallas_call | solution.py:308
  275.6 6.7 %shard_map.59 = f32[512,1024]{1,0:T(8,128)} custom-call(s32[2]{0:T(128)S(1)} %pad_add_fusion.c_ref, f32[512,512]{1,0:T(8,128)} %shard_map.56.near_ref, f32[512,512]{1,0:T(8,128)S(1)} %collective-permute-done.19.sibling_ref, f32[2,3,512,512]{3,2,1,0:T(8,128)} %all-gather.5.cloned.1.call-done.r0_ref.r1_ref.r2_ref, ...), custom_call_target="tpu_custom_call" | custom-call | flops 2415919104 | bytes 9437184 | tf_op jit(solution)/shard_map/pallas_call | solution.py:332
  (49 shorter events, 0.2 us)
Async XLA Ops:
  6.5 157.7 %all-gather.3.cloned.1.call-start = ((), (), s32[]{:S(2)}) async-start(), calls=%async_computation | async-start | bytes 1769472 | tf_op jit(solution)/shard_map/all_gather | solution.py:162
  7.4 20.5 %collective-permute-start = (f32[1,16,1024]{2,1,0:T(8,128)S(1)}, f32[1,16,1024]{2,1,0:T(8,128)S(1)}, u32[]{:S(2)}, u32[]{:S(2)}) collective-permute-start(f32[1,16,1024]{2,1,0:T(8,128)S(1)} %slice_select_fusion), channel_id=1, source_target_pairs={{0,64},{1,65},{2,66},{3,67},{4,68},{5,69},{6,70},{7,71},{8,72},{9,... | collective-permute-start | bytes 196616 | tf_op jit(solution)/shard_map/ppermute | solution.py:22
  18.1 32.4 %collective-permute-start.1 = (f32[128,512]{1,0:T(8,128)S(1)}, f32[128,512]{1,0:T(8,128)S(1)}, u32[]{:S(2)}, u32[]{:S(2)}) collective-permute-start(f32[128,512]{1,0:T(8,128)S(1)} %get-tuple-element.44), channel_id=1, source_target_pairs={{0,8},{1,9},{2,10},{3,11},{4,12},{5,13},{6,14},{7,15},{8,0},{9,1},... | collective-permute-start | bytes 786440 | tf_op jit(solution)/shard_map/ppermute | solution.py:22
  50.5 14.5 %copy-start.15 = (f32[512,1024]{1,0:T(8,128)S(1)}, f32[512,1024]{1,0:T(8,128)}, u32[]{:S(2)}) copy-start(f32[512,1024]{1,0:T(8,128)} %band_ref.3) | copy-start | bytes 6291460
  50.6 8.2 %collective-permute-start.2 = (f32[2,1,1,16,1024]{4,3,2,1,0:T(8,128)S(1)}, f32[2,1,1,16,1024]{4,3,2,1,0:T(8,128)S(1)}, u32[]{:S(2)}, u32[]{:S(2)}) collective-permute-start(f32[2,1,1,16,1024]{4,3,2,1,0:T(8,128)S(1)} %maximum_bitcast_fusion), channel_id=1, source_target_pairs={{32,0},{33,1},{34,2},{35,3},{36,4},{37,5},{38,6},{39,7},{40,8},{41... | collective-permute-start | bytes 393224 | tf_op jit(solution)/shard_map/ppermute | solution.py:22
  58.8 4.6 %collective-permute-start.3 = (f32[2,2,1,16,1024]{4,3,2,1,0:T(8,128)S(1)}, f32[2,2,1,16,1024]{4,3,2,1,0:T(8,128)S(1)}, u32[]{:S(2)}, u32[]{:S(2)}) collective-permute-start(f32[2,2,1,16,1024]{4,3,2,1,0:T(8,128)S(1)} %pad_maximum_fusion.6), channel_id=1, source_target_pairs={{16,0},{17,1},{18,2},{19,3},{20,4},{21,5},{22,6},{23,7},{24,8},{25... | collective-permute-start | bytes 786440 | tf_op jit(solution)/shard_map/ppermute | solution.py:22
  60.2 208.6 %all-gather.5.cloned.1.call-start = ((), (), s32[]{:S(2)}) async-start(), calls=%async_computation.1 | async-start | bytes 7864320 | tf_op jit(solution)/shard_map/all_gather | solution.py:167
  63.5 14.4 %collective-permute-start.4 = (f32[1,128,1024]{2,1,0:T(8,128)S(1)}, f32[1,128,1024]{2,1,0:T(8,128)}, u32[]{:S(2)}, u32[]{:S(2)}) collective-permute-start(f32[1,128,1024]{2,1,0:T(8,128)S(1)} %bitcast.28), channel_id=1, source_target_pairs={{112,240},{113,241},{114,242},{115,243},{116,244},{117,245},{118,2... | collective-permute-start | bytes 1572872 | tf_op jit(solution)/shard_map/ppermute | solution.py:22
  66.3 43.7 %collective-permute-start.10 = (f32[2,128,512]{2,1,0:T(8,128)S(1)}, f32[2,128,512]{2,1,0:T(8,128)S(1)}, u32[]{:S(2)}, u32[]{:S(2)}) collective-permute-start(f32[2,128,512]{2,1,0:T(8,128)S(1)} %pad_maximum_fusion.2.refs_0_), channel_id=1, source_target_pairs={{0,2},{1,3},{2,4},{3,5},{4,6},{5,7},{6,0},{7,1},{8,10},{9,11},{10,... | collective-permute-start | bytes 1572872 | tf_op jit(solution)/shard_map/ppermute | solution.py:22
  68.2 41.8 %collective-permute-start.9 = (f32[2,128,512]{2,1,0:T(8,128)S(1)}, f32[2,128,512]{2,1,0:T(8,128)S(1)}, u32[]{:S(2)}, u32[]{:S(2)}) collective-permute-start(f32[2,128,512]{2,1,0:T(8,128)S(1)} %pad_maximum_fusion.2.refs_0_), channel_id=1, source_target_pairs={{0,4},{1,5},{2,6},{3,7},{4,0},{5,1},{6,2},{7,3},{8,12},{9,13},{10,... | collective-permute-start | bytes 1572872 | tf_op jit(solution)/shard_map/ppermute | solution.py:22
  72.3 28.7 %collective-permute-start.8 = (f32[2,128,512]{2,1,0:T(8,128)S(1)}, f32[2,128,512]{2,1,0:T(8,128)S(1)}, u32[]{:S(2)}, u32[]{:S(2)}) collective-permute-start(f32[2,128,512]{2,1,0:T(8,128)S(1)} %pad_maximum_fusion.2.refs_0_), channel_id=1, source_target_pairs={{0,6},{1,7},{2,0},{3,1},{4,2},{5,3},{6,4},{7,5},{8,14},{9,15},{10,... | collective-permute-start | bytes 1572872 | tf_op jit(solution)/shard_map/ppermute | solution.py:22
  74.3 11.3 %collective-permute-start.6 = (f32[512,128]{1,0:T(8,128)S(1)}, f32[512,128]{1,0:T(8,128)S(1)}, u32[]{:S(2)}, u32[]{:S(2)}) collective-permute-start(f32[512,128]{1,0:T(8,128)S(1)} %slice.26), channel_id=1, source_target_pairs={{16,0},{17,1},{18,2},{19,3},{20,4},{21,5},{22,6},{23,7},{24,8},{25... | collective-permute-start | bytes 786440 | tf_op jit(solution)/shard_map/ppermute | solution.py:22
  77.9 21.5 %collective-permute-start.5 = (f32[512,128]{1,0:T(8,128)S(1)}, f32[512,128]{1,0:T(8,128)S(1)}, u32[]{:S(2)}, u32[]{:S(2)}) collective-permute-start(f32[512,128]{1,0:T(8,128)S(1)} %slice.26), channel_id=1, source_target_pairs={{0,16},{1,17},{2,18},{3,19},{4,20},{5,21},{6,22},{7,23},{8,24},{9,... | collective-permute-start | bytes 786440 | tf_op jit(solution)/shard_map/ppermute | solution.py:22
  81.0 42.4 %copy-start.16 = (f32[1,128,1024]{2,1,0:T(8,128)}, f32[1,128,1024]{2,1,0:T(8,128)S(1)}, u32[]{:S(2)}) copy-start(f32[1,128,1024]{2,1,0:T(8,128)S(1)} %get-tuple-element.37) | copy-start | bytes 1572868
  81.0 42.4 %copy-start.18 = (f32[1,128,1024]{2,1,0:T(8,128)}, f32[1,128,1024]{2,1,0:T(8,128)S(1)}, u32[]{:S(2)}) copy-start(f32[1,128,1024]{2,1,0:T(8,128)S(1)} %get-tuple-element.38) | copy-start | bytes 1572868
  85.7 37.8 %copy-start.11 = (f32[512,128]{1,0:T(8,128)}, f32[512,128]{1,0:T(8,128)S(1)}, u32[]{:S(2)}) copy-start(f32[512,128]{1,0:T(8,128)S(1)} %collective-permute-done.6.refs_1_) | copy-start | bytes 786436
  99.4 24.1 %copy-start.13 = (f32[512,128]{1,0:T(8,128)}, f32[512,128]{1,0:T(8,128)S(1)}, u32[]{:S(2)}) copy-start(f32[512,128]{1,0:T(8,128)S(1)} %collective-permute-done.5.refs_0_) | copy-start | bytes 786436
  99.4 33.4 %collective-permute-start.7 = (f32[2,128,1024]{2,1,0:T(8,128)}, f32[2,128,1024]{2,1,0:T(8,128)}, u32[]{:S(2)}, u32[]{:S(2)}) collective-permute-start(f32[2,128,1024]{2,1,0:T(8,128)} %pad_maximum_fusion.1), channel_id=1, source_target_pairs={{240,496},{241,497},{242,498},{243,499},{244,500},{245,501},{246,5... | collective-permute-start | bytes 3145736 | tf_op jit(solution)/shard_map/ppermute | solution.py:22
  101.1 22.4 %copy-start.5 = (f32[2,128,512]{2,1,0:T(8,128)}, f32[2,128,512]{2,1,0:T(8,128)S(1)}, u32[]{:S(2)}) copy-start(f32[2,128,512]{2,1,0:T(8,128)S(1)} %collective-permute-done.8.refs_1_) | copy-start | bytes 1572868
  101.1 14.2 %collective-permute-start.11 = (f32[2,128,512]{2,1,0:T(8,128)S(1)}, f32[2,128,512]{2,1,0:T(8,128)S(1)}, u32[]{:S(2)}, u32[]{:S(2)}) collective-permute-start(f32[2,128,512]{2,1,0:T(8,128)S(1)} %pad_maximum_fusion.2.refs_0_), channel_id=1, source_target_pairs={{0,1},{1,0},{2,3},{3,2},{4,5},{5,4},{6,7},{7,6},{8,9},{9,8},{10,11... | collective-permute-start | bytes 1572872 | tf_op jit(solution)/shard_map/ppermute | solution.py:22
  108.0 15.5 %collective-permute-start.12 = (f32[2,128,512]{2,1,0:T(8,128)S(1)}, f32[2,128,512]{2,1,0:T(8,128)S(1)}, u32[]{:S(2)}, u32[]{:S(2)}) collective-permute-start(f32[2,128,512]{2,1,0:T(8,128)S(1)} %collective-permute-done.8.refs_1_), channel_id=1, source_target_pairs={{0,1},{1,0},{2,3},{3,2},{4,5},{5,4},{6,7},{7,6},{8,9},{9,8},{10,11... | collective-permute-start | bytes 1572872 | tf_op jit(solution)/shard_map/ppermute | solution.py:22
  109.9 16.4 %collective-permute-start.13 = (f32[2,128,512]{2,1,0:T(8,128)S(1)}, f32[2,128,512]{2,1,0:T(8,128)}, u32[]{:S(2)}, u32[]{:S(2)}) collective-permute-start(f32[2,128,512]{2,1,0:T(8,128)S(1)} %collective-permute-done.9.refs_2_), channel_id=1, source_target_pairs={{0,1},{1,0},{2,3},{3,2},{4,5},{5,4},{6,7},{7,6},{8,9},{9,8},{10,11... | collective-permute-start | bytes 1572872 | tf_op jit(solution)/shard_map/ppermute | solution.py:22
  112.3 14.0 %collective-permute-start.14 = (f32[2,128,512]{2,1,0:T(8,128)S(1)}, f32[2,128,512]{2,1,0:T(8,128)}, u32[]{:S(2)}, u32[]{:S(2)}) collective-permute-start(f32[2,128,512]{2,1,0:T(8,128)S(1)} %collective-permute-done.10.refs_3_), channel_id=1, source_target_pairs={{0,1},{1,0},{2,3},{3,2},{4,5},{5,4},{6,7},{7,6},{8,9},{9,8},{10,11... | collective-permute-start | bytes 1572872 | tf_op jit(solution)/shard_map/ppermute | solution.py:22
  115.2 0.8 copy-start.7
  116.1 28.3 %collective-permute-start.16 = (f32[512,384]{1,0:T(8,128)}, f32[512,384]{1,0:T(8,128)S(1)}, u32[]{:S(2)}, u32[]{:S(2)}) collective-permute-start(f32[512,384]{1,0:T(8,128)} %slice.27), channel_id=1, source_target_pairs={{16,0},{17,1},{18,2},{19,3},{20,4},{21,5},{22,6},{23,7},{24,8},{25... | collective-permute-start | bytes 2359304 | tf_op jit(solution)/shard_map/ppermute | solution.py:22
  123.5 0.8 copy-start.9
  124.3 39.9 %collective-permute-start.15 = (f32[512,384]{1,0:T(8,128)}, f32[512,384]{1,0:T(8,128)S(1)}, u32[]{:S(2)}, u32[]{:S(2)}) collective-permute-start(f32[512,384]{1,0:T(8,128)} %slice.27), channel_id=1, source_target_pairs={{0,16},{1,17},{2,18},{3,19},{4,20},{5,21},{6,22},{7,23},{8,24},{9,... | collective-permute-start | bytes 2359304 | tf_op jit(solution)/shard_map/ppermute | solution.py:22
  126.3 1.0 copy-start.6
  127.3 1.0 copy-start.8
  128.4 1.0 copy-start.10
  129.4 3.4 %copy-start.17 = (f32[1,128,1024]{2,1,0:T(8,128)S(1)}, f32[1,128,1024]{2,1,0:T(8,128)}, u32[]{:S(2)}) copy-start(f32[1,128,1024]{2,1,0:T(8,128)} %copy-done.16) | copy-start | bytes 1572868
  129.4 3.4 %copy-start.19 = (f32[1,128,1024]{2,1,0:T(8,128)S(1)}, f32[1,128,1024]{2,1,0:T(8,128)}, u32[]{:S(2)}) copy-start(f32[1,128,1024]{2,1,0:T(8,128)} %copy-done.18) | copy-start | bytes 1572868
  132.8 1.9 copy-start.1
  134.8 36.2 %copy-start = (bf16[3,512,512]{2,1,0:T(8,128)(2,1)S(1)}, bf16[3,512,512]{2,1,0:T(8,128)(2,1)}, u32[]{:S(2)}) copy-start(bf16[3,512,512]{2,1,0:T(8,128)(2,1)} %get-tuple-element.26.high_ref) | copy-start | bytes 4718596
  164.2 6.8 %copy-start.3 = (f32[512,384]{1,0:T(8,128)}, f32[512,384]{1,0:T(8,128)S(1)}, u32[]{:S(2)}) copy-start(f32[512,384]{1,0:T(8,128)S(1)} %collective-permute-done.15.refs_2_) | copy-start | bytes 2359300
  164.2 28.6 %collective-permute-start.18 = (f32[512,512]{1,0:T(8,128)}, f32[512,512]{1,0:T(8,128)S(1)}, u32[]{:S(2)}, u32[]{:S(2)}) collective-permute-start(f32[512,512]{1,0:T(8,128)} %get-tuple-element.29), channel_id=1, source_target_pairs={{16,0},{17,1},{18,2},{19,3},{20,4},{21,5},{22,6},{23,7},{24,8},{25... | collective-permute-start | bytes 3145736 | tf_op jit(solution)/shard_map/ppermute | solution.py:22
  168.9 48.1 %collective-permute-start.17 = (f32[512,512]{1,0:T(8,128)}, f32[512,512]{1,0:T(8,128)S(1)}, u32[]{:S(2)}, u32[]{:S(2)}) collective-permute-start(f32[512,512]{1,0:T(8,128)} %get-tuple-element.29), channel_id=1, source_target_pairs={{0,16},{1,17},{2,18},{3,19},{4,20},{5,21},{6,22},{7,23},{8,24},{9,... | collective-permute-start | bytes 3145736 | tf_op jit(solution)/shard_map/ppermute | solution.py:22
  171.0 1.1 copy-start.4
  172.1 0.9 copy-start.12
  173.0 0.9 copy-start.14
  179.3 89.5 %collective-permute-start.20 = (f32[512,512]{1,0:T(8,128)S(1)}, f32[512,512]{1,0:T(8,128)}, u32[]{:S(2)}, u32[]{:S(2)}) collective-permute-start(f32[512,512]{1,0:T(8,128)S(1)} %shard_map.57.near_ref), channel_id=1, source_target_pairs={{1,2},{2,1},{3,4},{4,3},{5,6},{6,5},{7,8},{8,7},{9,10},{10,9},{11,... | collective-permute-start | bytes 3145736 | tf_op jit(solution)/shard_map/ppermute | solution.py:22
  223.3 52.3 %collective-permute-start.19 = (f32[512,512]{1,0:T(8,128)}, f32[512,512]{1,0:T(8,128)S(1)}, u32[]{:S(2)}, u32[]{:S(2)}) collective-permute-start(f32[512,512]{1,0:T(8,128)} %shard_map.56.near_ref), channel_id=1, source_target_pairs={{0,1},{1,0},{2,3},{3,2},{4,5},{5,4},{6,7},{7,6},{8,9},{9,8},{10,11... | collective-permute-start | bytes 3145736 | tf_op jit(solution)/shard_map/ppermute | solution.py:22
  268.8 1.2 copy-start.2
Sparse Core Ops, SparseCore 0:
  60.3 68.8 all-gather.2
  164.3 73.0 all-gather.4

commit v3 on v2

--- a/solution.py
+++ b/solution.py
@@ -76,85 +76,101 @@
     return jnp.stack([own, other])
 
 
-def left_second(pair, place, *gate):
-    pieces = [pair, moved(pair, y_step(-1)), moved(pair, y_step(2)), moved(pair, y_step(1))]
-    mates = [moved(after(piece, *gate), core_swap) for piece in pieces]
-    return assembled(place, pieces + mates)
-
-
-def assemble_kernel(place_ref, *refs):
-    pieces, (high_ref, low_ref, side_ref) = refs[:8], refs[8:]
+def along_y(pair):
+    return [pair] + [moved(pair, y_step(d)) for d in (-1, 2, 1)]
+
+
+def assemble_kernel(place_ref, own_ref, mate_ref, high_ref, low_ref, side_ref):
     h, y, c = place_ref[0], place_ref[1], place_ref[2]
-    for k, piece in enumerate(pieces):
-        core = c if k < 4 else 1 - c
-        line = lax.rem(y + k % 4, NY)
-        for far in range(2):
-            side = h if far == 0 else 1 - h
-            at = pl.multiple_of(((side * NY + line) * NC + core) * 32, 32)
-            for m in range(3):
-                high, low = split(piece[far, pl.ds(m * 32, 32), :])
-                high_ref[m, pl.ds(at, 32), :] = high
-                low_ref[m, pl.ds(at, 32), :] = low
-            side_ref[pl.ds(at, 32), :] = piece[far, pl.ds(96, 32), :]
-
-
-def assembled(place, pieces):
-    size = pieces[0].shape[2]
+    for ref, core in ((own_ref, c), (mate_ref, 1 - c)):
+        for d in range(NY):
+            line = lax.rem(y + d, NY)
+            for far in range(2):
+                side = h if far == 0 else 1 - h
+                at = pl.multiple_of(((side * NY + line) * NC + core) * 32, 32)
+                for m in range(3):
+                    high, low = split(ref[d, far, pl.ds(m * 32, 32), :])
+                    high_ref[m, pl.ds(at, 32), :] = high
+                    low_ref[m, pl.ds(at, 32), :] = low
+                side_ref[pl.ds(at, 32), :] = ref[d, far, pl.ds(96, 32), :]
+
+
+def assembled(place, own, mate):
+    size = own.shape[3]
     half = jax.ShapeDtypeStruct((3, size, size), jnp.bfloat16)
     return pl.pallas_call(
         assemble_kernel,
         out_shape=(half, half, jax.ShapeDtypeStruct((size, size), jnp.float32)),
         in_specs=[pl.BlockSpec(memory_space=pltpu.SMEM)]
-        + [pl.BlockSpec(memory_space=pltpu.VMEM)] * 8,
+        + [pl.BlockSpec(memory_space=pltpu.VMEM)] * 2,
         out_specs=(pl.BlockSpec(memory_space=pltpu.VMEM),) * 3,
         compiler_params=PARAMS,
         cost_estimate=pl.CostEstimate(
             flops=0, bytes_accessed=32 * size**2, transcendentals=0
         ),
-    )(place, *pieces)
-
-
-def half_kernel(place_ref, band_ref, outside_ref, high_ref, low_ref, *refs):
-    (*parts, out_ref) = refs
-    upper, lower = (
-        jnp.concatenate([ref[...] for ref in parts[k::2]], axis=1) for k in range(2)
-    )
-    outside = outside_ref[...]
-    blocks = (
-        jnp.where(place_ref[1] == 0, outside, upper),
-        band_ref[...],
-        jnp.where(place_ref[1] == NX * NZ - 1, outside, lower),
-    )
+    )(place, own, mate)
+
+
+def half_kernel(place_ref, band_ref, high_ref, low_ref, *refs):
+    edges, parts, (out_ref, top, bottom) = refs[:NX], refs[NX:-3], refs[-3:]
+    at = 0
+    for upper_ref, lower_ref in zip(parts[::2], parts[1::2]):
+        width = upper_ref.shape[1]
+        top[:, at : at + width] = upper_ref[...]
+        bottom[:, at : at + width] = lower_ref[...]
+        at += width
+
+    def fill(ref, mirror):
+        for k, edge in enumerate(edges):
+            for d in range(4):
+                for far in range(2):
+                    x, z = (NX - 1 - k, 3 - d) if mirror else (k, d)
+                    at = (x * NZ + far * 4 + z) * 16
+                    ref[at : at + 16, :] = edge[(d * 2 + far) * 16 : (d * 2 + far + 1) * 16, :]
+
+    @pl.when(place_ref[1] == 0)
+    def _():
+        fill(top, False)
+
+    @pl.when(place_ref[1] == NX * NZ - 1)
+    def _():
+        fill(bottom, True)
+
     dims = (((0,), (0,)), ((), ()))
     total = None
-    for m in (1, 0, 2):
-        high, low = split(blocks[m])
+    for m, ref in ((1, band_ref), (0, top), (2, bottom)):
+        high, low = split(ref[...])
         for left, block in ((high_ref, low), (low_ref, high), (high_ref, high)):
             part = lax.dot_general(left[m], block, dims, preferred_element_type=jnp.float32)
             total = part if total is None else total + part
     out_ref[...] = total
 
 
-def half_products(inner, place, covariance, outside, high, low, parts):
+def half_products(inner, place, covariance, high, low, edges, parts):
+    size = covariance.shape[0]
     parts = [piece for part in parts for piece in part]
-    size = covariance.shape[0]
-    column = pl.BlockSpec((size, size), lambda i, place: (0, place[0] ^ inner))
+
+    def column(rows):
+        return pl.BlockSpec((rows, size), lambda i, place: (0, place[0] ^ inner))
+
     return pl.pallas_call(
         half_kernel,
         out_shape=jax.ShapeDtypeStruct((size, size), jnp.float32),
         grid_spec=pltpu.PrefetchScalarGridSpec(
             num_scalar_prefetch=1,
             grid=(1,),
-            in_specs=[column, column]
+            in_specs=[column(size)]
             + [whole(3, size, size)] * 2
+            + [column(size // NX)] * NX
             + [whole(*piece.shape) for piece in parts],
             out_specs=whole(size, size),
+            scratch_shapes=[pltpu.VMEM((size, size), jnp.float32)] * 2,
         ),
         compiler_params=PARAMS,
         cost_estimate=pl.CostEstimate(
             flops=18 * size**3, bytes_accessed=32 * size**2, transcendentals=0
         ),
-    )(place, covariance, outside, high, low, *parts)
+    )(place, covariance, high, low, *edges, *parts)
 
 
 def gather_line(right):
@@ -171,55 +187,43 @@
     return col_step(1 if c == 1 else -1)(x, z, h, y, c)
 
 
-def toward(bit):
+def toward(distance):
     def target(x, z, h, y, c):
-        if bit == 4:
-            return (x, z ^ 4, h, y, c)
-        low = z < 4
-        rest = z if low else NZ - 1 - z
-        if bit <= rest < 2 * bit:
-            return (x, z - bit if low else z + bit, h, y, c)
+        if z == distance:
+            return (x, 0, h, y, c)
+        if NZ - 1 - z == distance:
+            return (x, NZ - 1, h, y, c)
         return None
 
     return target
 
 
-def rows_first(edge, z, gate):
+def across(distance):
+    def target(x, z, h, y, c):
+        if z == 0 and x == distance:
+            return (0, z, h, y, c)
+        if z == NZ - 1 and NX - 1 - x == distance:
+            return (NX - 1, z, h, y, c)
+        return None
+
+    return target
+
+
+def rows_first(edge, z):
     low = z < 4
-    keep = jnp.where(low, edge[0], edge[1])[None]
-    send = jnp.where(low, edge[1], edge[0])[None]
-    got = moved(send, toward(4))
-    block = jnp.concatenate([jnp.where(low, keep, got), jnp.where(low, got, keep)])
-    block = block.reshape(2, 1, 1, 16, 1024)
-    got = moved(after(block, gate), toward(2))
-    block = jnp.concatenate([jnp.where(low, block, got), jnp.where(low, got, block)], axis=1)
-    got = moved(block, toward(1))
-    block = jnp.concatenate([jnp.where(low, block, got), jnp.where(low, got, block)], axis=2)
-    return block.reshape(1, 128, 1024)
-
-
-def rows_second(block, z, *gate):
-    low = z < 4
-
-    def x_one(x, z, h, y, c):
-        if z == 0:
-            return (x - 1, z, h, y, c) if x % 2 == 1 else None
-        if z == NZ - 1:
-            return (x + 1, z, h, y, c) if x % 2 == 0 else None
-        return None
-
-    def x_two(x, z, h, y, c):
-        if z == 0:
-            return (0, z, h, y, c) if x == 2 else None
-        if z == NZ - 1:
-            return (3, z, h, y, c) if x == 1 else None
-        return None
-
-    got = moved(block, x_one)
-    block = jnp.concatenate([jnp.where(low, block, got), jnp.where(low, got, block)])
-    got = moved(after(block, *gate), x_two)
-    block = jnp.concatenate([jnp.where(low, block, got), jnp.where(low, got, block)])
-    return block.reshape(512, 1024)
+    keep = jnp.where(low, edge[0], edge[1])
+    got = moved(jnp.where(low, edge[1], edge[0]), z_swap(4))
+    return jnp.concatenate([jnp.where(low, keep, got), jnp.where(low, got, keep)])
+
+
+def rows_second(share, gate):
+    sent = after(share, *gate)
+    return jnp.concatenate([share] + [moved(sent, toward(d)) for d in (1, 2, 3)])
+
+
+def rows_third(share, gate):
+    sent = after(share, *gate)
+    return [share] + [moved(sent, across(d)) for d in (1, 2, 3)]
 
 
 def on_device(covariance, left_ops, right_ops, edge_rows, edge_cols):
@@ -234,21 +238,23 @@
     line = gather_line(right_ops)
     left = left_ops[0].transpose(0, 2, 1).reshape(96, size)
     pair = left_first(left, edge_cols.transpose(1, 2, 0), h)
-    shares = rows_first(edge_rows, z, pair)
-    lead = size // 4
-    band = after(band_of(covariance, 0), pair, shares)
-    outer = [rows_of(part) for part in (band[:, :lead], band[:, lead:])]
-    high, low, side = left_second(pair, jnp.stack([h, y, c]), *outer[0])
-    outside = rows_second(shares, z, *outer[0])
-    line, band = lax.optimization_barrier(
-        (line, band_of(covariance, 1), *outer[0], *outer[1], side, outside)
-    )[:2]
-    right_full = gather_ring(line)
+    share = rows_first(edge_rows, z)
+    band = band_of(covariance, 0)
+    outer = [rows_of(band[:, : size // 2])]
+    pieces = along_y(after(pair, share, *outer[0]))
+    outer.append(rows_of(after(band[:, size // 2 :], share, pair)))
+    share = rows_second(share, outer[1])
+    right_full = gather_ring(after(line, *outer[1], *pieces))
+    pieces = jnp.stack(pieces)
+    mates = moved(after(pieces, *outer[1]), core_swap)
+    band = after(band_of(covariance, 1), *outer[1])
     inner = [rows_of(band)]
+    edges = rows_third(share, outer[0])
+    high, low, side = assembled(jnp.stack([h, y, c]), pieces, mates)
     place = jnp.stack([c, row])
-    half_outer = half_products(0, place, covariance, outside, high, low, outer)
+    half_outer = half_products(0, place, covariance, high, low, edges, outer)
     cross = moved(half_outer, outward)
-    half_inner = half_products(1, place, covariance, outside, high, low, inner)
+    half_inner = half_products(1, place, covariance, high, low, edges, inner)
     sibling = moved(half_inner, core_swap)
     core = jnp.stack([c, jnp.where((col == 0) | (col == 15), 1, 0)])
     sums = first_products(core, half_outer, cross, side, right_full)

time: 290 us -> 264 us (0.910)
  starting transfers between devices: 115 us -> 79.6 us
  waiting for transfers between devices: 112 us -> 126 us
  other arithmetic: 9.84 us -> 3.28 us
    ppermute x21 -> x20, starting transfers between devices: 115 us -> 79.5 us  [moved(): return lax.ppermute(array, AXES, pairs)]
    ppermute x21 -> x20, waiting for transfers between devices: 112 us -> 126 us  [moved(): return lax.ppermute(array, AXES, pairs)]
    select_n x6 -> x1, other arithmetic: 4.85 us -> 0.01 us  [rows_first(): got = moved(jnp.where(low, edge[1], edge[0]), z_swap(4))]
    another operation x1 -> x2, other arithmetic: 0.08 us -> 2.98 us  [the longest x1 2.9 us: on_device(): pieces = jnp.stack(pieces)]
    unnamed x40 -> x44, local copies, waits for them, and re-layouts: 9.03 us -> 8.39 us
  transfers between devices with their start and end apart: 23 -> 22, of which waited for: 9 -> 7; matrix products, arithmetic and copies ran while one was open for 4% -> 3% of each run, Pallas kernels for 7% -> 8%
where the time goes in v3:
time: 264 us; the launch traced here: 263 us
  waiting for transfers between devices  126 us (48%)
  starting transfers between devices  79.6 us (30%)
  Pallas kernels  26.5 us (10%)
  between operations  14 us (5%)
  local copies, waits for them, and re-layouts  13.1 us (5%)
  other arithmetic  3.28 us (1%)
    ppermute x20, waiting for transfers between devices, moved(): return lax.ppermute(array, AXES, pairs)  126 us
    ppermute x20, starting transfers between devices, moved(): return lax.ppermute(array, AXES, pairs)  79.5 us
    pallas_call x2, Pallas kernels, half_products(): pl.pallas_call(half_kernel, out_shape=jax.ShapeDtypeStruct((size, size),...  11.8 us
    unnamed x44, local copies, waits for them, and re-layouts  8.39 us
    pallas_call x1, Pallas kernels, last_products(): pl.pallas_call(last_kernel, out_shape=jax.ShapeDtypeStruct((size, 2 * siz...  6.36 us
    pallas_call x1, Pallas kernels, first_products(): pl.pallas_call(first_kernel, out_shape=(square, square), grid_spec=pltpu....  5.59 us
  transfers between devices with their start and end apart: 22, of which 7 were waited for; matrix products, arithmetic and copies ran while one was open for 3% of the time, Pallas kernels for 8%

profile of v3, /device:TPU:61, one launch (start us, length us, event | category | flops | bytes accessed | tf_op | source)
XLA Modules:
  0.0 262.8 jit_solution(4387997370862687451)
XLA Ops:
  6.5 0.7 all-gather.3.cloned.1.call-update
  7.3 0.0 all-gather.5.cloned.1.call-start
  7.3 2.2 constant_dynamic-slice_fusion.2
  9.6 3.5 %collective-permute-start.2 = (f32[512,256]{1,0:T(8,128)}, f32[512,256]{1,0:T(8,128)S(1)}, u32[]{:S(2)}, u32[]{:S(2)}) collective-permute-start(f32[512,256]{1,0:T(8,128)} %get-tuple-element.34), channel_id=1, source_target_pairs={{0,16},{1,17},{2,18},{3,19},{4,20},{5,21},{6,22},{7,23},{8,24},{9,... | collective-permute-start | bytes 1572872 | tf_op jit(solution)/shard_map/ppermute | solution.py:22
  13.1 1.9 collective-permute-start.3
  15.1 8.8 %collective-permute-start.1 = (f32[16,1024]{1,0:T(8,128)S(1)}, f32[16,1024]{1,0:T(8,128)S(1)}, u32[]{:S(2)}, u32[]{:S(2)}) collective-permute-start(f32[16,1024]{1,0:T(8,128)S(1)} %select_bitcast_fusion), channel_id=1, source_target_pairs={{0,64},{1,65},{2,66},{3,67},{4,68},{5,69},{6,70},{7,71},{8,72},{9,... | collective-permute-start | bytes 196616 | tf_op jit(solution)/shard_map/ppermute | solution.py:22
  24.0 0.1 fusion
  24.0 9.6 %collective-permute-start = (f32[128,512]{1,0:T(8,128)S(1)}, f32[128,512]{1,0:T(8,128)S(1)}, u32[]{:S(2)}, u32[]{:S(2)}) collective-permute-start(f32[128,512]{1,0:T(8,128)S(1)} %get-tuple-element.36), channel_id=1, source_target_pairs={{0,8},{1,9},{2,10},{3,11},{4,12},{5,13},{6,14},{7,15},{8,0},{9,1},... | collective-permute-start | bytes 786440 | tf_op jit(solution)/shard_map/ppermute | solution.py:22
  33.6 34.1 %collective-permute-done.1 = f32[16,1024]{1,0:T(8,128)S(1)} collective-permute-done((f32[16,1024]{1,0:T(8,128)S(1)}, f32[16,1024]{1,0:T(8,128)S(1)}, u32[]{:S(2)}, u32[]{:S(2)}) %collective-permute-start.1) | collective-permute-done | bytes 65568 | tf_op jit(solution)/shard_map/ppermute | solution.py:22
  67.8 6.3 %collective-permute-done = f32[128,512]{1,0:T(8,128)S(1)} collective-permute-done((f32[128,512]{1,0:T(8,128)S(1)}, f32[128,512]{1,0:T(8,128)S(1)}, u32[]{:S(2)}, u32[]{:S(2)}) %collective-permute-start) | collective-permute-done | bytes 262176 | tf_op jit(solution)/shard_map/ppermute | solution.py:22
  74.1 13.8 %collective-permute-start.7 = (f32[512,256]{1,0:T(8,128)}, f32[512,256]{1,0:T(8,128)S(1)}, u32[]{:S(2)}, u32[]{:S(2)}) collective-permute-start(f32[512,256]{1,0:T(8,128)} %get-tuple-element.18), channel_id=1, source_target_pairs={{0,16},{1,17},{2,18},{3,19},{4,20},{5,21},{6,22},{7,23},{8,24},{9,... | collective-permute-start | bytes 1572872 | tf_op jit(solution)/shard_map/ppermute | solution.py:22
  87.9 1.9 collective-permute-start.8
  89.8 0.0 collective-permute-done.2.refs_4_
  89.8 0.0 collective-permute-done.3.refs_5_
  89.9 2.4 collective-permute-start.4
  92.3 2.6 collective-permute-start.5
  94.9 3.8 %collective-permute-start.6 = (f32[2,128,512]{2,1,0:T(8,128)S(1)}, f32[2,128,512]{2,1,0:T(8,128)}, u32[]{:S(2)}, u32[]{:S(2)}) collective-permute-start(f32[2,128,512]{2,1,0:T(8,128)S(1)} %pad_maximum_fusion.1), channel_id=1, source_target_pairs={{0,2},{1,3},{2,4},{3,5},{4,6},{5,7},{6,0},{7,1},{8,10},{9,11},{10,... | collective-permute-start | bytes 1572872 | tf_op jit(solution)/shard_map/ppermute | solution.py:22
  98.7 6.8 %collective-permute-done.7.refs_6_ = f32[512,256]{1,0:T(8,128)S(1)} collective-permute-done((f32[512,256]{1,0:T(8,128)}, f32[512,256]{1,0:T(8,128)S(1)}, u32[]{:S(2)}, u32[]{:S(2)}) %collective-permute-start.7) | collective-permute-done | bytes 524320 | tf_op jit(solution)/shard_map/ppermute | solution.py:22
  105.5 15.9 %collective-permute-done.8.refs_7_ = f32[512,256]{1,0:T(8,128)S(1)} collective-permute-done((f32[512,256]{1,0:T(8,128)}, f32[512,256]{1,0:T(8,128)S(1)}, u32[]{:S(2)}, u32[]{:S(2)}) %collective-permute-start.8) | collective-permute-done | bytes 524320 | tf_op jit(solution)/shard_map/ppermute | solution.py:22
  121.4 0.0 collective-permute-done.4
  121.4 0.0 collective-permute-done.5
  121.4 0.9 copy-done.17
  122.3 0.8 copy-done.18
  123.1 0.0 collective-permute-done.6
  123.1 0.0 all-gather.5.cloned.1.call-update
  123.1 2.9 %pad_maximum_fusion.own_ref = f32[4,2,128,512]{3,2,1,0:T(8,128)} fusion(f32[1,2,128,512]{3,2,1,0:T(8,128)} %bitcast.20, f32[1,2,128,512]{3,2,1,0:T(8,128)} %bitcast.31, f32[1,2,128,512]{3,2,1,0:T(8,128)} %bitcast.30, f32[1,2,128,512]{3,2,1,0:T(8,128)S(1)} %bitcast.29), kind=kLoop, calls=%fused_computation | loop fusion | flops 1572864 | bytes 4194304 | tf_op jit(solution)/shard_map/stack | solution.py:248
  126.0 4.5 %collective-permute-start.9 = (f32[4,2,128,512]{3,2,1,0:T(8,128)}, f32[4,2,128,512]{3,2,1,0:T(8,128)}, u32[]{:S(2)}, u32[]{:S(2)}) collective-permute-start(f32[4,2,128,512]{3,2,1,0:T(8,128)} %pad_maximum_fusion.own_ref), channel_id=1, source_target_pairs={{0,1},{1,0},{2,3},{3,2},{4,5},{5,4},{6,7},{7,6},{8,9},{9,8},{10,11... | collective-permute-start | bytes 6291464 | tf_op jit(solution)/shard_map/ppermute | solution.py:22
  130.5 10.9 %collective-permute-start.10 = (f32[32,1024]{1,0:T(8,128)S(1)}, f32[32,1024]{1,0:T(8,128)S(1)}, u32[]{:S(2)}, u32[]{:S(2)}) collective-permute-start(f32[32,1024]{1,0:T(8,128)S(1)} %pad_maximum_fusion.4), channel_id=1, source_target_pairs={{16,0},{17,1},{18,2},{19,3},{20,4},{21,5},{22,6},{23,7},{24,8},{25... | collective-permute-start | bytes 393224 | tf_op jit(solution)/shard_map/ppermute | solution.py:22
  141.4 0.7 collective-permute-start.11
  142.1 2.4 constant_dynamic-slice_fusion.1
  144.5 0.7 collective-permute-start.12
  145.2 3.7 %collective-permute-start.16 = (f32[512,512]{1,0:T(8,128)}, f32[512,512]{1,0:T(8,128)}, u32[]{:S(2)}, u32[]{:S(2)}) collective-permute-start(f32[512,512]{1,0:T(8,128)} %constant_dynamic-slice_fusion.1), channel_id=1, source_target_pairs={{0,16},{1,17},{2,18},{3,19},{4,20},{5,21},{6,22},{7,23},{8,24},{9,... | collective-permute-start | bytes 3145736 | tf_op jit(solution)/shard_map/ppermute | solution.py:22
  148.9 0.0 collective-permute-done.10
  148.9 2.4 collective-permute-start.17
  151.3 0.0 collective-permute-done.11
  151.4 0.0 collective-permute-done.12
  151.4 0.7 collective-permute-start.13
  152.1 0.7 collective-permute-start.14
  152.8 0.0 collective-permute-done.9.mate_ref
  152.8 0.7 collective-permute-start.15
  153.6 0.1 pad_add_fusion.1.place_ref
  153.6 0.1 pad_add_fusion.2.place_ref
  153.7 2.8 %shard_map.55 = (bf16[3,512,512]{2,1,0:T(8,128)(2,1)S(1)}, bf16[3,512,512]{2,1,0:T(8,128)(2,1)S(1)}, f32[512,512]{1,0:T(8,128)S(1)}) custom-call(s32[3]{0:T(128)S(1)} %pad_add_fusion.2.place_ref, f32[4,2,128,512]{3,2,1,0:T(8,128)} %pad_maximum_fusion.own_ref, f32[4,2,128,512]{3,2,1,0:T(8,128)} %collective-permute-done.9.mate_ref), custom_call_target="tpu_custom_call" | custom-call | bytes 8388608 | tf_op jit(solution)/shard_map/pallas_call | solution.py:101
  156.5 0.0 copy-start
  156.5 1.1 copy-done
  157.7 1.2 copy-done.1
  158.9 1.0 copy-done.6
  159.9 0.0 collective-permute-done.13.refs_1_
  159.9 0.0 collective-permute-done.14.refs_2_
  159.9 0.0 collective-permute-done.15.refs_3_
  159.9 5.6 %shard_map.57.near_ref = f32[512,512]{1,0:T(8,128)S(1)} custom-call(s32[2]{0:T(128)S(1)} %pad_add_fusion.1.place_ref, f32[512,1024]{1,0:T(8,128)} %band_ref.3, bf16[3,512,512]{2,1,0:T(8,128)(2,1)} %copy-done, bf16[3,512,512]{2,1,0:T(8,128)(2,1)} %copy-done.1, f32[128,1024]{1,0:T(8,128)S(1)} %constant_dynamic-update-slice_fusion.refs_0_, ...), custom_call_target="tpu_custom_call" | custom-call | flops 2415919104 | bytes 8388608 | tf_op jit(solution)/shard_map/pallas_call | solution.py:156
  165.6 3.5 %collective-permute-start.19 = (f32[512,512]{1,0:T(8,128)S(1)}, f32[512,512]{1,0:T(8,128)}, u32[]{:S(2)}, u32[]{:S(2)}) collective-permute-start(f32[512,512]{1,0:T(8,128)S(1)} %shard_map.57.near_ref), channel_id=1, source_target_pairs={{1,2},{2,1},{3,4},{4,3},{5,6},{6,5},{7,8},{8,7},{9,10},{10,9},{11,... | collective-permute-start | bytes 3145736 | tf_op jit(solution)/shard_map/ppermute | solution.py:22
  169.0 2.8 %collective-permute-done.16.refs_4_ = f32[512,512]{1,0:T(8,128)} collective-permute-done((f32[512,512]{1,0:T(8,128)}, f32[512,512]{1,0:T(8,128)}, u32[]{:S(2)}, u32[]{:S(2)}) %collective-permute-start.16) | collective-permute-done | bytes 1048608 | tf_op jit(solution)/shard_map/ppermute | solution.py:22
  171.9 49.1 %collective-permute-done.17.refs_5_ = f32[512,512]{1,0:T(8,128)} collective-permute-done((f32[512,512]{1,0:T(8,128)}, f32[512,512]{1,0:T(8,128)}, u32[]{:S(2)}, u32[]{:S(2)}) %collective-permute-start.17) | collective-permute-done | bytes 1048608 | tf_op jit(solution)/shard_map/ppermute | solution.py:22
  221.0 1.0 copy-done.3
  222.0 1.0 copy-done.5
  223.1 6.2 %shard_map.56.near_ref = f32[512,512]{1,0:T(8,128)S(1)} custom-call(s32[2]{0:T(128)S(1)} %pad_add_fusion.1.place_ref, f32[512,1024]{1,0:T(8,128)} %band_ref.3, bf16[3,512,512]{2,1,0:T(8,128)(2,1)} %copy-done, bf16[3,512,512]{2,1,0:T(8,128)(2,1)} %copy-done.1, f32[128,1024]{1,0:T(8,128)S(1)} %constant_dynamic-update-slice_fusion.refs_0_, ...), custom_call_target="tpu_custom_call" | custom-call | flops 2415919104 | bytes 8388608 | tf_op jit(solution)/shard_map/pallas_call | solution.py:156
  229.3 2.9 %collective-permute-start.18 = (f32[512,512]{1,0:T(8,128)S(1)}, f32[512,512]{1,0:T(8,128)S(1)}, u32[]{:S(2)}, u32[]{:S(2)}) collective-permute-start(f32[512,512]{1,0:T(8,128)S(1)} %shard_map.56.near_ref), channel_id=1, source_target_pairs={{0,1},{1,0},{2,3},{3,2},{4,5},{5,4},{6,7},{7,6},{8,9},{9,8},{10,11... | collective-permute-start | bytes 3145736 | tf_op jit(solution)/shard_map/ppermute | solution.py:22
  232.1 0.1 pad_add_fusion.c_ref
  232.2 10.6 %collective-permute-done.19.cross_ref = f32[512,512]{1,0:T(8,128)} collective-permute-done((f32[512,512]{1,0:T(8,128)S(1)}, f32[512,512]{1,0:T(8,128)}, u32[]{:S(2)}, u32[]{:S(2)}) %collective-permute-start.19) | collective-permute-done | bytes 1048608 | tf_op jit(solution)/shard_map/ppermute | solution.py:22
  242.8 1.2 copy-done.7
  244.0 5.6 %shard_map.58 = (f32[512,512]{1,0:T(8,128)S(1)}, f32[512,512]{1,0:T(8,128)S(1)}) custom-call(s32[2]{0:T(128)S(1)} %pad_add_fusion.c_ref, f32[512,512]{1,0:T(8,128)S(1)} %shard_map.57.near_ref, f32[512,512]{1,0:T(8,128)} %collective-permute-done.19.cross_ref, f32[512,512]{1,0:T(8,128)S(1)} %copy-done.7, ...), custom_call_target="tpu_custom_call" | custom-call | flops 2415919104 | bytes 7340032 | tf_op jit(solution)/shard_map/pallas_call | solution.py:314
  249.6 0.0 collective-permute-done.18.sibling_ref
  249.6 6.4 %shard_map.59 = f32[512,1024]{1,0:T(8,128)} custom-call(s32[2]{0:T(128)S(1)} %pad_add_fusion.c_ref, f32[512,512]{1,0:T(8,128)S(1)} %shard_map.56.near_ref, f32[512,512]{1,0:T(8,128)S(1)} %collective-permute-done.18.sibling_ref, f32[2,3,512,512]{3,2,1,0:T(8,128)} %all-gather.5.cloned.1.call-done.r0_ref.r1_ref.r2_ref, ...), custom_call_target="tpu_custom_call" | custom-call | flops 2415919104 | bytes 9437184 | tf_op jit(solution)/shard_map/pallas_call | solution.py:338
  (45 shorter events, 0.2 us)
Async XLA Ops:
  6.5 8.5 %copy-start.16 = (f32[2,16,1024]{2,1,0:T(8,128)S(1)}, f32[2,16,1024]{2,1,0:T(8,128)}, u32[]{:S(2)}) copy-start(f32[2,16,1024]{2,1,0:T(8,128)} %param.8) | copy-start | bytes 393220
  6.5 17.4 %copy-start.20 = (f32[512,2,32]{0,2,1:T(8,128)S(1)}, f32[512,2,32]{0,2,1:T(8,128)}, u32[]{:S(2)}) copy-start(f32[512,2,32]{0,2,1:T(8,128)} %param.9) | copy-start | bytes 393220
  6.5 17.4 %copy-start.19 = (f32[1,3,512,32]{2,3,1,0:T(8,128)S(1)}, f32[1,3,512,32]{2,3,1,0:T(8,128)}, u32[]{:S(2)}) copy-start(f32[1,3,512,32]{2,3,1,0:T(8,128)} %param.6) | copy-start | bytes 589828
  6.5 116.5 %all-gather.3.cloned.1.call-start = ((), (), s32[]{:S(2)}) async-start(), calls=%async_computation | async-start | bytes 1769472 | tf_op jit(solution)/shard_map/all_gather | solution.py:178
  7.3 235.6 %all-gather.5.cloned.1.call-start = ((), (), s32[]{:S(2)}) async-start(), calls=%async_computation.1 | async-start | bytes 7864320 | tf_op jit(solution)/shard_map/all_gather | solution.py:183
  9.6 80.2 %collective-permute-start.2 = (f32[512,256]{1,0:T(8,128)}, f32[512,256]{1,0:T(8,128)S(1)}, u32[]{:S(2)}, u32[]{:S(2)}) collective-permute-start(f32[512,256]{1,0:T(8,128)} %get-tuple-element.34), channel_id=1, source_target_pairs={{0,16},{1,17},{2,18},{3,19},{4,20},{5,21},{6,22},{7,23},{8,24},{9,... | collective-permute-start | bytes 1572872 | tf_op jit(solution)/shard_map/ppermute | solution.py:22
  13.1 76.7 %collective-permute-start.3 = (f32[512,256]{1,0:T(8,128)}, f32[512,256]{1,0:T(8,128)S(1)}, u32[]{:S(2)}, u32[]{:S(2)}) collective-permute-start(f32[512,256]{1,0:T(8,128)} %get-tuple-element.34), channel_id=1, source_target_pairs={{16,0},{17,1},{18,2},{19,3},{20,4},{21,5},{22,6},{23,7},{24,8},{25... | collective-permute-start | bytes 1572872 | tf_op jit(solution)/shard_map/ppermute | solution.py:22
  15.1 52.6 %collective-permute-start.1 = (f32[16,1024]{1,0:T(8,128)S(1)}, f32[16,1024]{1,0:T(8,128)S(1)}, u32[]{:S(2)}, u32[]{:S(2)}) collective-permute-start(f32[16,1024]{1,0:T(8,128)S(1)} %select_bitcast_fusion), channel_id=1, source_target_pairs={{0,64},{1,65},{2,66},{3,67},{4,68},{5,69},{6,70},{7,71},{8,72},{9,... | collective-permute-start | bytes 196616 | tf_op jit(solution)/shard_map/ppermute | solution.py:22
  24.0 50.0 %collective-permute-start = (f32[128,512]{1,0:T(8,128)S(1)}, f32[128,512]{1,0:T(8,128)S(1)}, u32[]{:S(2)}, u32[]{:S(2)}) collective-permute-start(f32[128,512]{1,0:T(8,128)S(1)} %get-tuple-element.36), channel_id=1, source_target_pairs={{0,8},{1,9},{2,10},{3,11},{4,12},{5,13},{6,14},{7,15},{8,0},{9,1},... | collective-permute-start | bytes 786440 | tf_op jit(solution)/shard_map/ppermute | solution.py:22
  74.1 31.4 %collective-permute-start.7 = (f32[512,256]{1,0:T(8,128)}, f32[512,256]{1,0:T(8,128)S(1)}, u32[]{:S(2)}, u32[]{:S(2)}) collective-permute-start(f32[512,256]{1,0:T(8,128)} %get-tuple-element.18), channel_id=1, source_target_pairs={{0,16},{1,17},{2,18},{3,19},{4,20},{5,21},{6,22},{7,23},{8,24},{9,... | collective-permute-start | bytes 1572872 | tf_op jit(solution)/shard_map/ppermute | solution.py:22
  87.9 33.5 %collective-permute-start.8 = (f32[512,256]{1,0:T(8,128)}, f32[512,256]{1,0:T(8,128)S(1)}, u32[]{:S(2)}, u32[]{:S(2)}) collective-permute-start(f32[512,256]{1,0:T(8,128)} %get-tuple-element.18), channel_id=1, source_target_pairs={{16,0},{17,1},{18,2},{19,3},{20,4},{21,5},{22,6},{23,7},{24,8},{25... | collective-permute-start | bytes 1572872 | tf_op jit(solution)/shard_map/ppermute | solution.py:22
  89.8 36.2 %copy-start.8 = (f32[512,256]{1,0:T(8,128)}, f32[512,256]{1,0:T(8,128)S(1)}, u32[]{:S(2)}) copy-start(f32[512,256]{1,0:T(8,128)S(1)} %collective-permute-done.2.refs_4_) | copy-start | bytes 1572868
  89.8 36.2 %copy-start.10 = (f32[512,256]{1,0:T(8,128)}, f32[512,256]{1,0:T(8,128)S(1)}, u32[]{:S(2)}) copy-start(f32[512,256]{1,0:T(8,128)S(1)} %collective-permute-done.3.refs_5_) | copy-start | bytes 1572868
  89.9 31.5 %collective-permute-start.4 = (f32[2,128,512]{2,1,0:T(8,128)S(1)}, f32[2,128,512]{2,1,0:T(8,128)S(1)}, u32[]{:S(2)}, u32[]{:S(2)}) collective-permute-start(f32[2,128,512]{2,1,0:T(8,128)S(1)} %pad_maximum_fusion.1), channel_id=1, source_target_pairs={{0,6},{1,7},{2,0},{3,1},{4,2},{5,3},{6,4},{7,5},{8,14},{9,15},{10,... | collective-permute-start | bytes 1572872 | tf_op jit(solution)/shard_map/ppermute | solution.py:22
  92.3 29.1 %collective-permute-start.5 = (f32[2,128,512]{2,1,0:T(8,128)S(1)}, f32[2,128,512]{2,1,0:T(8,128)S(1)}, u32[]{:S(2)}, u32[]{:S(2)}) collective-permute-start(f32[2,128,512]{2,1,0:T(8,128)S(1)} %pad_maximum_fusion.1), channel_id=1, source_target_pairs={{0,4},{1,5},{2,6},{3,7},{4,0},{5,1},{6,2},{7,3},{8,12},{9,13},{10,... | collective-permute-start | bytes 1572872 | tf_op jit(solution)/shard_map/ppermute | solution.py:22
  94.9 28.2 %collective-permute-start.6 = (f32[2,128,512]{2,1,0:T(8,128)S(1)}, f32[2,128,512]{2,1,0:T(8,128)}, u32[]{:S(2)}, u32[]{:S(2)}) collective-permute-start(f32[2,128,512]{2,1,0:T(8,128)S(1)} %pad_maximum_fusion.1), channel_id=1, source_target_pairs={{0,2},{1,3},{2,4},{3,5},{4,6},{5,7},{6,0},{7,1},{8,10},{9,11},{10,... | collective-permute-start | bytes 1572872 | tf_op jit(solution)/shard_map/ppermute | solution.py:22
  105.5 20.5 %copy-start.12 = (f32[512,256]{1,0:T(8,128)}, f32[512,256]{1,0:T(8,128)S(1)}, u32[]{:S(2)}) copy-start(f32[512,256]{1,0:T(8,128)S(1)} %collective-permute-done.7.refs_6_) | copy-start | bytes 1572868
  121.4 4.6 %copy-start.14 = (f32[512,256]{1,0:T(8,128)}, f32[512,256]{1,0:T(8,128)S(1)}, u32[]{:S(2)}) copy-start(f32[512,256]{1,0:T(8,128)S(1)} %collective-permute-done.8.refs_7_) | copy-start | bytes 1572868
  121.4 0.9 copy-start.17
  122.3 0.8 copy-start.18
  126.0 26.8 %collective-permute-start.9 = (f32[4,2,128,512]{3,2,1,0:T(8,128)}, f32[4,2,128,512]{3,2,1,0:T(8,128)}, u32[]{:S(2)}, u32[]{:S(2)}) collective-permute-start(f32[4,2,128,512]{3,2,1,0:T(8,128)} %pad_maximum_fusion.own_ref), channel_id=1, source_target_pairs={{0,1},{1,0},{2,3},{3,2},{4,5},{5,4},{6,7},{7,6},{8,9},{9,8},{10,11... | collective-permute-start | bytes 6291464 | tf_op jit(solution)/shard_map/ppermute | solution.py:22
  130.5 18.4 %collective-permute-start.10 = (f32[32,1024]{1,0:T(8,128)S(1)}, f32[32,1024]{1,0:T(8,128)S(1)}, u32[]{:S(2)}, u32[]{:S(2)}) collective-permute-start(f32[32,1024]{1,0:T(8,128)S(1)} %pad_maximum_fusion.4), channel_id=1, source_target_pairs={{16,0},{17,1},{18,2},{19,3},{20,4},{21,5},{22,6},{23,7},{24,8},{25... | collective-permute-start | bytes 393224 | tf_op jit(solution)/shard_map/ppermute | solution.py:22
  141.4 9.9 %collective-permute-start.11 = (f32[32,1024]{1,0:T(8,128)S(1)}, f32[32,1024]{1,0:T(8,128)S(1)}, u32[]{:S(2)}, u32[]{:S(2)}) collective-permute-start(f32[32,1024]{1,0:T(8,128)S(1)} %pad_maximum_fusion.4), channel_id=1, source_target_pairs={{32,0},{33,1},{34,2},{35,3},{36,4},{37,5},{38,6},{39,7},{40,8},{41... | collective-permute-start | bytes 393224 | tf_op jit(solution)/shard_map/ppermute | solution.py:22
  144.5 6.8 %collective-permute-start.12 = (f32[32,1024]{1,0:T(8,128)S(1)}, f32[32,1024]{1,0:T(8,128)S(1)}, u32[]{:S(2)}, u32[]{:S(2)}) collective-permute-start(f32[32,1024]{1,0:T(8,128)S(1)} %pad_maximum_fusion.4), channel_id=1, source_target_pairs={{48,0},{49,1},{50,2},{51,3},{52,4},{53,5},{54,6},{55,7},{56,8},{57... | collective-permute-start | bytes 393224 | tf_op jit(solution)/shard_map/ppermute | solution.py:22
  145.2 26.7 %collective-permute-start.16 = (f32[512,512]{1,0:T(8,128)}, f32[512,512]{1,0:T(8,128)}, u32[]{:S(2)}, u32[]{:S(2)}) collective-permute-start(f32[512,512]{1,0:T(8,128)} %constant_dynamic-slice_fusion.1), channel_id=1, source_target_pairs={{0,16},{1,17},{2,18},{3,19},{4,20},{5,21},{6,22},{7,23},{8,24},{9,... | collective-permute-start | bytes 3145736 | tf_op jit(solution)/shard_map/ppermute | solution.py:22
  148.9 72.0 %collective-permute-start.17 = (f32[512,512]{1,0:T(8,128)}, f32[512,512]{1,0:T(8,128)}, u32[]{:S(2)}, u32[]{:S(2)}) collective-permute-start(f32[512,512]{1,0:T(8,128)} %constant_dynamic-slice_fusion.1), channel_id=1, source_target_pairs={{16,0},{17,1},{18,2},{19,3},{20,4},{21,5},{22,6},{23,7},{24,8},{25... | collective-permute-start | bytes 3145736 | tf_op jit(solution)/shard_map/ppermute | solution.py:22
  151.4 8.5 %collective-permute-start.13 = (f32[128,1024]{1,0:T(8,128)S(1)}, f32[128,1024]{1,0:T(8,128)S(1)}, u32[]{:S(2)}, u32[]{:S(2)}) collective-permute-start(f32[128,1024]{1,0:T(8,128)S(1)} %constant_dynamic-update-slice_fusion.refs_0_), channel_id=1, source_target_pairs={{128,0},{129,1},{130,2},{131,3},{132,4},{133,5},{134,6},{135,7},{1... | collective-permute-start | bytes 1572872 | tf_op jit(solution)/shard_map/ppermute | solution.py:22
  152.1 7.8 %collective-permute-start.14 = (f32[128,1024]{1,0:T(8,128)S(1)}, f32[128,1024]{1,0:T(8,128)S(1)}, u32[]{:S(2)}, u32[]{:S(2)}) collective-permute-start(f32[128,1024]{1,0:T(8,128)S(1)} %constant_dynamic-update-slice_fusion.refs_0_), channel_id=1, source_target_pairs={{240,496},{241,497},{242,498},{243,499},{244,500},{245,501},{246,5... | collective-permute-start | bytes 1572872 | tf_op jit(solution)/shard_map/ppermute | solution.py:22
  152.8 7.1 %collective-permute-start.15 = (f32[128,1024]{1,0:T(8,128)S(1)}, f32[128,1024]{1,0:T(8,128)S(1)}, u32[]{:S(2)}, u32[]{:S(2)}) collective-permute-start(f32[128,1024]{1,0:T(8,128)S(1)} %constant_dynamic-update-slice_fusion.refs_0_), channel_id=1, source_target_pairs={{112,496},{113,497},{114,498},{115,499},{116,500},{117,501},{118,5... | collective-permute-start | bytes 1572872 | tf_op jit(solution)/shard_map/ppermute | solution.py:22
  153.7 6.2 %copy-start.9 = (f32[512,256]{1,0:T(8,128)S(1)}, f32[512,256]{1,0:T(8,128)}, u32[]{:S(2)}) copy-start(f32[512,256]{1,0:T(8,128)} %copy-done.8) | copy-start | bytes 1572868
  153.7 6.2 %copy-start.11 = (f32[512,256]{1,0:T(8,128)S(1)}, f32[512,256]{1,0:T(8,128)}, u32[]{:S(2)}) copy-start(f32[512,256]{1,0:T(8,128)} %copy-done.10) | copy-start | bytes 1572868
  153.7 6.2 %copy-start.13 = (f32[512,256]{1,0:T(8,128)S(1)}, f32[512,256]{1,0:T(8,128)}, u32[]{:S(2)}) copy-start(f32[512,256]{1,0:T(8,128)} %copy-done.12) | copy-start | bytes 1572868
  153.7 6.2 %copy-start.15 = (f32[512,256]{1,0:T(8,128)S(1)}, f32[512,256]{1,0:T(8,128)}, u32[]{:S(2)}) copy-start(f32[512,256]{1,0:T(8,128)} %copy-done.14) | copy-start | bytes 1572868
  156.5 1.1 copy-start
  157.7 1.2 copy-start.1
  158.9 1.0 copy-start.6
  159.9 5.7 %copy-start.2 = (f32[128,1024]{1,0:T(8,128)}, f32[128,1024]{1,0:T(8,128)S(1)}, u32[]{:S(2)}) copy-start(f32[128,1024]{1,0:T(8,128)S(1)} %collective-permute-done.14.refs_2_) | copy-start | bytes 1572868
  159.9 5.7 %copy-start.4 = (f32[128,1024]{1,0:T(8,128)}, f32[128,1024]{1,0:T(8,128)S(1)}, u32[]{:S(2)}) copy-start(f32[128,1024]{1,0:T(8,128)S(1)} %collective-permute-done.15.refs_3_) | copy-start | bytes 1572868
  165.6 77.3 %collective-permute-start.19 = (f32[512,512]{1,0:T(8,128)S(1)}, f32[512,512]{1,0:T(8,128)}, u32[]{:S(2)}, u32[]{:S(2)}) collective-permute-start(f32[512,512]{1,0:T(8,128)S(1)} %shard_map.57.near_ref), channel_id=1, source_target_pairs={{1,2},{2,1},{3,4},{4,3},{5,6},{6,5},{7,8},{8,7},{9,10},{10,9},{11,... | collective-permute-start | bytes 3145736 | tf_op jit(solution)/shard_map/ppermute | solution.py:22
  221.0 1.0 copy-start.3
  222.0 1.0 copy-start.5
  229.3 20.4 %collective-permute-start.18 = (f32[512,512]{1,0:T(8,128)S(1)}, f32[512,512]{1,0:T(8,128)S(1)}, u32[]{:S(2)}, u32[]{:S(2)}) collective-permute-start(f32[512,512]{1,0:T(8,128)S(1)} %shard_map.56.near_ref), channel_id=1, source_target_pairs={{0,1},{1,0},{2,3},{3,2},{4,5},{5,4},{6,7},{7,6},{8,9},{9,8},{10,11... | collective-permute-start | bytes 3145736 | tf_op jit(solution)/shard_map/ppermute | solution.py:22
  242.8 1.2 copy-start.7
Sparse Core Ops, SparseCore 0:
  9.4 104.6 all-gather.2
  123.2 75.5 all-gather.4

commit v4 on v3

--- a/solution.py
+++ b/solution.py
@@ -242,7 +242,7 @@
     band = band_of(covariance, 0)
     outer = [rows_of(band[:, : size // 2])]
     pieces = along_y(after(pair, share, *outer[0]))
-    outer.append(rows_of(after(band[:, size // 2 :], share, pair)))
+    outer.append(rows_of(after(band[:, size // 2 :], share)))
     share = rows_second(share, outer[1])
     right_full = gather_ring(after(line, *outer[1], *pieces))
     pieces = jnp.stack(pieces)
@@ -257,8 +257,7 @@
     half_inner = half_products(1, place, covariance, high, low, edges, inner)
     sibling = moved(half_inner, core_swap)
     core = jnp.stack([c, jnp.where((col == 0) | (col == 15), 1, 0)])
-    sums = first_products(core, half_outer, cross, side, right_full)
-    return last_products(core, half_inner, sibling, right_full, *sums)
+    return final_products(core, cross, side, half_outer, half_inner, sibling, right_full)
 
 
 def split(array):
@@ -273,88 +272,69 @@
     return total + lax.dot_general(a[0], b[0], dims, preferred_element_type=jnp.float32)
 
 
-def first_kernel(
-    c_ref, near_ref, cross_ref, side_ref, r0_ref, r1_ref, r2_ref, outer_ref, inner_ref, held
+def final_kernel(
+    c_ref, cross_ref, side_ref, outer_ref, inner_ref, sibling_ref, r0, r1, r2, out_ref, held, high, low
 ):
-    held[...] = cross_ref[...]
-
-    @pl.when(c_ref[1] == 1)
+    band, part = pl.program_id(0), pl.program_id(1)
+
+    @pl.when((band == 0) & (part == 0))
     def _():
-        held[...] = side_ref[...].T
-
-    near, cross = split(near_ref[...]), split(held[...])
-    inner_ref[...] = times(near, split(r2_ref[...]))
-    outer_ref[...] = times(near, split(r1_ref[...])) + times(cross, split(r0_ref[...]))
-
-
-def last_kernel(c_ref, near_ref, sibling_ref, r0_ref, r1_ref, r2_ref, outer_ref, inner_ref, out_ref):
-    c, size = c_ref[0], near_ref.shape[0]
-    near = split(near_ref[...])
-    at = pl.multiple_of(c * size, 128)
-    out_ref[:, pl.ds(at, size)] = outer_ref[...] + times(near, split(r2_ref[...]))
-    at = pl.multiple_of((1 - c) * size, 128)
-    total = inner_ref[...] + times(near, split(r1_ref[...]))
-    out_ref[:, pl.ds(at, size)] = total + times(split(sibling_ref[...]), split(r0_ref[...]))
+        held[...] = cross_ref[...]
+
+        @pl.when(c_ref[1] == 1)
+        def _():
+            held[...] = side_ref[...].T
+
+        for k, ref in enumerate((held, outer_ref, inner_ref, sibling_ref)):
+            high[k], low[k] = split(ref[...])
+
+    for b, order in ((0, (0, 1, 2)), (1, (3, 2, 1))):
+
+        @pl.when(band == b)
+        def _():
+            total = None
+            for k, ref in zip(order, (r0, r1, r2)):
+                product = times((high[k], low[k]), split(ref[...]))
+                total = product if total is None else total + product
+            out_ref[...] = total
 
 
 def whole(*shape):
-    return pl.BlockSpec(shape, lambda i, c: (0,) * len(shape))
-
-
-def block_at(place, size):
-    return pl.BlockSpec((None, None, size, size), lambda i, c: (*place(c[0]), 0, 0))
+    return pl.BlockSpec(shape, lambda *_: (0,) * len(shape))
 
 
 PARAMS = pltpu.CompilerParams(vmem_limit_bytes=48 * 2**20)
 
 
-def first_products(c, near, cross, side, right):
-    size = near.shape[0]
-    square = jax.ShapeDtypeStruct((size, size), jnp.float32)
+def final_products(core, cross, side, outer, inner, sibling, right):
+    size, parts = outer.shape[0], 2
+
+    def right_at(place):
+        def index(band, part, c):
+            j = c[0] ^ band
+            return (j, place(j), part, 0)
+
+        return pl.BlockSpec((None, None, size // parts, size), index)
+
     return pl.pallas_call(
-        first_kernel,
-        out_shape=(square, square),
-        grid_spec=pltpu.PrefetchScalarGridSpec(
-            num_scalar_prefetch=1,
-            grid=(1,),
-            in_specs=[whole(size, size)] * 3
-            + [
-                block_at(lambda c: (c, 2 * c), size),
-                block_at(lambda c: (c, 1), size),
-                block_at(lambda c: (1 - c, 2 * c), size),
-            ],
-            out_specs=(whole(size, size), whole(size, size)),
-            scratch_shapes=[pltpu.VMEM((size, size), jnp.float32)],
-        ),
-        compiler_params=PARAMS,
-        cost_estimate=pl.CostEstimate(
-            flops=18 * size**3, bytes_accessed=28 * size**2, transcendentals=0
-        ),
-    )(c, near, cross, side, right, right, right)
-
-
-def last_products(c, near, sibling, right, outer, inner):
-    size = near.shape[0]
-    return pl.pallas_call(
-        last_kernel,
+        final_kernel,
         out_shape=jax.ShapeDtypeStruct((size, 2 * size), jnp.float32),
         grid_spec=pltpu.PrefetchScalarGridSpec(
             num_scalar_prefetch=1,
-            grid=(1,),
-            in_specs=[whole(size, size)] * 2
-            + [
-                block_at(lambda c: (1 - c, 2 - 2 * c), size),
-                block_at(lambda c: (1 - c, 1), size),
-                block_at(lambda c: (c, 2 - 2 * c), size),
-            ]
-            + [whole(size, size)] * 2,
-            out_specs=whole(size, 2 * size),
+            grid=(2, parts),
+            in_specs=[whole(size, size)] * 5
+            + [right_at(lambda j: 2 * j), right_at(lambda j: 1), right_at(lambda j: 2 - 2 * j)],
+            out_specs=pl.BlockSpec(
+                (size, size // parts), lambda band, part, c: (0, (c[0] ^ band) * parts + part)
+            ),
+            scratch_shapes=[pltpu.VMEM((size, size), jnp.float32)]
+            + [pltpu.VMEM((4, size, size), jnp.bfloat16)] * 2,
         ),
         compiler_params=PARAMS,
         cost_estimate=pl.CostEstimate(
-            flops=18 * size**3, bytes_accessed=36 * size**2, transcendentals=0
-        ),
-    )(c, near, sibling, right, right, right, outer, inner)
+            flops=36 * size**3, bytes_accessed=52 * size**2, transcendentals=0
+        ),
+    )(core, cross, side, outer, inner, sibling, right, right, right)
 
 
 def solution(mesh):

time: 264 us -> 268 us (1.015)
  starting transfers between devices: 79.6 us -> 108 us
  waiting for transfers between devices: 126 us -> 104 us
    ppermute x20, starting transfers between devices: 79.5 us -> 108 us  [moved(): return lax.ppermute(array, AXES, pairs)]
    ppermute x20, waiting for transfers between devices: 126 us -> 103 us  [moved(): return lax.ppermute(array, AXES, pairs)]
    pallas_call x2 -> x1, Pallas kernels: 11.9 us -> 9.84 us  [final_products(): pl.pallas_call(final_kernel, out_shape=jax.ShapeDtypeStruct((size, 2 * si...]
  transfers between devices with their start and end apart: 22 -> 22, of which waited for: 7 -> 6; matrix products, arithmetic and copies ran while one was open for 3% -> 3% of each run, Pallas kernels for 8% -> 6%
where the time goes in v4:
time: 268 us
  starting transfers between devices  108 us (40%)
  waiting for transfers between devices  104 us (39%)
  Pallas kernels  24.7 us (9%)
  between operations  14 us (5%)
  local copies, waits for them, and re-layouts  13 us (5%)
  other arithmetic  3.29 us (1%)
    ppermute x20, starting transfers between devices, moved(): return lax.ppermute(array, AXES, pairs)  108 us
    ppermute x20, waiting for transfers between devices, moved(): return lax.ppermute(array, AXES, pairs)  103 us
    pallas_call x2, Pallas kernels, half_products(): pl.pallas_call(half_kernel, out_shape=jax.ShapeDtypeStruct((size, size),...  12.1 us
    pallas_call x1, Pallas kernels, final_products(): pl.pallas_call(final_kernel, out_shape=jax.ShapeDtypeStruct((size, 2 * si...  9.84 us
    unnamed x44, local copies, waits for them, and re-layouts  8.38 us
  transfers between devices with their start and end apart: 22, of which 6 were waited for; matrix products, arithmetic and copies ran while one was open for 3% of the time, Pallas kernels for 6%

profile of v4, /device:TPU:61, one launch (start us, length us, event | category | flops | bytes accessed | tf_op | source)
XLA Modules:
  0.0 267.6 jit_solution(16845261904648816171)
XLA Ops:
  6.5 0.7 all-gather.3.cloned.1.call-update
  7.3 0.0 all-gather.5.cloned.1.call-start
  7.3 2.2 constant_dynamic-slice_fusion.2
  9.6 3.5 %collective-permute-start.2 = (f32[512,256]{1,0:T(8,128)}, f32[512,256]{1,0:T(8,128)S(1)}, u32[]{:S(2)}, u32[]{:S(2)}) collective-permute-start(f32[512,256]{1,0:T(8,128)} %get-tuple-element.30), channel_id=1, source_target_pairs={{0,16},{1,17},{2,18},{3,19},{4,20},{5,21},{6,22},{7,23},{8,24},{9,... | collective-permute-start | bytes 1572872 | tf_op jit(solution)/shard_map/ppermute | solution.py:22
  13.1 1.9 collective-permute-start.3
  15.1 8.8 %collective-permute-start.1 = (f32[16,1024]{1,0:T(8,128)S(1)}, f32[16,1024]{1,0:T(8,128)S(1)}, u32[]{:S(2)}, u32[]{:S(2)}) collective-permute-start(f32[16,1024]{1,0:T(8,128)S(1)} %select_bitcast_fusion), channel_id=1, source_target_pairs={{0,64},{1,65},{2,66},{3,67},{4,68},{5,69},{6,70},{7,71},{8,72},{9,... | collective-permute-start | bytes 196616 | tf_op jit(solution)/shard_map/ppermute | solution.py:22
  24.0 0.1 fusion
  24.0 9.6 %collective-permute-start = (f32[128,512]{1,0:T(8,128)S(1)}, f32[128,512]{1,0:T(8,128)S(1)}, u32[]{:S(2)}, u32[]{:S(2)}) collective-permute-start(f32[128,512]{1,0:T(8,128)S(1)} %get-tuple-element.32), channel_id=1, source_target_pairs={{0,8},{1,9},{2,10},{3,11},{4,12},{5,13},{6,14},{7,15},{8,0},{9,1},... | collective-permute-start | bytes 786440 | tf_op jit(solution)/shard_map/ppermute | solution.py:22
  33.6 34.1 %collective-permute-done.1 = f32[16,1024]{1,0:T(8,128)S(1)} collective-permute-done((f32[16,1024]{1,0:T(8,128)S(1)}, f32[16,1024]{1,0:T(8,128)S(1)}, u32[]{:S(2)}, u32[]{:S(2)}) %collective-permute-start.1) | collective-permute-done | bytes 65568 | tf_op jit(solution)/shard_map/ppermute | solution.py:22
  67.8 1.9 collective-permute-start.7
  69.7 13.0 %collective-permute-start.8 = (f32[512,256]{1,0:T(8,128)}, f32[512,256]{1,0:T(8,128)S(1)}, u32[]{:S(2)}, u32[]{:S(2)}) collective-permute-start(f32[512,256]{1,0:T(8,128)} %get-tuple-element.16), channel_id=1, source_target_pairs={{16,0},{17,1},{18,2},{19,3},{20,4},{21,5},{22,6},{23,7},{24,8},{25... | collective-permute-start | bytes 1572872 | tf_op jit(solution)/shard_map/ppermute | solution.py:22
  82.7 0.0 collective-permute-done
  82.8 0.0 collective-permute-done.2.refs_4_
  82.8 0.0 collective-permute-done.3.refs_5_
  82.8 2.2 collective-permute-start.6
  85.0 4.0 %collective-permute-start.5 = (f32[2,128,512]{2,1,0:T(8,128)S(1)}, f32[2,128,512]{2,1,0:T(8,128)S(1)}, u32[]{:S(2)}, u32[]{:S(2)}) collective-permute-start(f32[2,128,512]{2,1,0:T(8,128)S(1)} %pad_maximum_fusion.1), channel_id=1, source_target_pairs={{0,4},{1,5},{2,6},{3,7},{4,0},{5,1},{6,2},{7,3},{8,12},{9,13},{10,... | collective-permute-start | bytes 1572872 | tf_op jit(solution)/shard_map/ppermute | solution.py:22
  89.0 1.9 collective-permute-start.4
  90.9 9.1 %collective-permute-done.7.refs_6_ = f32[512,256]{1,0:T(8,128)S(1)} collective-permute-done((f32[512,256]{1,0:T(8,128)}, f32[512,256]{1,0:T(8,128)S(1)}, u32[]{:S(2)}, u32[]{:S(2)}) %collective-permute-start.7) | collective-permute-done | bytes 524320 | tf_op jit(solution)/shard_map/ppermute | solution.py:22
  100.0 19.2 %collective-permute-done.8.refs_7_ = f32[512,256]{1,0:T(8,128)S(1)} collective-permute-done((f32[512,256]{1,0:T(8,128)}, f32[512,256]{1,0:T(8,128)S(1)}, u32[]{:S(2)}, u32[]{:S(2)}) %collective-permute-start.8) | collective-permute-done | bytes 524320 | tf_op jit(solution)/shard_map/ppermute | solution.py:22
  119.3 0.0 collective-permute-done.6
  119.3 0.0 collective-permute-done.5
  119.3 0.8 copy-done.17
  120.1 0.8 copy-done.18
  121.0 0.0 collective-permute-done.4
  121.0 0.1 all-gather.3.cloned.1.call-done
  121.0 0.0 all-gather.5.cloned.1.call-update
  121.0 2.9 %pad_maximum_fusion.own_ref = f32[4,2,128,512]{3,2,1,0:T(8,128)} fusion(f32[1,2,128,512]{3,2,1,0:T(8,128)} %bitcast.30, f32[1,2,128,512]{3,2,1,0:T(8,128)} %bitcast.31, f32[1,2,128,512]{3,2,1,0:T(8,128)} %bitcast.18, f32[1,2,128,512]{3,2,1,0:T(8,128)S(1)} %bitcast.29), kind=kLoop, calls=%fused_computation | loop fusion | flops 1572864 | bytes 4194304 | tf_op jit(solution)/shard_map/stack | solution.py:248
  124.0 3.3 %collective-permute-start.9 = (f32[4,2,128,512]{3,2,1,0:T(8,128)}, f32[4,2,128,512]{3,2,1,0:T(8,128)}, u32[]{:S(2)}, u32[]{:S(2)}) collective-permute-start(f32[4,2,128,512]{3,2,1,0:T(8,128)} %pad_maximum_fusion.own_ref), channel_id=1, source_target_pairs={{0,1},{1,0},{2,3},{3,2},{4,5},{5,4},{6,7},{7,6},{8,9},{9,8},{10,11... | collective-permute-start | bytes 6291464 | tf_op jit(solution)/shard_map/ppermute | solution.py:22
  127.3 3.2 %collective-permute-start.10 = (f32[32,1024]{1,0:T(8,128)S(1)}, f32[32,1024]{1,0:T(8,128)S(1)}, u32[]{:S(2)}, u32[]{:S(2)}) collective-permute-start(f32[32,1024]{1,0:T(8,128)S(1)} %pad_maximum_fusion.4), channel_id=1, source_target_pairs={{16,0},{17,1},{18,2},{19,3},{20,4},{21,5},{22,6},{23,7},{24,8},{25... | collective-permute-start | bytes 393224 | tf_op jit(solution)/shard_map/ppermute | solution.py:22
  130.5 0.7 collective-permute-start.11
  131.2 2.3 constant_dynamic-slice_fusion.1
  133.5 0.7 collective-permute-start.12
  134.2 3.7 %collective-permute-start.17 = (f32[512,512]{1,0:T(8,128)}, f32[512,512]{1,0:T(8,128)}, u32[]{:S(2)}, u32[]{:S(2)}) collective-permute-start(f32[512,512]{1,0:T(8,128)} %constant_dynamic-slice_fusion.1), channel_id=1, source_target_pairs={{0,16},{1,17},{2,18},{3,19},{4,20},{5,21},{6,22},{7,23},{8,24},{9,... | collective-permute-start | bytes 3145736 | tf_op jit(solution)/shard_map/ppermute | solution.py:22
  137.9 0.0 collective-permute-done.10
  137.9 2.4 collective-permute-start.18
  140.4 0.0 collective-permute-done.11
  140.4 0.0 collective-permute-done.12
  140.4 0.7 collective-permute-start.13
  141.1 0.7 collective-permute-start.14
  141.8 0.0 collective-permute-done.9.mate_ref
  141.8 0.7 collective-permute-start.15
  142.6 0.1 pad_add_fusion.1.place_ref
  142.6 0.1 pad_add_fusion.2.place_ref
  142.7 2.8 %shard_map.55 = (bf16[3,512,512]{2,1,0:T(8,128)(2,1)S(1)}, bf16[3,512,512]{2,1,0:T(8,128)(2,1)S(1)}, f32[512,512]{1,0:T(8,128)S(1)}) custom-call(s32[3]{0:T(128)S(1)} %pad_add_fusion.2.place_ref, f32[4,2,128,512]{3,2,1,0:T(8,128)} %pad_maximum_fusion.own_ref, f32[4,2,128,512]{3,2,1,0:T(8,128)} %collective-permute-done.9.mate_ref), custom_call_target="tpu_custom_call" | custom-call | bytes 8388608 | tf_op jit(solution)/shard_map/pallas_call | solution.py:101
  145.5 0.0 copy-start
  145.5 1.1 copy-done
  146.7 1.2 copy-done.1
  147.9 1.0 copy-done.6
  148.9 0.0 collective-permute-done.13.refs_1_
  148.9 0.0 collective-permute-done.14.refs_2_
  148.9 0.0 collective-permute-done.15.refs_3_
  148.9 5.9 %shard_map.56.outer_ref = f32[512,512]{1,0:T(8,128)S(1)} custom-call(s32[2]{0:T(128)S(1)} %pad_add_fusion.1.place_ref, f32[512,1024]{1,0:T(8,128)} %band_ref.3, bf16[3,512,512]{2,1,0:T(8,128)(2,1)} %copy-done, bf16[3,512,512]{2,1,0:T(8,128)(2,1)} %copy-done.1, f32[128,1024]{1,0:T(8,128)S(1)} %constant_dynamic-update-slice_fusion.refs_0_, ...), custom_call_target="tpu_custom_call" | custom-call | flops 2415919104 | bytes 8388608 | tf_op jit(solution)/shard_map/pallas_call | solution.py:156
  154.9 43.1 %collective-permute-start.16 = (f32[512,512]{1,0:T(8,128)S(1)}, f32[512,512]{1,0:T(8,128)}, u32[]{:S(2)}, u32[]{:S(2)}) collective-permute-start(f32[512,512]{1,0:T(8,128)S(1)} %shard_map.56.outer_ref), channel_id=1, source_target_pairs={{1,2},{2,1},{3,4},{4,3},{5,6},{6,5},{7,8},{8,7},{9,10},{10,9},{11,... | collective-permute-start | bytes 3145736 | tf_op jit(solution)/shard_map/ppermute | solution.py:22
  198.0 0.0 collective-permute-done.17.refs_4_
  198.0 11.2 %collective-permute-done.18.refs_5_ = f32[512,512]{1,0:T(8,128)} collective-permute-done((f32[512,512]{1,0:T(8,128)}, f32[512,512]{1,0:T(8,128)}, u32[]{:S(2)}, u32[]{:S(2)}) %collective-permute-start.18) | collective-permute-done | bytes 1048608 | tf_op jit(solution)/shard_map/ppermute | solution.py:22
  209.2 1.0 copy-done.3
  210.3 1.0 copy-done.5
  211.3 6.2 %shard_map.57.inner_ref = f32[512,512]{1,0:T(8,128)S(1)} custom-call(s32[2]{0:T(128)S(1)} %pad_add_fusion.1.place_ref, f32[512,1024]{1,0:T(8,128)} %band_ref.3, bf16[3,512,512]{2,1,0:T(8,128)(2,1)} %copy-done, bf16[3,512,512]{2,1,0:T(8,128)(2,1)} %copy-done.1, f32[128,1024]{1,0:T(8,128)S(1)} %constant_dynamic-update-slice_fusion.refs_0_, ...), custom_call_target="tpu_custom_call" | custom-call | flops 2415919104 | bytes 8388608 | tf_op jit(solution)/shard_map/pallas_call | solution.py:156
  217.5 2.4 collective-permute-start.19
  219.9 0.1 pad_add_fusion.c_ref
  220.0 29.7 %collective-permute-done.16.cross_ref = f32[512,512]{1,0:T(8,128)} collective-permute-done((f32[512,512]{1,0:T(8,128)S(1)}, f32[512,512]{1,0:T(8,128)}, u32[]{:S(2)}, u32[]{:S(2)}) %collective-permute-start.16) | collective-permute-done | bytes 1048608 | tf_op jit(solution)/shard_map/ppermute | solution.py:22
  249.6 0.0 collective-permute-done.19.sibling_ref
  249.7 1.2 copy-done.7
  250.9 9.8 %shard_map.58 = f32[512,1024]{1,0:T(8,128)} custom-call(s32[2]{0:T(128)S(1)} %pad_add_fusion.c_ref, f32[512,512]{1,0:T(8,128)} %collective-permute-done.16.cross_ref, f32[512,512]{1,0:T(8,128)S(1)} %copy-done.7, f32[512,512]{1,0:T(8,128)S(1)} %shard_map.56.outer_ref, f32[512,512]{1,0:T(8,128)S(1)} %shard_map.57.inner_ref, ...), custom_call_target="tpu_custom_call" | custom-call | flops 4831838208 | bytes 13631488 | tf_op jit(solution)/shard_map/pallas_call | solution.py:319
  (44 shorter events, 0.2 us)
Async XLA Ops:
  6.5 8.5 %copy-start.16 = (f32[2,16,1024]{2,1,0:T(8,128)S(1)}, f32[2,16,1024]{2,1,0:T(8,128)}, u32[]{:S(2)}) copy-start(f32[2,16,1024]{2,1,0:T(8,128)} %param.8) | copy-start | bytes 393220
  6.5 17.4 %copy-start.20 = (f32[512,2,32]{0,2,1:T(8,128)S(1)}, f32[512,2,32]{0,2,1:T(8,128)}, u32[]{:S(2)}) copy-start(f32[512,2,32]{0,2,1:T(8,128)} %param.9) | copy-start | bytes 393220
  6.5 17.4 %copy-start.19 = (f32[1,3,512,32]{2,3,1,0:T(8,128)S(1)}, f32[1,3,512,32]{2,3,1,0:T(8,128)}, u32[]{:S(2)}) copy-start(f32[1,3,512,32]{2,3,1,0:T(8,128)} %param.6) | copy-start | bytes 589828
  6.5 114.5 %all-gather.3.cloned.1.call-start = ((), (), s32[]{:S(2)}) async-start(), calls=%async_computation | async-start | bytes 1769472 | tf_op jit(solution)/shard_map/all_gather | solution.py:178
  7.3 242.4 %all-gather.5.cloned.1.call-start = ((), (), s32[]{:S(2)}) async-start(), calls=%async_computation.1 | async-start | bytes 7864320 | tf_op jit(solution)/shard_map/all_gather | solution.py:183
  9.6 73.2 %collective-permute-start.2 = (f32[512,256]{1,0:T(8,128)}, f32[512,256]{1,0:T(8,128)S(1)}, u32[]{:S(2)}, u32[]{:S(2)}) collective-permute-start(f32[512,256]{1,0:T(8,128)} %get-tuple-element.30), channel_id=1, source_target_pairs={{0,16},{1,17},{2,18},{3,19},{4,20},{5,21},{6,22},{7,23},{8,24},{9,... | collective-permute-start | bytes 1572872 | tf_op jit(solution)/shard_map/ppermute | solution.py:22
  13.1 69.7 %collective-permute-start.3 = (f32[512,256]{1,0:T(8,128)}, f32[512,256]{1,0:T(8,128)S(1)}, u32[]{:S(2)}, u32[]{:S(2)}) collective-permute-start(f32[512,256]{1,0:T(8,128)} %get-tuple-element.30), channel_id=1, source_target_pairs={{16,0},{17,1},{18,2},{19,3},{20,4},{21,5},{22,6},{23,7},{24,8},{25... | collective-permute-start | bytes 1572872 | tf_op jit(solution)/shard_map/ppermute | solution.py:22
  15.1 52.6 %collective-permute-start.1 = (f32[16,1024]{1,0:T(8,128)S(1)}, f32[16,1024]{1,0:T(8,128)S(1)}, u32[]{:S(2)}, u32[]{:S(2)}) collective-permute-start(f32[16,1024]{1,0:T(8,128)S(1)} %select_bitcast_fusion), channel_id=1, source_target_pairs={{0,64},{1,65},{2,66},{3,67},{4,68},{5,69},{6,70},{7,71},{8,72},{9,... | collective-permute-start | bytes 196616 | tf_op jit(solution)/shard_map/ppermute | solution.py:22
  24.0 58.7 %collective-permute-start = (f32[128,512]{1,0:T(8,128)S(1)}, f32[128,512]{1,0:T(8,128)S(1)}, u32[]{:S(2)}, u32[]{:S(2)}) collective-permute-start(f32[128,512]{1,0:T(8,128)S(1)} %get-tuple-element.32), channel_id=1, source_target_pairs={{0,8},{1,9},{2,10},{3,11},{4,12},{5,13},{6,14},{7,15},{8,0},{9,1},... | collective-permute-start | bytes 786440 | tf_op jit(solution)/shard_map/ppermute | solution.py:22
  67.8 32.3 %collective-permute-start.7 = (f32[512,256]{1,0:T(8,128)}, f32[512,256]{1,0:T(8,128)S(1)}, u32[]{:S(2)}, u32[]{:S(2)}) collective-permute-start(f32[512,256]{1,0:T(8,128)} %get-tuple-element.16), channel_id=1, source_target_pairs={{0,16},{1,17},{2,18},{3,19},{4,20},{5,21},{6,22},{7,23},{8,24},{9,... | collective-permute-start | bytes 1572872 | tf_op jit(solution)/shard_map/ppermute | solution.py:22
  69.7 49.6 %collective-permute-start.8 = (f32[512,256]{1,0:T(8,128)}, f32[512,256]{1,0:T(8,128)S(1)}, u32[]{:S(2)}, u32[]{:S(2)}) collective-permute-start(f32[512,256]{1,0:T(8,128)} %get-tuple-element.16), channel_id=1, source_target_pairs={{16,0},{17,1},{18,2},{19,3},{20,4},{21,5},{22,6},{23,7},{24,8},{25... | collective-permute-start | bytes 1572872 | tf_op jit(solution)/shard_map/ppermute | solution.py:22
  82.8 41.2 %copy-start.8 = (f32[512,256]{1,0:T(8,128)}, f32[512,256]{1,0:T(8,128)S(1)}, u32[]{:S(2)}) copy-start(f32[512,256]{1,0:T(8,128)S(1)} %collective-permute-done.2.refs_4_) | copy-start | bytes 1572868
  82.8 41.1 %copy-start.10 = (f32[512,256]{1,0:T(8,128)}, f32[512,256]{1,0:T(8,128)S(1)}, u32[]{:S(2)}) copy-start(f32[512,256]{1,0:T(8,128)S(1)} %collective-permute-done.3.refs_5_) | copy-start | bytes 1572868
  82.8 36.5 %collective-permute-start.6 = (f32[2,128,512]{2,1,0:T(8,128)S(1)}, f32[2,128,512]{2,1,0:T(8,128)S(1)}, u32[]{:S(2)}, u32[]{:S(2)}) collective-permute-start(f32[2,128,512]{2,1,0:T(8,128)S(1)} %pad_maximum_fusion.1), channel_id=1, source_target_pairs={{0,2},{1,3},{2,4},{3,5},{4,6},{5,7},{6,0},{7,1},{8,10},{9,11},{10,... | collective-permute-start | bytes 1572872 | tf_op jit(solution)/shard_map/ppermute | solution.py:22
  85.0 34.3 %collective-permute-start.5 = (f32[2,128,512]{2,1,0:T(8,128)S(1)}, f32[2,128,512]{2,1,0:T(8,128)S(1)}, u32[]{:S(2)}, u32[]{:S(2)}) collective-permute-start(f32[2,128,512]{2,1,0:T(8,128)S(1)} %pad_maximum_fusion.1), channel_id=1, source_target_pairs={{0,4},{1,5},{2,6},{3,7},{4,0},{5,1},{6,2},{7,3},{8,12},{9,13},{10,... | collective-permute-start | bytes 1572872 | tf_op jit(solution)/shard_map/ppermute | solution.py:22
  89.0 32.0 %collective-permute-start.4 = (f32[2,128,512]{2,1,0:T(8,128)S(1)}, f32[2,128,512]{2,1,0:T(8,128)}, u32[]{:S(2)}, u32[]{:S(2)}) collective-permute-start(f32[2,128,512]{2,1,0:T(8,128)S(1)} %pad_maximum_fusion.1), channel_id=1, source_target_pairs={{0,6},{1,7},{2,0},{3,1},{4,2},{5,3},{6,4},{7,5},{8,14},{9,15},{10,... | collective-permute-start | bytes 1572872 | tf_op jit(solution)/shard_map/ppermute | solution.py:22
  100.0 23.9 %copy-start.12 = (f32[512,256]{1,0:T(8,128)}, f32[512,256]{1,0:T(8,128)S(1)}, u32[]{:S(2)}) copy-start(f32[512,256]{1,0:T(8,128)S(1)} %collective-permute-done.7.refs_6_) | copy-start | bytes 1572868
  119.3 4.7 %copy-start.14 = (f32[512,256]{1,0:T(8,128)}, f32[512,256]{1,0:T(8,128)S(1)}, u32[]{:S(2)}) copy-start(f32[512,256]{1,0:T(8,128)S(1)} %collective-permute-done.8.refs_7_) | copy-start | bytes 1572868
  119.3 0.8 copy-start.17
  120.1 0.8 copy-start.18
  124.0 17.9 %collective-permute-start.9 = (f32[4,2,128,512]{3,2,1,0:T(8,128)}, f32[4,2,128,512]{3,2,1,0:T(8,128)}, u32[]{:S(2)}, u32[]{:S(2)}) collective-permute-start(f32[4,2,128,512]{3,2,1,0:T(8,128)} %pad_maximum_fusion.own_ref), channel_id=1, source_target_pairs={{0,1},{1,0},{2,3},{3,2},{4,5},{5,4},{6,7},{7,6},{8,9},{9,8},{10,11... | collective-permute-start | bytes 6291464 | tf_op jit(solution)/shard_map/ppermute | solution.py:22
  127.3 10.6 %collective-permute-start.10 = (f32[32,1024]{1,0:T(8,128)S(1)}, f32[32,1024]{1,0:T(8,128)S(1)}, u32[]{:S(2)}, u32[]{:S(2)}) collective-permute-start(f32[32,1024]{1,0:T(8,128)S(1)} %pad_maximum_fusion.4), channel_id=1, source_target_pairs={{16,0},{17,1},{18,2},{19,3},{20,4},{21,5},{22,6},{23,7},{24,8},{25... | collective-permute-start | bytes 393224 | tf_op jit(solution)/shard_map/ppermute | solution.py:22
  130.5 9.8 %collective-permute-start.11 = (f32[32,1024]{1,0:T(8,128)S(1)}, f32[32,1024]{1,0:T(8,128)S(1)}, u32[]{:S(2)}, u32[]{:S(2)}) collective-permute-start(f32[32,1024]{1,0:T(8,128)S(1)} %pad_maximum_fusion.4), channel_id=1, source_target_pairs={{32,0},{33,1},{34,2},{35,3},{36,4},{37,5},{38,6},{39,7},{40,8},{41... | collective-permute-start | bytes 393224 | tf_op jit(solution)/shard_map/ppermute | solution.py:22
  133.5 6.9 %collective-permute-start.12 = (f32[32,1024]{1,0:T(8,128)S(1)}, f32[32,1024]{1,0:T(8,128)S(1)}, u32[]{:S(2)}, u32[]{:S(2)}) collective-permute-start(f32[32,1024]{1,0:T(8,128)S(1)} %pad_maximum_fusion.4), channel_id=1, source_target_pairs={{48,0},{49,1},{50,2},{51,3},{52,4},{53,5},{54,6},{55,7},{56,8},{57... | collective-permute-start | bytes 393224 | tf_op jit(solution)/shard_map/ppermute | solution.py:22
  134.2 63.8 %collective-permute-start.17 = (f32[512,512]{1,0:T(8,128)}, f32[512,512]{1,0:T(8,128)}, u32[]{:S(2)}, u32[]{:S(2)}) collective-permute-start(f32[512,512]{1,0:T(8,128)} %constant_dynamic-slice_fusion.1), channel_id=1, source_target_pairs={{0,16},{1,17},{2,18},{3,19},{4,20},{5,21},{6,22},{7,23},{8,24},{9,... | collective-permute-start | bytes 3145736 | tf_op jit(solution)/shard_map/ppermute | solution.py:22
  137.9 71.3 %collective-permute-start.18 = (f32[512,512]{1,0:T(8,128)}, f32[512,512]{1,0:T(8,128)}, u32[]{:S(2)}, u32[]{:S(2)}) collective-permute-start(f32[512,512]{1,0:T(8,128)} %constant_dynamic-slice_fusion.1), channel_id=1, source_target_pairs={{16,0},{17,1},{18,2},{19,3},{20,4},{21,5},{22,6},{23,7},{24,8},{25... | collective-permute-start | bytes 3145736 | tf_op jit(solution)/shard_map/ppermute | solution.py:22
  140.4 8.4 %collective-permute-start.13 = (f32[128,1024]{1,0:T(8,128)S(1)}, f32[128,1024]{1,0:T(8,128)S(1)}, u32[]{:S(2)}, u32[]{:S(2)}) collective-permute-start(f32[128,1024]{1,0:T(8,128)S(1)} %constant_dynamic-update-slice_fusion.refs_0_), channel_id=1, source_target_pairs={{128,0},{129,1},{130,2},{131,3},{132,4},{133,5},{134,6},{135,7},{1... | collective-permute-start | bytes 1572872 | tf_op jit(solution)/shard_map/ppermute | solution.py:22
  141.1 7.7 %collective-permute-start.14 = (f32[128,1024]{1,0:T(8,128)S(1)}, f32[128,1024]{1,0:T(8,128)S(1)}, u32[]{:S(2)}, u32[]{:S(2)}) collective-permute-start(f32[128,1024]{1,0:T(8,128)S(1)} %constant_dynamic-update-slice_fusion.refs_0_), channel_id=1, source_target_pairs={{240,496},{241,497},{242,498},{243,499},{244,500},{245,501},{246,5... | collective-permute-start | bytes 1572872 | tf_op jit(solution)/shard_map/ppermute | solution.py:22
  141.8 7.0 %collective-permute-start.15 = (f32[128,1024]{1,0:T(8,128)S(1)}, f32[128,1024]{1,0:T(8,128)S(1)}, u32[]{:S(2)}, u32[]{:S(2)}) collective-permute-start(f32[128,1024]{1,0:T(8,128)S(1)} %constant_dynamic-update-slice_fusion.refs_0_), channel_id=1, source_target_pairs={{112,496},{113,497},{114,498},{115,499},{116,500},{117,501},{118,5... | collective-permute-start | bytes 1572872 | tf_op jit(solution)/shard_map/ppermute | solution.py:22
  142.7 6.2 %copy-start.9 = (f32[512,256]{1,0:T(8,128)S(1)}, f32[512,256]{1,0:T(8,128)}, u32[]{:S(2)}) copy-start(f32[512,256]{1,0:T(8,128)} %copy-done.8) | copy-start | bytes 1572868
  142.7 6.2 %copy-start.11 = (f32[512,256]{1,0:T(8,128)S(1)}, f32[512,256]{1,0:T(8,128)}, u32[]{:S(2)}) copy-start(f32[512,256]{1,0:T(8,128)} %copy-done.10) | copy-start | bytes 1572868
  142.7 6.2 %copy-start.13 = (f32[512,256]{1,0:T(8,128)S(1)}, f32[512,256]{1,0:T(8,128)}, u32[]{:S(2)}) copy-start(f32[512,256]{1,0:T(8,128)} %copy-done.12) | copy-start | bytes 1572868
  142.7 6.2 %copy-start.15 = (f32[512,256]{1,0:T(8,128)S(1)}, f32[512,256]{1,0:T(8,128)}, u32[]{:S(2)}) copy-start(f32[512,256]{1,0:T(8,128)} %copy-done.14) | copy-start | bytes 1572868
  145.5 1.1 copy-start
  146.7 1.2 copy-start.1
  147.9 1.0 copy-start.6
  148.9 6.0 %copy-start.2 = (f32[128,1024]{1,0:T(8,128)}, f32[128,1024]{1,0:T(8,128)S(1)}, u32[]{:S(2)}) copy-start(f32[128,1024]{1,0:T(8,128)S(1)} %collective-permute-done.14.refs_2_) | copy-start | bytes 1572868
  148.9 6.0 %copy-start.4 = (f32[128,1024]{1,0:T(8,128)}, f32[128,1024]{1,0:T(8,128)S(1)}, u32[]{:S(2)}) copy-start(f32[128,1024]{1,0:T(8,128)S(1)} %collective-permute-done.15.refs_3_) | copy-start | bytes 1572868
  154.9 94.8 %collective-permute-start.16 = (f32[512,512]{1,0:T(8,128)S(1)}, f32[512,512]{1,0:T(8,128)}, u32[]{:S(2)}, u32[]{:S(2)}) collective-permute-start(f32[512,512]{1,0:T(8,128)S(1)} %shard_map.56.outer_ref), channel_id=1, source_target_pairs={{1,2},{2,1},{3,4},{4,3},{5,6},{6,5},{7,8},{8,7},{9,10},{10,9},{11,... | collective-permute-start | bytes 3145736 | tf_op jit(solution)/shard_map/ppermute | solution.py:22
  209.2 1.0 copy-start.3
  210.3 1.0 copy-start.5
  217.5 32.1 %collective-permute-start.19 = (f32[512,512]{1,0:T(8,128)S(1)}, f32[512,512]{1,0:T(8,128)S(1)}, u32[]{:S(2)}, u32[]{:S(2)}) collective-permute-start(f32[512,512]{1,0:T(8,128)S(1)} %shard_map.57.inner_ref), channel_id=1, source_target_pairs={{0,1},{1,0},{2,3},{3,2},{4,5},{5,4},{6,7},{7,6},{8,9},{9,8},{10,11... | collective-permute-start | bytes 3145736 | tf_op jit(solution)/shard_map/ppermute | solution.py:22
  249.7 1.2 copy-start.7
Sparse Core Ops, SparseCore 0:
  9.4 111.5 all-gather.2
  123.1 79.0 all-gather.4

commit v5 on v4

--- a/solution.py
+++ b/solution.py
@@ -242,7 +242,7 @@
     band = band_of(covariance, 0)
     outer = [rows_of(band[:, : size // 2])]
     pieces = along_y(after(pair, share, *outer[0]))
-    outer.append(rows_of(after(band[:, size // 2 :], share)))
+    outer.append(rows_of(after(band[:, size // 2 :], share, pair)))
     share = rows_second(share, outer[1])
     right_full = gather_ring(after(line, *outer[1], *pieces))
     pieces = jnp.stack(pieces)

time: 268 us -> 261 us (0.974)
  the two profiles are of different devices: /device:TPU:61 before, /device:TPU:292 now
where the time goes in v5:
time: 261 us; the launch traced here: 260 us
  waiting for transfers between devices  127 us (49%)
  starting transfers between devices  78.1 us (30%)
  Pallas kernels  24.8 us (10%)
  between operations  14 us (5%)
  local copies, waits for them, and re-layouts  13 us (5%)
  other arithmetic  3.29 us (1%)
    ppermute x20, waiting for transfers between devices, moved(): return lax.ppermute(array, AXES, pairs)  126 us
    ppermute x20, starting transfers between devices, moved(): return lax.ppermute(array, AXES, pairs)  78.1 us
    pallas_call x2, Pallas kernels, half_products(): pl.pallas_call(half_kernel, out_shape=jax.ShapeDtypeStruct((size, size),...  11.7 us
    pallas_call x1, Pallas kernels, final_products(): pl.pallas_call(final_kernel, out_shape=jax.ShapeDtypeStruct((size, 2 * si...  9.84 us
    unnamed x44, local copies, waits for them, and re-layouts  8.38 us
  transfers between devices with their start and end apart: 22, of which 6 were waited for; matrix products, arithmetic and copies ran while one was open for 3% of the time, Pallas kernels for 6%

profile of v5, /device:TPU:292, one launch (start us, length us, event | category | flops | bytes accessed | tf_op | source)
XLA Modules:
  0.0 260.0 jit_solution(1988419792450463097)
XLA Ops:
  6.5 0.7 all-gather.3.cloned.1.call-update
  7.3 0.0 all-gather.5.cloned.1.call-start
  7.3 2.2 constant_dynamic-slice_fusion.2
  9.6 2.9 %collective-permute-start.2 = (f32[512,256]{1,0:T(8,128)}, f32[512,256]{1,0:T(8,128)S(1)}, u32[]{:S(2)}, u32[]{:S(2)}) collective-permute-start(f32[512,256]{1,0:T(8,128)} %get-tuple-element.30), channel_id=1, source_target_pairs={{0,16},{1,17},{2,18},{3,19},{4,20},{5,21},{6,22},{7,23},{8,24},{9,... | collective-permute-start | bytes 1572872 | tf_op jit(solution)/shard_map/ppermute | solution.py:22
  12.5 2.9 %collective-permute-start.3 = (f32[512,256]{1,0:T(8,128)}, f32[512,256]{1,0:T(8,128)S(1)}, u32[]{:S(2)}, u32[]{:S(2)}) collective-permute-start(f32[512,256]{1,0:T(8,128)} %get-tuple-element.30), channel_id=1, source_target_pairs={{16,0},{17,1},{18,2},{19,3},{20,4},{21,5},{22,6},{23,7},{24,8},{25... | collective-permute-start | bytes 1572872 | tf_op jit(solution)/shard_map/ppermute | solution.py:22
  15.5 4.3 %collective-permute-start.1 = (f32[16,1024]{1,0:T(8,128)S(1)}, f32[16,1024]{1,0:T(8,128)S(1)}, u32[]{:S(2)}, u32[]{:S(2)}) collective-permute-start(f32[16,1024]{1,0:T(8,128)S(1)} %select_bitcast_fusion), channel_id=1, source_target_pairs={{0,64},{1,65},{2,66},{3,67},{4,68},{5,69},{6,70},{7,71},{8,72},{9,... | collective-permute-start | bytes 196616 | tf_op jit(solution)/shard_map/ppermute | solution.py:22
  19.8 0.0 copy-done.20
  19.8 0.1 fusion
  19.9 4.5 %collective-permute-start = (f32[128,512]{1,0:T(8,128)S(1)}, f32[128,512]{1,0:T(8,128)S(1)}, u32[]{:S(2)}, u32[]{:S(2)}) collective-permute-start(f32[128,512]{1,0:T(8,128)S(1)} %get-tuple-element.32), channel_id=1, source_target_pairs={{0,8},{1,9},{2,10},{3,11},{4,12},{5,13},{6,14},{7,15},{8,0},{9,1},... | collective-permute-start | bytes 786440 | tf_op jit(solution)/shard_map/ppermute | solution.py:22
  24.4 42.9 %collective-permute-done.1 = f32[16,1024]{1,0:T(8,128)S(1)} collective-permute-done((f32[16,1024]{1,0:T(8,128)S(1)}, f32[16,1024]{1,0:T(8,128)S(1)}, u32[]{:S(2)}, u32[]{:S(2)}) %collective-permute-start.1) | collective-permute-done | bytes 65568 | tf_op jit(solution)/shard_map/ppermute | solution.py:22
  67.4 0.0 collective-permute-done
  67.4 13.0 %collective-permute-start.7 = (f32[512,256]{1,0:T(8,128)}, f32[512,256]{1,0:T(8,128)S(1)}, u32[]{:S(2)}, u32[]{:S(2)}) collective-permute-start(f32[512,256]{1,0:T(8,128)} %get-tuple-element.16), channel_id=1, source_target_pairs={{0,16},{1,17},{2,18},{3,19},{4,20},{5,21},{6,22},{7,23},{8,24},{9,... | collective-permute-start | bytes 1572872 | tf_op jit(solution)/shard_map/ppermute | solution.py:22
  80.4 8.5 %collective-permute-start.8 = (f32[512,256]{1,0:T(8,128)}, f32[512,256]{1,0:T(8,128)S(1)}, u32[]{:S(2)}, u32[]{:S(2)}) collective-permute-start(f32[512,256]{1,0:T(8,128)} %get-tuple-element.16), channel_id=1, source_target_pairs={{16,0},{17,1},{18,2},{19,3},{20,4},{21,5},{22,6},{23,7},{24,8},{25... | collective-permute-start | bytes 1572872 | tf_op jit(solution)/shard_map/ppermute | solution.py:22
  88.9 0.0 collective-permute-done.2.refs_4_
  89.0 0.0 collective-permute-done.3.refs_5_
  89.0 3.7 %collective-permute-start.6 = (f32[2,128,512]{2,1,0:T(8,128)S(1)}, f32[2,128,512]{2,1,0:T(8,128)S(1)}, u32[]{:S(2)}, u32[]{:S(2)}) collective-permute-start(f32[2,128,512]{2,1,0:T(8,128)S(1)} %pad_maximum_fusion.1), channel_id=1, source_target_pairs={{0,2},{1,3},{2,4},{3,5},{4,6},{5,7},{6,0},{7,1},{8,10},{9,11},{10,... | collective-permute-start | bytes 1572872 | tf_op jit(solution)/shard_map/ppermute | solution.py:22
  92.7 5.0 %collective-permute-start.5 = (f32[2,128,512]{2,1,0:T(8,128)S(1)}, f32[2,128,512]{2,1,0:T(8,128)S(1)}, u32[]{:S(2)}, u32[]{:S(2)}) collective-permute-start(f32[2,128,512]{2,1,0:T(8,128)S(1)} %pad_maximum_fusion.1), channel_id=1, source_target_pairs={{0,4},{1,5},{2,6},{3,7},{4,0},{5,1},{6,2},{7,3},{8,12},{9,13},{10,... | collective-permute-start | bytes 1572872 | tf_op jit(solution)/shard_map/ppermute | solution.py:22
  97.6 3.1 %collective-permute-start.4 = (f32[2,128,512]{2,1,0:T(8,128)S(1)}, f32[2,128,512]{2,1,0:T(8,128)}, u32[]{:S(2)}, u32[]{:S(2)}) collective-permute-start(f32[2,128,512]{2,1,0:T(8,128)S(1)} %pad_maximum_fusion.1), channel_id=1, source_target_pairs={{0,6},{1,7},{2,0},{3,1},{4,2},{5,3},{6,4},{7,5},{8,14},{9,15},{10,... | collective-permute-start | bytes 1572872 | tf_op jit(solution)/shard_map/ppermute | solution.py:22
  100.7 4.6 %collective-permute-done.7.refs_6_ = f32[512,256]{1,0:T(8,128)S(1)} collective-permute-done((f32[512,256]{1,0:T(8,128)}, f32[512,256]{1,0:T(8,128)S(1)}, u32[]{:S(2)}, u32[]{:S(2)}) %collective-permute-start.7) | collective-permute-done | bytes 524320 | tf_op jit(solution)/shard_map/ppermute | solution.py:22
  105.3 13.6 %collective-permute-done.8.refs_7_ = f32[512,256]{1,0:T(8,128)S(1)} collective-permute-done((f32[512,256]{1,0:T(8,128)}, f32[512,256]{1,0:T(8,128)S(1)}, u32[]{:S(2)}, u32[]{:S(2)}) %collective-permute-start.8) | collective-permute-done | bytes 524320 | tf_op jit(solution)/shard_map/ppermute | solution.py:22
  118.9 0.0 collective-permute-done.6
  118.9 0.0 collective-permute-done.5
  119.0 0.8 copy-done.17
  119.8 0.8 copy-done.18
  120.6 0.0 collective-permute-done.4
  120.6 0.0 all-gather.5.cloned.1.call-update
  120.7 2.9 %pad_maximum_fusion.own_ref = f32[4,2,128,512]{3,2,1,0:T(8,128)} fusion(f32[1,2,128,512]{3,2,1,0:T(8,128)} %bitcast.30, f32[1,2,128,512]{3,2,1,0:T(8,128)} %bitcast.31, f32[1,2,128,512]{3,2,1,0:T(8,128)} %bitcast.18, f32[1,2,128,512]{3,2,1,0:T(8,128)S(1)} %bitcast.29), kind=kLoop, calls=%fused_computation | loop fusion | flops 1572864 | bytes 4194304 | tf_op jit(solution)/shard_map/stack | solution.py:248
  123.6 1.9 collective-permute-start.9
  125.5 1.4 collective-permute-start.10
  127.0 0.7 collective-permute-start.11
  127.6 2.3 constant_dynamic-slice_fusion.1
  130.0 0.7 collective-permute-start.12
  130.6 4.0 %collective-permute-start.17 = (f32[512,512]{1,0:T(8,128)}, f32[512,512]{1,0:T(8,128)}, u32[]{:S(2)}, u32[]{:S(2)}) collective-permute-start(f32[512,512]{1,0:T(8,128)} %constant_dynamic-slice_fusion.1), channel_id=1, source_target_pairs={{0,16},{1,17},{2,18},{3,19},{4,20},{5,21},{6,22},{7,23},{8,24},{9,... | collective-permute-start | bytes 3145736 | tf_op jit(solution)/shard_map/ppermute | solution.py:22
  134.6 0.0 collective-permute-done.10
  134.6 3.0 %collective-permute-start.18 = (f32[512,512]{1,0:T(8,128)}, f32[512,512]{1,0:T(8,128)}, u32[]{:S(2)}, u32[]{:S(2)}) collective-permute-start(f32[512,512]{1,0:T(8,128)} %constant_dynamic-slice_fusion.1), channel_id=1, source_target_pairs={{16,0},{17,1},{18,2},{19,3},{20,4},{21,5},{22,6},{23,7},{24,8},{25... | collective-permute-start | bytes 3145736 | tf_op jit(solution)/shard_map/ppermute | solution.py:22
  137.7 0.0 collective-permute-done.11
  137.7 0.0 collective-permute-done.12
  137.8 0.7 collective-permute-start.13
  138.5 0.7 collective-permute-start.14
  139.2 0.0 collective-permute-done.9.mate_ref
  139.2 0.7 collective-permute-start.15
  139.9 0.1 pad_add_fusion.1.place_ref
  140.0 0.1 pad_add_fusion.2.place_ref
  140.1 3.3 %shard_map.55 = (bf16[3,512,512]{2,1,0:T(8,128)(2,1)S(1)}, bf16[3,512,512]{2,1,0:T(8,128)(2,1)S(1)}, f32[512,512]{1,0:T(8,128)S(1)}) custom-call(s32[3]{0:T(128)S(1)} %pad_add_fusion.2.place_ref, f32[4,2,128,512]{3,2,1,0:T(8,128)} %pad_maximum_fusion.own_ref, f32[4,2,128,512]{3,2,1,0:T(8,128)} %collective-permute-done.9.mate_ref), custom_call_target="tpu_custom_call" | custom-call | bytes 8388608 | tf_op jit(solution)/shard_map/pallas_call | solution.py:101
  143.4 0.0 copy-start
  143.4 1.1 copy-done
  144.6 1.2 copy-done.1
  145.7 1.0 copy-done.6
  146.7 0.0 collective-permute-done.13.refs_1_
  146.7 0.0 collective-permute-done.14.refs_2_
  146.8 0.0 collective-permute-done.15.refs_3_
  146.8 5.5 %shard_map.56.outer_ref = f32[512,512]{1,0:T(8,128)S(1)} custom-call(s32[2]{0:T(128)S(1)} %pad_add_fusion.1.place_ref, f32[512,1024]{1,0:T(8,128)} %band_ref.3, bf16[3,512,512]{2,1,0:T(8,128)(2,1)} %copy-done, bf16[3,512,512]{2,1,0:T(8,128)(2,1)} %copy-done.1, f32[128,1024]{1,0:T(8,128)S(1)} %constant_dynamic-update-slice_fusion.refs_0_, ...), custom_call_target="tpu_custom_call" | custom-call | flops 2415919104 | bytes 8388608 | tf_op jit(solution)/shard_map/pallas_call | solution.py:156
  152.4 14.4 %collective-permute-start.16 = (f32[512,512]{1,0:T(8,128)S(1)}, f32[512,512]{1,0:T(8,128)}, u32[]{:S(2)}, u32[]{:S(2)}) collective-permute-start(f32[512,512]{1,0:T(8,128)S(1)} %shard_map.56.outer_ref), channel_id=1, source_target_pairs={{1,2},{2,1},{3,4},{4,3},{5,6},{6,5},{7,8},{8,7},{9,10},{10,9},{11,... | collective-permute-start | bytes 3145736 | tf_op jit(solution)/shard_map/ppermute | solution.py:22
  166.8 13.4 %collective-permute-done.17.refs_4_ = f32[512,512]{1,0:T(8,128)} collective-permute-done((f32[512,512]{1,0:T(8,128)}, f32[512,512]{1,0:T(8,128)}, u32[]{:S(2)}, u32[]{:S(2)}) %collective-permute-start.17) | collective-permute-done | bytes 1048608 | tf_op jit(solution)/shard_map/ppermute | solution.py:22
  180.2 4.4 %collective-permute-done.18.refs_5_ = f32[512,512]{1,0:T(8,128)} collective-permute-done((f32[512,512]{1,0:T(8,128)}, f32[512,512]{1,0:T(8,128)}, u32[]{:S(2)}, u32[]{:S(2)}) %collective-permute-start.18) | collective-permute-done | bytes 1048608 | tf_op jit(solution)/shard_map/ppermute | solution.py:22
  184.7 1.0 copy-done.3
  185.7 1.0 copy-done.5
  186.8 6.1 %shard_map.57.inner_ref = f32[512,512]{1,0:T(8,128)S(1)} custom-call(s32[2]{0:T(128)S(1)} %pad_add_fusion.1.place_ref, f32[512,1024]{1,0:T(8,128)} %band_ref.3, bf16[3,512,512]{2,1,0:T(8,128)(2,1)} %copy-done, bf16[3,512,512]{2,1,0:T(8,128)(2,1)} %copy-done.1, f32[128,1024]{1,0:T(8,128)S(1)} %constant_dynamic-update-slice_fusion.refs_0_, ...), custom_call_target="tpu_custom_call" | custom-call | flops 2415919104 | bytes 8388608 | tf_op jit(solution)/shard_map/pallas_call | solution.py:156
  192.9 1.9 collective-permute-start.19
  194.8 0.1 pad_add_fusion.c_ref
  194.9 47.2 %collective-permute-done.16.cross_ref = f32[512,512]{1,0:T(8,128)} collective-permute-done((f32[512,512]{1,0:T(8,128)S(1)}, f32[512,512]{1,0:T(8,128)}, u32[]{:S(2)}, u32[]{:S(2)}) %collective-permute-start.16) | collective-permute-done | bytes 1048608 | tf_op jit(solution)/shard_map/ppermute | solution.py:22
  242.1 0.0 collective-permute-done.19.sibling_ref
  242.1 1.2 copy-done.7
  243.3 9.8 %shard_map.58 = f32[512,1024]{1,0:T(8,128)} custom-call(s32[2]{0:T(128)S(1)} %pad_add_fusion.c_ref, f32[512,512]{1,0:T(8,128)} %collective-permute-done.16.cross_ref, f32[512,512]{1,0:T(8,128)S(1)} %copy-done.7, f32[512,512]{1,0:T(8,128)S(1)} %shard_map.56.outer_ref, f32[512,512]{1,0:T(8,128)S(1)} %shard_map.57.inner_ref, ...), custom_call_target="tpu_custom_call" | custom-call | flops 4831838208 | bytes 13631488 | tf_op jit(solution)/shard_map/pallas_call | solution.py:319
  (44 shorter events, 0.2 us)
Async XLA Ops:
  6.5 8.9 %copy-start.16 = (f32[2,16,1024]{2,1,0:T(8,128)S(1)}, f32[2,16,1024]{2,1,0:T(8,128)}, u32[]{:S(2)}) copy-start(f32[2,16,1024]{2,1,0:T(8,128)} %param.8) | copy-start | bytes 393220
  6.5 13.2 %copy-start.20 = (f32[512,2,32]{0,2,1:T(8,128)S(1)}, f32[512,2,32]{0,2,1:T(8,128)}, u32[]{:S(2)}) copy-start(f32[512,2,32]{0,2,1:T(8,128)} %param.9) | copy-start | bytes 393220
  6.5 13.3 %copy-start.19 = (f32[1,3,512,32]{2,3,1,0:T(8,128)S(1)}, f32[1,3,512,32]{2,3,1,0:T(8,128)}, u32[]{:S(2)}) copy-start(f32[1,3,512,32]{2,3,1,0:T(8,128)} %param.6) | copy-start | bytes 589828
  6.5 114.1 %all-gather.3.cloned.1.call-start = ((), (), s32[]{:S(2)}) async-start(), calls=%async_computation | async-start | bytes 1769472 | tf_op jit(solution)/shard_map/all_gather | solution.py:178
  7.3 234.8 %all-gather.5.cloned.1.call-start = ((), (), s32[]{:S(2)}) async-start(), calls=%async_computation.1 | async-start | bytes 7864320 | tf_op jit(solution)/shard_map/all_gather | solution.py:183
  9.6 79.4 %collective-permute-start.2 = (f32[512,256]{1,0:T(8,128)}, f32[512,256]{1,0:T(8,128)S(1)}, u32[]{:S(2)}, u32[]{:S(2)}) collective-permute-start(f32[512,256]{1,0:T(8,128)} %get-tuple-element.30), channel_id=1, source_target_pairs={{0,16},{1,17},{2,18},{3,19},{4,20},{5,21},{6,22},{7,23},{8,24},{9,... | collective-permute-start | bytes 1572872 | tf_op jit(solution)/shard_map/ppermute | solution.py:22
  12.5 76.5 %collective-permute-start.3 = (f32[512,256]{1,0:T(8,128)}, f32[512,256]{1,0:T(8,128)S(1)}, u32[]{:S(2)}, u32[]{:S(2)}) collective-permute-start(f32[512,256]{1,0:T(8,128)} %get-tuple-element.30), channel_id=1, source_target_pairs={{16,0},{17,1},{18,2},{19,3},{20,4},{21,5},{22,6},{23,7},{24,8},{25... | collective-permute-start | bytes 1572872 | tf_op jit(solution)/shard_map/ppermute | solution.py:22
  15.5 51.8 %collective-permute-start.1 = (f32[16,1024]{1,0:T(8,128)S(1)}, f32[16,1024]{1,0:T(8,128)S(1)}, u32[]{:S(2)}, u32[]{:S(2)}) collective-permute-start(f32[16,1024]{1,0:T(8,128)S(1)} %select_bitcast_fusion), channel_id=1, source_target_pairs={{0,64},{1,65},{2,66},{3,67},{4,68},{5,69},{6,70},{7,71},{8,72},{9,... | collective-permute-start | bytes 196616 | tf_op jit(solution)/shard_map/ppermute | solution.py:22
  19.9 47.5 %collective-permute-start = (f32[128,512]{1,0:T(8,128)S(1)}, f32[128,512]{1,0:T(8,128)S(1)}, u32[]{:S(2)}, u32[]{:S(2)}) collective-permute-start(f32[128,512]{1,0:T(8,128)S(1)} %get-tuple-element.32), channel_id=1, source_target_pairs={{0,8},{1,9},{2,10},{3,11},{4,12},{5,13},{6,14},{7,15},{8,0},{9,1},... | collective-permute-start | bytes 786440 | tf_op jit(solution)/shard_map/ppermute | solution.py:22
  67.4 37.9 %collective-permute-start.7 = (f32[512,256]{1,0:T(8,128)}, f32[512,256]{1,0:T(8,128)S(1)}, u32[]{:S(2)}, u32[]{:S(2)}) collective-permute-start(f32[512,256]{1,0:T(8,128)} %get-tuple-element.16), channel_id=1, source_target_pairs={{0,16},{1,17},{2,18},{3,19},{4,20},{5,21},{6,22},{7,23},{8,24},{9,... | collective-permute-start | bytes 1572872 | tf_op jit(solution)/shard_map/ppermute | solution.py:22
  80.4 38.5 %collective-permute-start.8 = (f32[512,256]{1,0:T(8,128)}, f32[512,256]{1,0:T(8,128)S(1)}, u32[]{:S(2)}, u32[]{:S(2)}) collective-permute-start(f32[512,256]{1,0:T(8,128)} %get-tuple-element.16), channel_id=1, source_target_pairs={{16,0},{17,1},{18,2},{19,3},{20,4},{21,5},{22,6},{23,7},{24,8},{25... | collective-permute-start | bytes 1572872 | tf_op jit(solution)/shard_map/ppermute | solution.py:22
  89.0 34.6 %copy-start.8 = (f32[512,256]{1,0:T(8,128)}, f32[512,256]{1,0:T(8,128)S(1)}, u32[]{:S(2)}) copy-start(f32[512,256]{1,0:T(8,128)S(1)} %collective-permute-done.2.refs_4_) | copy-start | bytes 1572868
  89.0 34.6 %copy-start.10 = (f32[512,256]{1,0:T(8,128)}, f32[512,256]{1,0:T(8,128)S(1)}, u32[]{:S(2)}) copy-start(f32[512,256]{1,0:T(8,128)S(1)} %collective-permute-done.3.refs_5_) | copy-start | bytes 1572868
  89.0 30.0 %collective-permute-start.6 = (f32[2,128,512]{2,1,0:T(8,128)S(1)}, f32[2,128,512]{2,1,0:T(8,128)S(1)}, u32[]{:S(2)}, u32[]{:S(2)}) collective-permute-start(f32[2,128,512]{2,1,0:T(8,128)S(1)} %pad_maximum_fusion.1), channel_id=1, source_target_pairs={{0,2},{1,3},{2,4},{3,5},{4,6},{5,7},{6,0},{7,1},{8,10},{9,11},{10,... | collective-permute-start | bytes 1572872 | tf_op jit(solution)/shard_map/ppermute | solution.py:22
  92.7 26.3 %collective-permute-start.5 = (f32[2,128,512]{2,1,0:T(8,128)S(1)}, f32[2,128,512]{2,1,0:T(8,128)S(1)}, u32[]{:S(2)}, u32[]{:S(2)}) collective-permute-start(f32[2,128,512]{2,1,0:T(8,128)S(1)} %pad_maximum_fusion.1), channel_id=1, source_target_pairs={{0,4},{1,5},{2,6},{3,7},{4,0},{5,1},{6,2},{7,3},{8,12},{9,13},{10,... | collective-permute-start | bytes 1572872 | tf_op jit(solution)/shard_map/ppermute | solution.py:22
  97.6 23.0 %collective-permute-start.4 = (f32[2,128,512]{2,1,0:T(8,128)S(1)}, f32[2,128,512]{2,1,0:T(8,128)}, u32[]{:S(2)}, u32[]{:S(2)}) collective-permute-start(f32[2,128,512]{2,1,0:T(8,128)S(1)} %pad_maximum_fusion.1), channel_id=1, source_target_pairs={{0,6},{1,7},{2,0},{3,1},{4,2},{5,3},{6,4},{7,5},{8,14},{9,15},{10,... | collective-permute-start | bytes 1572872 | tf_op jit(solution)/shard_map/ppermute | solution.py:22
  105.3 18.2 %copy-start.12 = (f32[512,256]{1,0:T(8,128)}, f32[512,256]{1,0:T(8,128)S(1)}, u32[]{:S(2)}) copy-start(f32[512,256]{1,0:T(8,128)S(1)} %collective-permute-done.7.refs_6_) | copy-start | bytes 1572868
  118.9 4.6 %copy-start.14 = (f32[512,256]{1,0:T(8,128)}, f32[512,256]{1,0:T(8,128)S(1)}, u32[]{:S(2)}) copy-start(f32[512,256]{1,0:T(8,128)S(1)} %collective-permute-done.8.refs_7_) | copy-start | bytes 1572868
  118.9 0.8 copy-start.17
  119.8 0.8 copy-start.18
  123.6 15.6 %collective-permute-start.9 = (f32[4,2,128,512]{3,2,1,0:T(8,128)}, f32[4,2,128,512]{3,2,1,0:T(8,128)}, u32[]{:S(2)}, u32[]{:S(2)}) collective-permute-start(f32[4,2,128,512]{3,2,1,0:T(8,128)} %pad_maximum_fusion.own_ref), channel_id=1, source_target_pairs={{0,1},{1,0},{2,3},{3,2},{4,5},{5,4},{6,7},{7,6},{8,9},{9,8},{10,11... | collective-permute-start | bytes 6291464 | tf_op jit(solution)/shard_map/ppermute | solution.py:22
  125.5 9.1 %collective-permute-start.10 = (f32[32,1024]{1,0:T(8,128)S(1)}, f32[32,1024]{1,0:T(8,128)S(1)}, u32[]{:S(2)}, u32[]{:S(2)}) collective-permute-start(f32[32,1024]{1,0:T(8,128)S(1)} %pad_maximum_fusion.4), channel_id=1, source_target_pairs={{16,0},{17,1},{18,2},{19,3},{20,4},{21,5},{22,6},{23,7},{24,8},{25... | collective-permute-start | bytes 393224 | tf_op jit(solution)/shard_map/ppermute | solution.py:22
  127.0 10.7 %collective-permute-start.11 = (f32[32,1024]{1,0:T(8,128)S(1)}, f32[32,1024]{1,0:T(8,128)S(1)}, u32[]{:S(2)}, u32[]{:S(2)}) collective-permute-start(f32[32,1024]{1,0:T(8,128)S(1)} %pad_maximum_fusion.4), channel_id=1, source_target_pairs={{32,0},{33,1},{34,2},{35,3},{36,4},{37,5},{38,6},{39,7},{40,8},{41... | collective-permute-start | bytes 393224 | tf_op jit(solution)/shard_map/ppermute | solution.py:22
  130.0 7.8 %collective-permute-start.12 = (f32[32,1024]{1,0:T(8,128)S(1)}, f32[32,1024]{1,0:T(8,128)S(1)}, u32[]{:S(2)}, u32[]{:S(2)}) collective-permute-start(f32[32,1024]{1,0:T(8,128)S(1)} %pad_maximum_fusion.4), channel_id=1, source_target_pairs={{48,0},{49,1},{50,2},{51,3},{52,4},{53,5},{54,6},{55,7},{56,8},{57... | collective-permute-start | bytes 393224 | tf_op jit(solution)/shard_map/ppermute | solution.py:22
  130.6 49.6 %collective-permute-start.17 = (f32[512,512]{1,0:T(8,128)}, f32[512,512]{1,0:T(8,128)}, u32[]{:S(2)}, u32[]{:S(2)}) collective-permute-start(f32[512,512]{1,0:T(8,128)} %constant_dynamic-slice_fusion.1), channel_id=1, source_target_pairs={{0,16},{1,17},{2,18},{3,19},{4,20},{5,21},{6,22},{7,23},{8,24},{9,... | collective-permute-start | bytes 3145736 | tf_op jit(solution)/shard_map/ppermute | solution.py:22
  134.6 50.0 %collective-permute-start.18 = (f32[512,512]{1,0:T(8,128)}, f32[512,512]{1,0:T(8,128)}, u32[]{:S(2)}, u32[]{:S(2)}) collective-permute-start(f32[512,512]{1,0:T(8,128)} %constant_dynamic-slice_fusion.1), channel_id=1, source_target_pairs={{16,0},{17,1},{18,2},{19,3},{20,4},{21,5},{22,6},{23,7},{24,8},{25... | collective-permute-start | bytes 3145736 | tf_op jit(solution)/shard_map/ppermute | solution.py:22
  137.8 9.0 %collective-permute-start.13 = (f32[128,1024]{1,0:T(8,128)S(1)}, f32[128,1024]{1,0:T(8,128)S(1)}, u32[]{:S(2)}, u32[]{:S(2)}) collective-permute-start(f32[128,1024]{1,0:T(8,128)S(1)} %constant_dynamic-update-slice_fusion.refs_0_), channel_id=1, source_target_pairs={{128,0},{129,1},{130,2},{131,3},{132,4},{133,5},{134,6},{135,7},{1... | collective-permute-start | bytes 1572872 | tf_op jit(solution)/shard_map/ppermute | solution.py:22
  138.5 8.3 %collective-permute-start.14 = (f32[128,1024]{1,0:T(8,128)S(1)}, f32[128,1024]{1,0:T(8,128)S(1)}, u32[]{:S(2)}, u32[]{:S(2)}) collective-permute-start(f32[128,1024]{1,0:T(8,128)S(1)} %constant_dynamic-update-slice_fusion.refs_0_), channel_id=1, source_target_pairs={{240,496},{241,497},{242,498},{243,499},{244,500},{245,501},{246,5... | collective-permute-start | bytes 1572872 | tf_op jit(solution)/shard_map/ppermute | solution.py:22
  139.2 7.6 %collective-permute-start.15 = (f32[128,1024]{1,0:T(8,128)S(1)}, f32[128,1024]{1,0:T(8,128)S(1)}, u32[]{:S(2)}, u32[]{:S(2)}) collective-permute-start(f32[128,1024]{1,0:T(8,128)S(1)} %constant_dynamic-update-slice_fusion.refs_0_), channel_id=1, source_target_pairs={{112,496},{113,497},{114,498},{115,499},{116,500},{117,501},{118,5... | collective-permute-start | bytes 1572872 | tf_op jit(solution)/shard_map/ppermute | solution.py:22
  140.1 6.7 %copy-start.9 = (f32[512,256]{1,0:T(8,128)S(1)}, f32[512,256]{1,0:T(8,128)}, u32[]{:S(2)}) copy-start(f32[512,256]{1,0:T(8,128)} %copy-done.8) | copy-start | bytes 1572868
  140.1 6.7 %copy-start.11 = (f32[512,256]{1,0:T(8,128)S(1)}, f32[512,256]{1,0:T(8,128)}, u32[]{:S(2)}) copy-start(f32[512,256]{1,0:T(8,128)} %copy-done.10) | copy-start | bytes 1572868
  140.1 6.7 %copy-start.13 = (f32[512,256]{1,0:T(8,128)S(1)}, f32[512,256]{1,0:T(8,128)}, u32[]{:S(2)}) copy-start(f32[512,256]{1,0:T(8,128)} %copy-done.12) | copy-start | bytes 1572868
  140.1 6.7 %copy-start.15 = (f32[512,256]{1,0:T(8,128)S(1)}, f32[512,256]{1,0:T(8,128)}, u32[]{:S(2)}) copy-start(f32[512,256]{1,0:T(8,128)} %copy-done.14) | copy-start | bytes 1572868
  143.4 1.1 copy-start
  144.6 1.2 copy-start.1
  145.7 1.0 copy-start.6
  146.7 5.6 %copy-start.2 = (f32[128,1024]{1,0:T(8,128)}, f32[128,1024]{1,0:T(8,128)S(1)}, u32[]{:S(2)}) copy-start(f32[128,1024]{1,0:T(8,128)S(1)} %collective-permute-done.14.refs_2_) | copy-start | bytes 1572868
  146.8 5.6 %copy-start.4 = (f32[128,1024]{1,0:T(8,128)}, f32[128,1024]{1,0:T(8,128)S(1)}, u32[]{:S(2)}) copy-start(f32[128,1024]{1,0:T(8,128)S(1)} %collective-permute-done.15.refs_3_) | copy-start | bytes 1572868
  152.4 89.7 %collective-permute-start.16 = (f32[512,512]{1,0:T(8,128)S(1)}, f32[512,512]{1,0:T(8,128)}, u32[]{:S(2)}, u32[]{:S(2)}) collective-permute-start(f32[512,512]{1,0:T(8,128)S(1)} %shard_map.56.outer_ref), channel_id=1, source_target_pairs={{1,2},{2,1},{3,4},{4,3},{5,6},{6,5},{7,8},{8,7},{9,10},{10,9},{11,... | collective-permute-start | bytes 3145736 | tf_op jit(solution)/shard_map/ppermute | solution.py:22
  184.7 1.0 copy-start.3
  185.7 1.0 copy-start.5
  192.9 49.2 %collective-permute-start.19 = (f32[512,512]{1,0:T(8,128)S(1)}, f32[512,512]{1,0:T(8,128)S(1)}, u32[]{:S(2)}, u32[]{:S(2)}) collective-permute-start(f32[512,512]{1,0:T(8,128)S(1)} %shard_map.57.inner_ref), channel_id=1, source_target_pairs={{0,1},{1,0},{2,3},{3,2},{4,5},{5,4},{6,7},{7,6},{8,9},{9,8},{10,11... | collective-permute-start | bytes 3145736 | tf_op jit(solution)/shard_map/ppermute | solution.py:22
  242.1 1.2 copy-start.7
Sparse Core Ops, SparseCore 0:
  9.4 106.1 all-gather.2
  120.8 75.1 all-gather.4
